TPU v7x, 32 devices: a whole 2x2x4 slice. The times are simulated.
32 devices in a mesh: group: 2 (over y), tile: 4 (over z), band: 4 (over x, core).
Axes of the slice: x: 2, y: 2, z: 4, core: 2. Of those that a mesh axis runs over, the one named last changes fastest.
Arguments:
- features: bfloat16 [256, 1024, 24], P(('group', 'band'), 'tile'), parts along dimension 0, may hold values from -6 to 6
- land_mask: int32 [128, 1024], P('band', 'tile'), may hold values 0 or 1
- cell_blocks: int32 [4, 4, 81, 128], P('band', 'tile'), may hold values from 0 to 8192, as said below
- region_ids: int32 [4, 4, 81], P('band', 'tile'), may hold values from 0 to 13999
- targets: float32 [28160], P(('group', 'tile', 'band')), parts along dimension 0, may hold values from -6 to 6
- w_embed: bfloat16 [384, 256], replicated, may hold values from -0.3125 to 0.3125
- k_first: bfloat16 [9, 256], replicated, may hold values from -2 to 2
- w_mix: bfloat16 [256, 256], replicated, may hold values from -0.375 to 0.375
- k_deep: bfloat16 [9, 256], replicated, may hold values from -2 to 2
- w_head: bfloat16 [256, 16], replicated, may hold values from -0.375 to 0.375
Outputs:
- cell_pred: float32 [256, 1024], P(('group', 'band'), 'tile'), parts along dimension 0
- region_mean: float32 [28160], P(('group', 'tile', 'band')), parts along dimension 0
- loss_value: float32 [2], P('group'), parts along dimension 0
- input_grad: bfloat16 [256, 1024, 24], P(('group', 'band'), 'tile'), parts along dimension 0
There are 2 independent parts, one for each index of `group`. A program takes and returns all parts, laid end to end along the dimension named above; an argument that names none is the same for every part. Nothing has to cross between parts.
Inputs may be any that keep to these rules, and one draw needn't show every extreme that they name: `cell_blocks`: each device's blocks name each of its 32 x 256 cells at most once, by its row-major index in that device's block of cells; the value 32 * 256 marks an empty slot.
All inputs are finite; a program needn't handle non-finite values. No bound on the sum of `land_mask` on one device may be relied on, other than what follows from the above.
Results may differ from a plain program's by a relative error of at most 0.014.
Values may be sent and summed in bfloat16 or wider, within the bound.
No kernel may reach another device: no remote copies, remote signals or barrier semaphores. Data moves between devices by JAX's collectives and lax.ppermute only.
A program may use at most 64 MiB of HBM per device.

v0:
```python
import jax
import jax.numpy as jnp
from jax import lax
from jax.sharding import PartitionSpec as P

REGIONS = 14000


SQRT_HALF = 0.7071067811865476
INV_ROOT = 0.3989422804014327


def with_halo(shard, sides, width):
    for axis, dim in sides:
        size, length = (lax.axis_size(axis), shard.shape[dim])
        up = [(i, (i + 1) % size) for i in range(size - 1)]
        down = [(j, i) for i, j in up]
        last = lax.slice_in_dim(shard, length - width, length, axis=dim)
        initial = lax.slice_in_dim(shard, 0, width, axis=dim)
        before = lax.ppermute(last, axis, up)
        after = lax.ppermute(initial, axis, down)
        shard = jnp.concatenate([before, shard, after], axis=dim)
    return shard


def gelu_exact(inputs):
    return 0.5 * inputs * (1.0 + lax.erf(inputs * SQRT_HALF))


def gelu_slope(inputs):
    return (
        0.5 * (1.0 + lax.erf(inputs * SQRT_HALF))
        + inputs * jnp.exp(-0.5 * inputs * inputs) * INV_ROOT
    )


def to_coarse(grid_field):
    height, breadth, depth = grid_field.shape
    blocks = grid_field.reshape(height // 4, 4, breadth // 4, 4, depth)
    return blocks.transpose(0, 2, 1, 3, 4).reshape(height // 4, breadth // 4, 16 * depth)


def to_fine(coarse):
    height, breadth, depth = coarse.shape
    inner = depth // 16
    blocks = coarse.reshape(height, breadth, 4, 4, inner)
    return blocks.transpose(0, 2, 1, 3, 4).reshape(4 * height, 4 * breadth, inner)


def project(operand, matrix):
    leading = operand.shape[:-1]
    flat = operand.reshape(-1, operand.shape[-1])
    return jnp.dot(flat, matrix, preferred_element_type=jnp.float32).reshape(
        leading + (matrix.shape[-1],)
    )


def depthwise(padded, kernel, row_count, col_count):
    kernel_wide = kernel.astype(jnp.float32)
    padded_wide = padded.astype(jnp.float32)
    running = jnp.zeros((row_count, col_count, kernel.shape[1]), jnp.float32)
    for row_off in range(3):
        for col_off in range(3):
            window = padded_wide[row_off : row_off + row_count, col_off : col_off + col_count]
            running = running + kernel_wide[3 * row_off + col_off] * window
    return running


def per_device(
    features, land_mask, cell_blocks, region_ids, targets, w_embed, k_first, w_mix, k_deep, w_head
):
    land_cells = land_mask.astype(jnp.float32)
    fine_rows, fine_cols = land_mask.shape
    patches = to_coarse(features)
    pre_first = project(patches, w_embed)
    act_first = gelu_exact(pre_first).astype(jnp.bfloat16)
    coarse_rows, coarse_cols, channels = act_first.shape
    first_pad = with_halo(act_first, (("band", 0), ("tile", 1)), 1)
    mixed_in = depthwise(first_pad, k_first, coarse_rows, coarse_cols).astype(jnp.bfloat16)
    pre_mix = project(mixed_in, w_mix)
    act_mix = (act_first.astype(jnp.float32) + gelu_exact(pre_mix)).astype(jnp.bfloat16)
    tile_count = lax.axis_size("tile")
    band_count = lax.axis_size("band")
    mix_pad = with_halo(act_mix, (("band", 0), ("tile", 1)), 1)
    pre_deep = depthwise(mix_pad, k_deep, coarse_rows, coarse_cols)
    act_deep = (act_mix.astype(jnp.float32) + gelu_exact(pre_deep)).astype(jnp.bfloat16)
    cell_pred = to_fine(project(act_deep, w_head))[:, :, 0] * land_cells
    block_len = cell_blocks.shape[-1]
    slot_index = cell_blocks.reshape(-1)
    block_owner = region_ids.reshape(-1)
    spare = jnp.zeros((1,), jnp.float32)
    flat_pred = jnp.concatenate([cell_pred.reshape(-1), spare])
    flat_land = jnp.concatenate([land_cells.reshape(-1), spare])
    block_sums = jnp.take(flat_pred, slot_index).reshape(-1, block_len).sum(-1)
    block_counts = jnp.take(flat_land, slot_index).reshape(-1, block_len).sum(-1)
    share_len = targets.shape[0]
    region_len = share_len * tile_count * band_count
    part_sum = jax.ops.segment_sum(block_sums, block_owner, num_segments=region_len)
    part_count = jax.ops.segment_sum(block_counts, block_owner, num_segments=region_len)
    region_sum, region_count = (
        lax.psum_scatter(part_sum, ("tile", "band"), scatter_dimension=0, tiled=True),
        lax.psum_scatter(part_count, ("tile", "band"), scatter_dimension=0, tiled=True),
    )
    region_mean = region_sum / jnp.maximum(region_count, 1.0)
    first_region = (lax.axis_index("tile") * band_count + lax.axis_index("band")) * share_len
    inside = first_region + jnp.arange(share_len, dtype=jnp.int32) < REGIONS
    misfit = region_mean - targets
    local_loss = jnp.sum(jnp.where(inside, region_count * misfit * misfit, 0.0))
    cell_total = float(fine_rows * fine_cols * tile_count * band_count)
    loss_value = (lax.psum(local_loss, ("tile", "band")) / (2.0 * cell_total)).reshape(1)
    region_grad = jnp.where(inside, region_count * misfit / jnp.maximum(region_count, 1.0), 0.0)
    all_grads = lax.all_gather(region_grad, ("tile", "band"), axis=0, tiled=True)
    block_grad = jnp.take(all_grads, block_owner)
    slot_grad = jnp.broadcast_to(block_grad[:, None], (block_grad.shape[0], block_len)).reshape(-1)
    spread_grad = jnp.zeros((fine_rows * fine_cols + 1,), jnp.float32).at[slot_index].add(slot_grad)
    cell_grad = spread_grad[: fine_rows * fine_cols].reshape(fine_rows, fine_cols) * land_cells
    grad_out = to_coarse(cell_grad[:, :, None]).astype(jnp.bfloat16)
    grad_deep = project(grad_out, w_head.T).astype(jnp.bfloat16)
    slope_deep = grad_deep.astype(jnp.float32) * gelu_slope(pre_deep)
    slope_pad = with_halo(slope_deep, (("band", 0), ("tile", 1)), 1)
    back_deep = depthwise(slope_pad, k_deep[::-1], coarse_rows, coarse_cols)
    grad_mix = (grad_deep.astype(jnp.float32) + back_deep).astype(jnp.bfloat16)
    grad_pre_mix = (grad_mix.astype(jnp.float32) * gelu_slope(pre_mix)).astype(jnp.bfloat16)
    grad_mixed_in = project(grad_pre_mix, w_mix.T)
    mixed_pad = with_halo(grad_mixed_in, (("band", 0), ("tile", 1)), 1)
    grad_first = grad_mix.astype(jnp.float32) + depthwise(
        mixed_pad, k_first[::-1], coarse_rows, coarse_cols
    )
    grad_pre_first = (grad_first * gelu_slope(pre_first)).astype(jnp.bfloat16)
    input_grad = to_fine(project(grad_pre_first, w_embed.T)).astype(jnp.bfloat16)
    return (cell_pred, region_mean, loss_value, input_grad)


def solution(mesh):
    in_specs = (
        P(("group", "band"), "tile", None),
        P("band", "tile"),
        P("band", "tile", None, None),
        P("band", "tile", None),
        P(("group", "tile", "band")),
        P(),
        P(),
        P(),
        P(),
        P(),
    )
    out_specs = (
        P(("group", "band"), "tile"),
        P(("group", "tile", "band")),
        P("group"),
        P(("group", "band"), "tile", None),
    )
    return jax.shard_map(
        per_device, mesh=mesh, in_specs=in_specs, out_specs=out_specs, check_vma=False
    )
```

profile of v0, /device:TPU:0, one launch (start us, length us, event | category | flops | bytes accessed | tf_op | source)
XLA Modules:
  0.0 407.2 jit_solution(12427349392732659340)
XLA Ops:
  7.2 1.9 copy.38
  12.8 3.0 collective-permute-start
  16.7 1.3 collective-permute-start.3
  18.0 5.6 %collective-permute-start.2 = (bf16[10,1,256]{2,1,0:T(2,128)(2,1)S(1)}, bf16[10,1,256]{2,1,0:T(2,128)(2,1)S(1)}, u32[]{:S(2)}, u32[]{:S(2)}) collective-permute-start(bf16[10,1,256]{2,1,0:T(2,128)(2,1)S(1)} %get-tuple-element.45), channel_id=1, source_target_pairs={{0,4},{4,8},{8,12},{1,5},{5,9},{9,13},{2,6},{6,10},{10,14},{3,7},{... | collective-permute-start | bytes 15368 | tf_op jit(solution)/shard_map/ppermute | solution.py:20
  23.6 1.3 collective-permute-done.2
  25.8 1.3 collective-permute-start.5
  27.1 3.1 collective-permute-start.4
  31.0 1.3 collective-permute-start.7
  32.3 4.7 %collective-permute-start.6 = (bf16[10,1,256]{2,1,0:T(2,128)(2,1)S(1)}, bf16[10,1,256]{2,1,0:T(2,128)(2,1)S(1)}, u32[]{:S(2)}, u32[]{:S(2)}) collective-permute-start(bf16[10,1,256]{2,1,0:T(2,128)(2,1)S(1)} %get-tuple-element.43), channel_id=1, source_target_pairs={{0,4},{4,8},{8,12},{1,5},{5,9},{9,13},{2,6},{6,10},{10,14},{3,7},{... | collective-permute-start | bytes 15368 | tf_op jit(solution)/shard_map/ppermute | solution.py:20
  41.1 53.6 %gather_fusion.2 = f32[10368]{0:T(1024)S(1)} fusion(f32[8193]{0:T(1024)S(1)} %get-tuple-element.95, s32[11264]{0:T(1024)S(1)} %pad_clamp_fusion), kind=kCustom, calls=%fused_computation.1.clone | custom fusion | bytes 124416 | tf_op jit(solution)/shard_map/jit(_take)/gather | solution.py:95
  94.7 53.6 %gather_fusion.1 = f32[10368]{0:T(1024)S(1)} fusion(f32[8193]{0:T(1024)S(1)} %get-tuple-element.96, s32[11264]{0:T(1024)S(1)} %pad_clamp_fusion), kind=kCustom, calls=%fused_computation.clone | custom fusion | bytes 124416 | tf_op jit(solution)/shard_map/jit(_take)/gather | solution.py:94
  148.4 1.6 scatter_custom_fusion
  150.0 1.6 scatter_custom_fusion.1
  151.6 92.2 %all-reduce.7.cloned.1.call-done = (f32[14080]{0:T(1024)}, f32[14080]{0:T(1024)}) async-done(((f32[14080]{0:T(1024)}, f32[14080]{0:T(1024)}), (f32[14080]{0:T(1024)}, f32[14080]{0:T(1024)})) %all-reduce.7.cloned.1.call-update) | async-done | bytes 112656
  244.7 1.4 select_reduce_fusion
  246.1 61.2 %all-reduce.3 = (f32[]{:T(128)}, f32[14080]{0:T(1024)S(1)}) all-reduce(f32[]{:T(128)} %select_reduce_fusion, f32[14080]{0:T(1024)S(1)} %get-tuple-element.29), channel_id=1, replica_groups=mesh['group'=2,'tile'=4,'band'=4] {'tile','band'}, use_global_device_ids=true, to_apply=%region_7.9 | all-reduce | flops 14081 | bytes 112648 | tf_op jit(solution)/shard_map/psum | solution.py:110
  308.6 59.4 %scatter_custom_fusion.2 = f32[8193]{0:T(1024)S(1)} fusion(s32[10368]{0:T(1024)S(1)} %fusion.67, f32[10368]{0:T(1024)S(1)} %broadcast_bitcast_fusion, f32[]{:T(128)} %constant.17.clone.1), kind=kCustom, calls=%fused_computation.144 | custom fusion | flops 10368 | bytes 32776 | tf_op jit(solution)/shard_map/scatter-add | solution.py:115
  371.1 3.0 collective-permute-start.8
  377.7 4.2 %collective-permute-done.11 = f32[10,1,256]{2,1,0:T(1,128)S(1)} collective-permute-done((f32[10,1,256]{2,1,0:T(1,128)S(1)}, f32[10,1,256]{2,1,0:T(1,128)S(1)}, u32[]{:S(2)}, u32[]{:S(2)}) %collective-permute-start.11) | collective-permute-done | bytes 10272 | tf_op jit(solution)/shard_map/ppermute | solution.py:21
  384.2 3.0 collective-permute-start.12
  388.1 1.7 collective-permute-start.14
  391.8 3.6 collective-permute-done.15
  396.4 1.3 copy.44
  397.8 1.5 copy.45
  (100 shorter events, 23.0 us)
Async XLA Ops:
  7.2 236.6 %all-reduce.7.cloned.1.call-start = ((), (), s32[]{:S(2)}) async-start(), calls=%async_computation | async-start | bytes 229376
  9.2 14.4 %copy-start.6 = (bf16[9,256]{1,0:T(8,128)(2,1)S(1)}, bf16[9,256]{1,0:T(8,128)(2,1)}, u32[]{:S(2)}) copy-start(bf16[9,256]{1,0:T(8,128)(2,1)} %param.20) | copy-start | bytes 13828
  10.3 14.8 %copy-start.4 = (bf16[256,256]{1,0:T(8,128)(2,1)S(1)}, bf16[256,256]{1,0:T(8,128)(2,1)}, u32[]{:S(2)}) copy-start(bf16[256,256]{1,0:T(8,128)(2,1)} %param.19) | copy-start | bytes 393220
  11.5 4.5 %collective-permute-start.1 = (bf16[1,64,256]{2,1,0:T(8,128)(2,1)S(1)}, bf16[1,64,256]{2,1,0:T(8,128)(2,1)S(1)}, u32[]{:S(2)}, u32[]{:S(2)}) collective-permute-start(bf16[1,64,256]{2,1,0:T(8,128)(2,1)S(1)} %get-tuple-element.50), channel_id=1, source_target_pairs={{1,0},{2,1},{3,2},{5,4},{6,5},{7,6},{9,8},{10,9},{11,10},{13,12},{... | collective-permute-start | bytes 98312 | tf_op jit(solution)/shard_map/ppermute | solution.py:21
  12.8 3.9 collective-permute-start
  16.7 6.9 %collective-permute-start.3 = (bf16[10,1,256]{2,1,0:T(2,128)(2,1)S(1)}, bf16[10,1,256]{2,1,0:T(2,128)(2,1)S(1)}, u32[]{:S(2)}, u32[]{:S(2)}) collective-permute-start(bf16[10,1,256]{2,1,0:T(2,128)(2,1)S(1)} %get-tuple-element.46), channel_id=1, source_target_pairs={{4,0},{8,4},{12,8},{5,1},{9,5},{13,9},{6,2},{10,6},{14,10},{7,3},{... | collective-permute-start | bytes 15368 | tf_op jit(solution)/shard_map/ppermute | solution.py:21
  18.0 6.9 %collective-permute-start.2 = (bf16[10,1,256]{2,1,0:T(2,128)(2,1)S(1)}, bf16[10,1,256]{2,1,0:T(2,128)(2,1)S(1)}, u32[]{:S(2)}, u32[]{:S(2)}) collective-permute-start(bf16[10,1,256]{2,1,0:T(2,128)(2,1)S(1)} %get-tuple-element.45), channel_id=1, source_target_pairs={{0,4},{4,8},{8,12},{1,5},{5,9},{9,13},{2,6},{6,10},{10,14},{3,7},{... | collective-permute-start | bytes 15368 | tf_op jit(solution)/shard_map/ppermute | solution.py:20
  25.1 12.2 %copy-start.11 = (u32[32]{0:T(128)S(1)}, u32[32]{0:T(128)}, u32[]{:S(2)}) copy-start(u32[32]{0:T(128)} %constant.67) | copy-start | bytes 388
  25.8 4.4 %collective-permute-start.5 = (bf16[1,64,256]{2,1,0:T(8,128)(2,1)S(1)}, bf16[1,64,256]{2,1,0:T(8,128)(2,1)S(1)}, u32[]{:S(2)}, u32[]{:S(2)}) collective-permute-start(bf16[1,64,256]{2,1,0:T(8,128)(2,1)S(1)} %get-tuple-element.48), channel_id=1, source_target_pairs={{1,0},{2,1},{3,2},{5,4},{6,5},{7,6},{9,8},{10,9},{11,10},{13,12},{... | collective-permute-start | bytes 98312 | tf_op jit(solution)/shard_map/ppermute | solution.py:21
  27.1 4.0 collective-permute-start.4
  31.0 8.2 %collective-permute-start.7 = (bf16[10,1,256]{2,1,0:T(2,128)(2,1)S(1)}, bf16[10,1,256]{2,1,0:T(2,128)(2,1)S(1)}, u32[]{:S(2)}, u32[]{:S(2)}) collective-permute-start(bf16[10,1,256]{2,1,0:T(2,128)(2,1)S(1)} %get-tuple-element.44), channel_id=1, source_target_pairs={{4,0},{8,4},{12,8},{5,1},{9,5},{13,9},{6,2},{10,6},{14,10},{7,3},{... | collective-permute-start | bytes 15368 | tf_op jit(solution)/shard_map/ppermute | solution.py:21
  32.3 6.9 %collective-permute-start.6 = (bf16[10,1,256]{2,1,0:T(2,128)(2,1)S(1)}, bf16[10,1,256]{2,1,0:T(2,128)(2,1)S(1)}, u32[]{:S(2)}, u32[]{:S(2)}) collective-permute-start(bf16[10,1,256]{2,1,0:T(2,128)(2,1)S(1)} %get-tuple-element.43), channel_id=1, source_target_pairs={{0,4},{4,8},{8,12},{1,5},{5,9},{9,13},{2,6},{6,10},{10,14},{3,7},{... | collective-permute-start | bytes 15368 | tf_op jit(solution)/shard_map/ppermute | solution.py:20
  41.0 53.6 %copy-start.5 = (f32[32,256]{1,0:T(8,128)}, f32[32,256]{1,0:T(8,128)S(1)}, u32[]{:S(2)}) copy-start(f32[32,256]{1,0:T(8,128)S(1)} %convert_multiply_fusion.1) | copy-start | bytes 98308
  94.7 149.1 %copy-start.8 = (f32[880]{0:T(1024)S(1)}, f32[880]{0:T(1024)}, u32[]{:S(2)}) copy-start(f32[880]{0:T(1024)} %param.16) | copy-start | bytes 10564
  244.7 130.3 %copy-start.9 = (f32[880]{0:T(1024)}, f32[880]{0:T(1024)S(1)}, u32[]{:S(2)}) copy-start(f32[880]{0:T(1024)S(1)} %get-tuple-element.30) | copy-start | bytes 10564
  369.8 4.4 %collective-permute-start.9 = (f32[1,64,256]{2,1,0:T(8,128)S(1)}, f32[1,64,256]{2,1,0:T(8,128)S(1)}, u32[]{:S(2)}, u32[]{:S(2)}) collective-permute-start(f32[1,64,256]{2,1,0:T(8,128)S(1)} %get-tuple-element.42), channel_id=1, source_target_pairs={{1,0},{2,1},{3,2},{5,4},{6,5},{7,6},{9,8},{10,9},{11,10},{13,12},{... | collective-permute-start | bytes 196616 | tf_op jit(solution)/shard_map/ppermute | solution.py:21
  371.1 3.9 collective-permute-start.8
  375.0 2.7 collective-permute-start.10
  376.3 5.6 %collective-permute-start.11 = (f32[10,1,256]{2,1,0:T(1,128)S(1)}, f32[10,1,256]{2,1,0:T(1,128)S(1)}, u32[]{:S(2)}, u32[]{:S(2)}) collective-permute-start(f32[10,1,256]{2,1,0:T(1,128)S(1)} %get-tuple-element.38), channel_id=1, source_target_pairs={{4,0},{8,4},{12,8},{5,1},{9,5},{13,9},{6,2},{10,6},{14,10},{7,3},{... | collective-permute-start | bytes 30728 | tf_op jit(solution)/shard_map/ppermute | solution.py:21
  382.6 12.9 %copy-start.1 = (f32[8,64,256]{2,1,0:T(8,128)S(1)}, f32[8,64,256]{2,1,0:T(8,128)}, u32[]{:S(2)}) copy-start(f32[8,64,256]{2,1,0:T(8,128)} %get-tuple-element.90) | copy-start | bytes 1572868
  382.9 4.4 %collective-permute-start.13 = (f32[1,64,256]{2,1,0:T(8,128)S(1)}, f32[1,64,256]{2,1,0:T(8,128)S(1)}, u32[]{:S(2)}, u32[]{:S(2)}) collective-permute-start(f32[1,64,256]{2,1,0:T(8,128)S(1)} %get-tuple-element.40), channel_id=1, source_target_pairs={{1,0},{2,1},{3,2},{5,4},{6,5},{7,6},{9,8},{10,9},{11,10},{13,12},{... | collective-permute-start | bytes 196616 | tf_op jit(solution)/shard_map/ppermute | solution.py:21
  384.2 3.9 collective-permute-start.12
  388.1 3.6 collective-permute-start.14
  389.8 5.6 %collective-permute-start.15 = (f32[10,1,256]{2,1,0:T(1,128)S(1)}, f32[10,1,256]{2,1,0:T(1,128)S(1)}, u32[]{:S(2)}, u32[]{:S(2)}) collective-permute-start(f32[10,1,256]{2,1,0:T(1,128)S(1)} %get-tuple-element.34), channel_id=1, source_target_pairs={{4,0},{8,4},{12,8},{5,1},{9,5},{13,9},{6,2},{10,6},{14,10},{7,3},{... | collective-permute-start | bytes 30728 | tf_op jit(solution)/shard_map/ppermute | solution.py:21
  (6 other events, 40.6 us)
Sparse Core Ops, SparseCore 0:
  151.7 92.0 all-reduce.6
where the time goes:
time: 410 us; the launch traced here: 407 us
  local copies, waits for them, and re-layouts  118 us (29%)
  waiting for transfers between devices  104 us (25%)
  other arithmetic  66.7 us (16%)
  blocking collectives  61.2 us (15%)
  starting transfers between devices  35.8 us (9%)
  between operations  17.9 us (4%)
    unnamed x2, waiting for transfers between devices  92.2 us
    psum x1, blocking collectives, per_device(): lax.psum(local_loss, ('tile', 'band')) / (2.0 * cell_total)  61.2 us
    scatter-add x1, other arithmetic, per_device(): jnp.zeros((fine_rows * fine_cols + 1,), jnp.float32).at[slot_index]  59.4 us
    gather x1, local copies, waits for them, and re-layouts, per_device(): jnp.take(flat_land, slot_index).reshape(-1, block_len).sum(-1)  53.6 us
    gather x1, local copies, waits for them, and re-layouts, per_device(): block_sums = jnp.take(flat_pred, slot_index).reshape(-1, block_len).sum(-1)  53.6 us
    ppermute x8, starting transfers between devices, with_halo(): before = lax.ppermute(last, axis, up)  25.5 us
    ppermute x8, starting transfers between devices, with_halo(): after = lax.ppermute(initial, axis, down)  10.3 us
  transfers between devices with their start and end apart: 17, of which 8 were waited for; matrix products, arithmetic and copies ran while one was open for 0% of the time, Pallas kernels for 0%

commit v1 on v0

v1 whole, which is shorter than its diff:
```python
import functools

import jax
import jax.numpy as jnp
from jax import lax
from jax.experimental import pallas as pl
from jax.experimental.pallas import tpu as pltpu
from jax.sharding import PartitionSpec as P

REGIONS = 14000
SQRT_HALF = 0.7071067811865476
INV_ROOT = 0.3989422804014327
F32 = jnp.float32
BF16 = jnp.bfloat16
LANES = 128
HALO = 4
OUTSIDE = -50.0
VMEM_LIMIT = 48 * 1024 * 1024


def gelu_exact(v):
    return 0.5 * v * (1.0 + lax.erf(v * SQRT_HALF))


def gelu_slope(v):
    return 0.5 * (1.0 + lax.erf(v * SQRT_HALF)) + v * jnp.exp(-0.5 * v * v) * INV_ROOT


def rounded(v):
    return v.astype(BF16).astype(F32)


def dot(a, b):
    return jnp.dot(a, b, preferred_element_type=F32)


def dot_nt(a, b):
    return lax.dot_general(a, b, (((1,), (1,)), ((), ())), preferred_element_type=F32)


def iota(shape, dim):
    return lax.broadcasted_iota(jnp.int32, shape, dim)


def spread_matrix(cols, transposed=False):
    quarter = cols // 4
    shape = (cols, cols)
    n = iota(shape, 0)
    c = iota(shape, 1)
    return jnp.where(c == 4 * (n % quarter) + n // quarter, 1.0, 0.0).astype(BF16)


def padded_embed(w_ref, c_in, c_pad):
    w = w_ref[...].astype(F32)
    zeros = jnp.zeros((c_pad - c_in, w.shape[1]), F32)
    parts = []
    for b in range(4):
        for a in range(4):
            start = (4 * a + b) * c_in
            parts += [w[start : start + c_in], zeros]
    return jnp.concatenate(parts, axis=0).astype(BF16)


def embed_kernel(
    flags, feat, w_embed, land, blocks, pre_out, act_out, bm_out, m1_out, m2_out, hot_a, hot_b
):
    rows, c_in, cols = feat.shape
    c_pad = 32
    crows, ccols = rows // 4, cols // 4
    nblk = blocks.shape[0]
    spread = spread_matrix(cols)
    field = feat[...].astype(F32)
    field = jnp.concatenate([field, jnp.zeros((rows, c_pad - c_in, cols), F32)], axis=1)
    field = field.reshape(rows * c_pad, cols).astype(BF16)
    moved = dot_nt(spread, field).astype(BF16)
    wide = 4 * c_pad
    lhs = jnp.concatenate(
        [
            jnp.concatenate(
                [
                    moved[b * ccols : (b + 1) * ccols, i * wide : (i + 1) * wide]
                    for b in range(4)
                ],
                axis=1,
            )
            for i in range(crows)
        ],
        axis=0,
    )
    pre = dot(lhs, padded_embed(w_embed, c_in, c_pad))
    pre_out[...] = pre
    act_out[...] = gelu_exact(pre).astype(BF16).reshape(crows, ccols, pre.shape[1])

    shift_row = cols.bit_length() - 1
    chunk = next(c for c in (9, 8, 7, 6, 5, 4, 3, 2, 1) if nblk % c == 0)
    total = jnp.zeros((ccols, LANES), F32)
    sub_a = iota((LANES, LANES), 0)
    sub_b = iota((ccols, LANES), 0)
    for first in range(0, nblk, chunk):
        for step in range(chunk):
            k = first + step
            cell = blocks[k : k + 1, :]
            named = cell < rows * cols
            q = jnp.where(named, (cell & 3) * rows + (cell >> shift_row), -1)
            j = (cell & (cols - 1)) >> 2
            span = slice(step * LANES, (step + 1) * LANES)
            hot_a[:, span] = jnp.where(sub_a == q, 1.0, 0.0).astype(BF16)
            hot_b[:, span] = jnp.where(sub_b == j, float(k + 1), 0.0).astype(BF16)
        total = total + dot_nt(hot_b[...], hot_a[...])
    land_moved = dot_nt(spread, land[...].astype(F32).astype(BF16))
    land_q = jnp.concatenate(
        [land_moved[b * ccols : (b + 1) * ccols, :] for b in range(4)], axis=1
    )
    bm = total * land_q
    bm_out[...] = bm
    half = ccols // 2
    bm_wide = jnp.concatenate([bm[:half], bm[half:]], axis=1).astype(BF16)
    chan = pre.shape[1]
    odd = flags[0]
    for out, start in ((m1_out, (1 - odd) * (crows - HALO)), (m2_out, odd * (crows - HALO))):
        out[0 : HALO * ccols] = act_out[pl.ds(start, HALO)].reshape(HALO * ccols, chan)
        out[HALO * ccols :] = bm_wide


def edges_kernel(flags, act, bm, p1, p2, m1_out, m2_out):
    crows, ccols, chan = act.shape
    odd_b = flags[0] == 1
    odd_t = flags[1] == 1
    n = HALO * ccols
    up = jnp.where(odd_b, p1[...].astype(F32), p2[...].astype(F32))
    down = jnp.where(odd_b, p2[...].astype(F32), p1[...].astype(F32))
    left, right = [], []
    for r in range(crows + 2 * HALO):
        if r < HALO:
            row = up[r * ccols : (r + 1) * ccols]
        elif r < HALO + crows:
            row = act[r - HALO].astype(F32)
        else:
            row = down[(r - HALO - crows) * ccols : (r - HALO - crows + 1) * ccols]
        left.append(row[:HALO])
        right.append(row[ccols - HALO :])
    half = ccols // 2
    own = bm[...]
    zeros = jnp.zeros((10, LANES), F32)
    bm_left = [up[n : n + 2, :LANES], own[0:2], down[n : n + 2, :LANES], zeros]
    bm_right = [
        up[n + half - 2 : n + half, LANES:],
        own[ccols - 2 :],
        down[n + half - 2 : n + half, LANES:],
        zeros,
    ]
    def message(cells, maps):
        maps = jnp.concatenate(maps, axis=0)
        maps = jnp.concatenate([maps, jnp.zeros((16, chan - LANES), F32)], axis=1)
        return jnp.concatenate(cells + [maps], axis=0)

    left = message(left, bm_left)
    right = message(right, bm_right)
    m1_out[...] = jnp.where(odd_t, left, right).astype(BF16)
    m2_out[...] = jnp.where(odd_t, right, left).astype(BF16)


def conv_pass(src, count, kernel, emit, chan):
    width = src.shape[1]
    for h in range(0, chan, LANES):
        span = slice(h, h + LANES)
        taps = [kernel[t : t + 1, span] for t in range(9)]

        def body(r, carry, span=span, taps=taps):
            older, newer = carry
            x = src[r, :, span]
            before = pltpu.roll(x, 1, 0)
            after = pltpu.roll(x, width - 1, 0)
            parts = [
                taps[3 * a] * before + taps[3 * a + 1] * x + taps[3 * a + 2] * after
                for a in range(3)
            ]
            emit(jnp.maximum(r - 2, 0), span, older + parts[2])
            return newer + parts[1], parts[0]

        zero = jnp.zeros((width, LANES), F32)
        lax.fori_loop(0, count, body, (zero, zero))


def forward_kernel(
    flags, act, bm, p1, p2, t1, t2, w_mix, k_first, k_deep, wall, msg_in,
    pre_mix, pre_deep, pred_out, msg_out, field, mixed,
):
    crows, ccols, chan = act.shape
    width = ccols + 2 * HALO
    odd_b = flags[0] == 1
    odd_t = flags[1] == 1
    nrow = crows + 2 * HALO
    n = HALO * ccols
    up = jnp.where(odd_b, p1[0:n].astype(F32), p2[0:n].astype(F32))
    down = jnp.where(odd_b, p2[0:n].astype(F32), p1[0:n].astype(F32))
    m = HALO * nrow
    left = jnp.where(odd_t, t1[0:m].astype(F32), t2[0:m].astype(F32))
    right = jnp.where(odd_t, t2[0:m].astype(F32), t1[0:m].astype(F32))
    for r in range(nrow):
        if r < HALO:
            row = up[r * ccols : (r + 1) * ccols]
        elif r < HALO + crows:
            row = act[r - HALO].astype(F32)
        else:
            row = down[(r - HALO - crows) * ccols : (r - HALO - crows + 1) * ccols]
        field[r, 0:ccols, :] = row
        field[r, ccols:, :] = jnp.concatenate(
            [right[HALO * r : HALO * (r + 1)], left[HALO * r : HALO * (r + 1)]], axis=0
        )

    def keep_mixed(r, span, value):
        mixed[r, :, span] = value

    conv_pass(field, nrow, k_first[...].astype(F32), keep_mixed, chan)

    col = iota((1, width, chan), 1)
    col_ok = (col < ccols) | ((col < ccols + HALO) & (flags[5] == 0)) | (
        (col >= ccols + HALO) & (flags[4] == 0)
    )
    first_row = flags[2] * (HALO - 1)
    last_row = nrow - 2 - flags[3] * (HALO - 1)
    weights = w_mix[...]

    def mix(g, carry):
        pair = mixed[pl.ds(2 * g, 2)].reshape(2 * width, chan).astype(BF16)
        pre = dot(pair, weights).reshape(2, width, chan)
        row = iota((2, width, chan), 0) + 2 * g
        ok = col_ok & (row >= first_row) & (row < last_row)
        pre = jnp.where(ok, pre, OUTSIDE)
        pre_mix[pl.ds(2 * g, 2)] = pre
        mixed[pl.ds(2 * g, 2)] = rounded(field[pl.ds(2 * g + 1, 2)] + gelu_exact(pre))
        return carry

    lax.fori_loop(0, (nrow - 2) // 2, mix, 0)

    def keep_deep(r, span, value):
        pre_deep[r, :, span] = value

    conv_pass(mixed, nrow - 2, k_deep[...].astype(F32), keep_deep, chan)

    head = wall[...]
    head_row = (iota(head.shape, 0) % (4 * crows)) // 4

    def deep(i, pred):
        pre = pre_deep[i + 2, 0:ccols, :]
        out = (mixed[i + 3, 0:ccols, :] + gelu_exact(pre)).astype(BF16)
        return pred + dot_nt(out, jnp.where(head_row == i, head, 0.0).astype(BF16))

    pred = lax.fori_loop(0, crows, deep, jnp.zeros((ccols, LANES), F32))
    pred_out[...] = pred

    maps = bm[...]
    slots = iota((LANES, LANES), 0).astype(F32)[:88]
    sums = jnp.zeros((88, LANES), F32)
    counts = jnp.zeros((88, LANES), F32)
    for j in range(ccols):
        hit = maps[j : j + 1, :] == slots
        sums = sums + jnp.where(hit, pred[j : j + 1, :], 0.0)
        counts = counts + jnp.where(hit, 1.0, 0.0)
    msg_out[...] = msg_in[...]
    used = iota((1, LANES), 1) > 0
    rest = jnp.zeros((LANES - 88, LANES), F32)
    for at, acc in enumerate((sums, counts)):
        across = jnp.concatenate([acc, rest], axis=0).T
        msg_out[at : at + 1, :] = jnp.where(used, jnp.sum(across, axis=0, keepdims=True), 0.0)


def slope_kernel(src, out):
    out[...] = gelu_slope(src[...])


def slope_pred_kernel(src, pred, land, out, cells):
    rows, cols = land.shape
    out[...] = gelu_slope(src[...])
    turned = pred[...].T
    wide = jnp.concatenate([turned[b * rows : (b + 1) * rows] for b in range(4)], axis=1)
    high = wide.astype(BF16)
    low = (wide - high.astype(F32)).astype(BF16)
    spread = spread_matrix(cols)
    cells[...] = (dot(high, spread) + dot(low, spread)) * land[...].astype(F32)


def backward_kernel(
    flags, msgs, bm, p1, p2, t1, t2, slope_deep, slope_mix, slope_first,
    w_mix, k_first, k_deep, wall, w_embed,
    mean_out, loss_out, grad_out,
    targets, table, grads, field, mixing, proj, share_rows, share, count, loss_scale, c_in,
):
    ndev = msgs.shape[0]
    crows = slope_first.shape[0]
    ccols = slope_first.shape[1]
    chan = slope_first.shape[2]
    width = ccols + 2 * HALO
    me = flags[6]
    height = ndev * share_rows
    chunk = min(16, ndev)
    first_target = msgs.shape[1] - share_rows
    sub = iota((height, LANES), 0).astype(F32)
    sub_lo = iota((LANES, LANES), 0).astype(F32)

    def gather_chunk(c, acc):
        hot_hi, hot_lo = [], []
        for o in range(chunk):
            owner = c * chunk + o
            m = msgs[owner ^ me]
            hot_hi.append(jnp.where(sub == m[2:3], 1.0, 0.0).astype(BF16))
            low_hit = sub_lo == m[3:4]
            high = rounded(m[0:1])
            parts = [high, m[0:1] - high, m[1:2]]
            hot_lo.append(
                jnp.concatenate(
                    [jnp.where(low_hit, part, 0.0).astype(BF16) for part in parts], axis=0
                )
            )
            targets[pl.ds(owner * share_rows, share_rows)] = m[first_target:]
        return acc + dot_nt(
            jnp.concatenate(hot_hi, axis=1), jnp.concatenate(hot_lo, axis=1)
        )

    acc = jnp.zeros((height, 3 * LANES), F32)
    if ndev == chunk:
        acc = gather_chunk(0, acc)
    else:
        acc = lax.fori_loop(0, ndev // chunk, gather_chunk, acc)
    region_sum = acc[:, :LANES] + acc[:, LANES : 2 * LANES]
    region_count = acc[:, 2 * LANES :]
    at_least = jnp.maximum(region_count, 1.0)
    mean = region_sum / at_least
    table[...] = mean
    misfit = mean - targets[...]
    row = iota((height, LANES), 0)
    place = (row % share_rows) * LANES + iota((height, LANES), 1)
    inside = (place < share) & ((row // share_rows) * share + place < REGIONS)
    terms = jnp.where(inside, region_count * misfit * misfit, 0.0)
    loss_out[...] = jnp.sum(
        jnp.sum(terms, axis=0, keepdims=True), axis=1, keepdims=True
    ) * loss_scale
    grads[...] = jnp.where(inside, region_count * misfit / at_least, 0.0)
    mean_out[...] = table[pl.ds(me * share_rows, share_rows)]

    sub8 = iota((8, LANES), 0).astype(F32)

    def block_grads(slot):
        m = msgs[slot]
        low = jnp.broadcast_to(jnp.maximum(m[3:4], 0.0), (8, LANES)).astype(jnp.int32)
        high = m[2:3]
        total = jnp.zeros((8, LANES), F32)
        for at in range(0, height, 8):
            found = jnp.take_along_axis(grads[at : at + 8], low, axis=1)
            total = total + jnp.where(high == sub8 + float(at), found, 0.0)
        return jnp.sum(total, axis=0, keepdims=True)

    n = HALO * ccols
    half = ccols // 2
    odd_b = flags[0] == 1
    odd_t = flags[1] == 1
    up = jnp.where(odd_b, p1[n:].astype(F32), p2[n:].astype(F32))
    down = jnp.where(odd_b, p2[n:].astype(F32), p1[n:].astype(F32))
    m = HALO * (crows + 2 * HALO)
    left = jnp.where(odd_t, t1[m:].astype(F32), t2[m:].astype(F32))[:, :LANES]
    right = jnp.where(odd_t, t2[m:].astype(F32), t1[m:].astype(F32))[:, :LANES]
    maps = [
        jnp.concatenate([up[:, :LANES], up[:, LANES:]], axis=0),
        bm[...],
        jnp.concatenate([down[:, :LANES], down[:, LANES:]], axis=0),
    ]
    cells = []
    gap = jnp.zeros((4, LANES), F32)
    for v in range(3):
        mid = block_grads(flags[8 + 3 * v + 1])
        lo = block_grads(flags[8 + 3 * v])
        hi = block_grads(flags[8 + 3 * v + 2])
        source = jnp.broadcast_to(mid, (8, LANES))
        parts = [
            jnp.take_along_axis(source, maps[v][at : at + 8].astype(jnp.int32), axis=1)
            for at in range(0, ccols, 8)
        ]
        edge = jnp.concatenate(
            [right[2 * v : 2 * v + 2], gap, left[2 * v : 2 * v + 2]], axis=0
        ).astype(jnp.int32)
        source = jnp.concatenate(
            [jnp.broadcast_to(hi, (4, LANES)), jnp.broadcast_to(lo, (4, LANES))], axis=0
        )
        parts.append(jnp.take_along_axis(source, edge, axis=1))
        cells.append(jnp.concatenate(parts, axis=0).astype(BF16))

    head = wall[...]
    head_row = (iota(head.shape, 0) % (4 * crows)) // 4
    nrow = crows + 4
    for r in range(nrow):
        v = 0 if r < 2 else 1 if r < crows + 2 else 2
        i = (crows - 2 + r) if v == 0 else (r - 2) if v == 1 else r - crows - 2
        weights = jnp.where(head_row == i, head, 0.0).astype(BF16)
        deep = rounded(dot(cells[v], weights))
        mixing[r] = deep
        field[r] = deep * slope_deep[r]

    def keep_mix(r, span, value):
        mixing[r + 1, :, span] = rounded(mixing[r + 1, :, span] + value)

    def reversed_taps(k):
        k = k[...].astype(F32)
        return jnp.concatenate([k[t : t + 1] for t in range(8, -1, -1)], axis=0)

    def first_pass():
        kernel = reversed_taps(k_deep)
        for h in range(0, chan, LANES):
            span = slice(h, h + LANES)
            taps = [kernel[t : t + 1, span] for t in range(9)]

            def parts_of(r):
                x = field[r, :, span]
                before = pltpu.roll(x, 1, 0)
                after = pltpu.roll(x, width - 1, 0)
                return [
                    taps[3 * a] * before + taps[3 * a + 1] * x + taps[3 * a + 2] * after
                    for a in range(3)
                ]

            def body(r, carry):
                older, newer = carry
                p = parts_of(r)
                keep_mix(r - 2, span, older + p[2])
                return newer + p[1], p[0]

            a = parts_of(0)
            b = parts_of(1)
            lax.fori_loop(2, nrow, body, (a[0] + b[1], b[0]))

    first_pass()
    weights = w_mix[...]

    def unmix(g, carry):
        pre = (mixing[pl.ds(2 * g + 1, 2)] * slope_mix[pl.ds(2 * g + 2, 2)]).reshape(
            2 * width, chan
        )
        field[pl.ds(2 * g, 2)] = dot_nt(pre.astype(BF16), weights).reshape(2, width, chan)
        return carry

    lax.fori_loop(0, (nrow - 2) // 2, unmix, 0)

    def keep_first(r, span, value):
        total = mixing[r + 2, 0:ccols, span] + value[0:ccols]
        proj[r, :, span] = (total * slope_first[r, :, span]).astype(BF16)

    conv_pass(field, nrow - 2, reversed_taps(k_first), keep_first, chan)

    c_pad = 32
    out = dot_nt(
        padded_embed(w_embed, c_in, c_pad), proj[...].reshape(crows * ccols, chan)
    ).astype(BF16)
    wide = 4 * c_pad
    lhs = jnp.concatenate(
        [
            jnp.concatenate(
                [
                    out[b * wide : (b + 1) * wide, i * ccols : (i + 1) * ccols]
                    for b in range(4)
                ],
                axis=1,
            )
            for i in range(crows)
        ],
        axis=0,
    )
    fine = dot(lhs, spread_matrix(4 * ccols))
    for r in range(4 * crows):
        grad_out[r] = fine[r * c_pad : r * c_pad + c_in].astype(BF16)


def call(kernel, outs, scratch=(), flops=10**6, smem=True):
    def run(*args):
        space = [pl.BlockSpec(memory_space=pltpu.VMEM)] * len(args)
        if smem:
            space[0] = pl.BlockSpec(memory_space=pltpu.SMEM)
        return pl.pallas_call(
            kernel,
            out_shape=[jax.ShapeDtypeStruct(s, d) for s, d in outs],
            in_specs=space,
            out_specs=[pl.BlockSpec(memory_space=pltpu.VMEM)] * len(outs),
            scratch_shapes=[pltpu.VMEM(s, d) for s, d in scratch],
            compiler_params=pltpu.CompilerParams(vmem_limit_bytes=VMEM_LIMIT),
            cost_estimate=pl.CostEstimate(flops=flops, bytes_accessed=10**6, transcendentals=0),
        )(*args)

    return run


def exchange(m1, m2, axis):
    size = lax.axis_size(axis)
    even = [(i, i + 1) for i in range(0, size - 1, 2)]
    odd = [(i, i + 1) for i in range(1, size - 1, 2)]
    both = lambda pairs: pairs + [(j, i) for i, j in pairs]
    return lax.ppermute(m1, axis, both(even)), lax.ppermute(m2, axis, both(odd))


def per_device(
    features, land_mask, cell_blocks, region_ids, targets, w_embed, k_first, w_mix, k_deep, w_head
):
    rows, cols = land_mask.shape
    crows, ccols = rows // 4, cols // 4
    c_in = features.shape[2]
    chan = w_embed.shape[1]
    width = ccols + 2 * HALO
    nblk = cell_blocks.shape[-2]
    bands, tiles = lax.axis_size("band"), lax.axis_size("tile")
    band, tile = lax.axis_index("band"), lax.axis_index("tile")
    ndev = bands * tiles
    share = targets.shape[0]
    share_rows = pl.next_power_of_2(pl.cdiv(share, LANES))
    msg_rows = pl.cdiv(4 + share_rows, 8) * 8
    me = tile * bands + band

    slots = []
    for v in (-1, 0, 1):
        for t in (-1, 0, 1):
            nb, nt = band + v, tile + t
            ok = (nb >= 0) & (nb < bands) & (nt >= 0) & (nt < tiles)
            slots.append(jnp.where(ok, (nt * bands + nb) ^ me, 0))
    flags = jnp.stack(
        [
            band % 2, tile % 2, band == 0, band == bands - 1, tile == 0, tile == tiles - 1, me, me,
        ]
        + slots
    ).astype(jnp.int32)

    rid = region_ids.reshape(1, nblk)
    owner, place = rid // share, rid % share
    pad = ((0, 0), (1, LANES - 1 - nblk))
    high = jnp.pad(owner * share_rows + place // LANES, pad, constant_values=-1)
    low = jnp.pad(place % LANES, pad, constant_values=-1)
    blank = jnp.zeros((1, LANES), F32)
    tgt = jnp.pad(targets, (0, share_rows * LANES - share)).reshape(share_rows, LANES)
    msg_in = jnp.concatenate(
        [blank, blank, high.astype(F32), low.astype(F32)]
        + [jnp.zeros((msg_rows - 4 - share_rows, LANES), F32), tgt],
        axis=0,
    )
    head = w_head.T.reshape(4, 4, chan).transpose(1, 0, 2).astype(F32)
    wall = jnp.broadcast_to(head[:, None], (4, crows, 4, chan)).reshape(16 * crows, chan)

    feat = features.transpose(0, 2, 1)
    msg1 = HALO * ccols + ccols // 2
    pre_first, act, bm, m1, m2 = call(
        embed_kernel,
        [
            ((crows * ccols, chan), F32),
            ((crows, ccols, chan), BF16),
            ((ccols, LANES), F32),
            ((msg1, chan), BF16),
            ((msg1, chan), BF16),
        ],
        [((LANES, 9 * LANES), BF16), ((ccols, 9 * LANES), BF16)],
    )(flags, feat, w_embed, land_mask, cell_blocks.reshape(nblk, LANES))
    p1, p2 = exchange(m1, m2, "band")
    msg2 = HALO * (crows + 2 * HALO) + 16
    m1, m2 = call(edges_kernel, [((msg2, chan), BF16)] * 2)(flags, act, bm, p1, p2)
    t1, t2 = exchange(m1, m2, "tile")
    nrow = crows + 2 * HALO
    pre_mix, pre_deep, pred, msg = call(
        forward_kernel,
        [
            ((nrow - 2, width, chan), F32),
            ((nrow - 4, width, chan), F32),
            ((ccols, LANES), F32),
            ((msg_rows, LANES), F32),
        ],
        [((nrow, width, chan), F32), ((nrow - 2, width, chan), F32)],
    )(flags, act, bm, p1, p2, t1, t2, w_mix, k_first, k_deep, wall, msg_in)

    (slope_first,) = call(slope_kernel, [((crows * ccols, chan), F32)], smem=False)(pre_first)
    (slope_mix,) = call(slope_kernel, [((nrow - 2, width, chan), F32)], smem=False)(pre_mix)
    slope_deep, cell_pred = call(
        slope_pred_kernel, [((nrow - 4, width, chan), F32), ((rows, cols), F32)], smem=False
    )(pre_deep, pred, land_mask)

    msgs = msg[None]
    for axis, size in (("band", bands), ("tile", tiles)):
        step = 1
        while step < size:
            other = lax.ppermute(msgs, axis, [(i, i ^ step) for i in range(size)])
            msgs = jnp.concatenate([msgs, other], axis=0)
            step *= 2

    height = ndev * share_rows
    mean, loss, grad = call(
        functools.partial(
            backward_kernel,
            share_rows=share_rows,
            share=share,
            count=ndev,
            loss_scale=1.0 / (2.0 * rows * cols * ndev),
            c_in=c_in,
        ),
        [((share_rows, LANES), F32), ((1, 1), F32), ((rows, c_in, cols), BF16)],
        [
            ((height, LANES), F32),
            ((height, LANES), F32),
            ((height, LANES), F32),
            ((nrow - 4, width, chan), F32),
            ((nrow - 4, width, chan), F32),
            ((crows, ccols, chan), BF16),
        ],
    )(
        flags, msgs, bm, p1, p2, t1, t2, slope_deep, slope_mix,
        slope_first.reshape(crows, ccols, chan), w_mix, k_first, k_deep, wall, w_embed,
    )
    return (
        cell_pred,
        mean.reshape(-1)[:share],
        loss.reshape(1),
        grad.transpose(0, 2, 1),
    )


def solution(mesh):
    in_specs = (
        P(("group", "band"), "tile", None),
        P("band", "tile"),
        P("band", "tile", None, None),
        P("band", "tile", None),
        P(("group", "tile", "band")),
        P(),
        P(),
        P(),
        P(),
        P(),
    )
    out_specs = (
        P(("group", "band"), "tile"),
        P(("group", "tile", "band")),
        P("group"),
        P(("group", "band"), "tile", None),
    )
    return jax.shard_map(
        per_device, mesh=mesh, in_specs=in_specs, out_specs=out_specs, check_vma=False
    )
```

time: 410 us -> 48.2 us (0.12)
  local copies, waits for them, and re-layouts: 118 us -> 3.36 us
  waiting for transfers between devices: 104 us -> 6.77 us
  other arithmetic: 66.7 us -> 0.14 us
  blocking collectives: 61.2 us -> 0 us
  Pallas kernels: 0 us -> 17.1 us
  between operations: 17.9 us -> 0.9 us
  starting transfers between devices: 35.8 us -> 19.6 us
    gather x3 -> x0, local copies, waits for them, and re-layouts: 108 us -> none  [the longest x1 53.6 us: per_device(): jnp.take(flat_land, slot_index).reshape(-1, block_len).sum(-1)]
    unnamed x2 -> x0, waiting for transfers between devices: 92.2 us -> none
    scatter-add x3 -> x0, other arithmetic: 62.6 us -> none  [the longest x1 59.4 us: per_device(): jnp.zeros((fine_rows * fine_cols + 1,), jnp.float32).at[slot_index]]
    psum x1 -> x0, blocking collectives: 61.2 us -> none  [per_device(): lax.psum(local_loss, ('tile', 'band')) / (2.0 * cell_total)]
    pallas_call x0 -> x7, Pallas kernels: none -> 17.1 us  [run(): pl.pallas_call(kernel, out_shape=[jax.ShapeDtypeStruct(s, d) for s, d in...]
    ppermute x16 -> x8, starting transfers between devices: 35.8 us -> 19.6 us  [the longest x4 15.1 us: per_device(): other = lax.ppermute(msgs, axis, [(i, i ^ step) for i in range(size)])]
    ppermute x16 -> x8, waiting for transfers between devices: 12.2 us -> 6.77 us  [the longest x4 5.9 us: per_device(): other = lax.ppermute(msgs, axis, [(i, i ^ step) for i in range(size)])]
  transfers between devices with their start and end apart: 17 -> 8, of which waited for: 8 -> 4; matrix products, arithmetic and copies ran while one was open for 0% -> 1% of each run, Pallas kernels for 0% -> 4%
where the time goes in v1:
time: 48.2 us; the launch traced here: 47.9 us
  starting transfers between devices  19.6 us (41%)
  Pallas kernels  17.1 us (35%)
  waiting for transfers between devices  6.77 us (14%)
  local copies, waits for them, and re-layouts  3.36 us (7%)
  between operations  0.9 us (2%)
    pallas_call x7, Pallas kernels, run(): pl.pallas_call(kernel, out_shape=[jax.ShapeDtypeStruct(s, d) for s, d in...  17.1 us
    ppermute x4, starting transfers between devices, per_device(): other = lax.ppermute(msgs, axis, [(i, i ^ step) for i in range(size)])  15.1 us
    ppermute x4, waiting for transfers between devices, per_device(): other = lax.ppermute(msgs, axis, [(i, i ^ step) for i in range(size)])  5.9 us
    ppermute x2, starting transfers between devices, exchange(): lax.ppermute(m1, axis, both(even))  3.18 us
    unnamed x23, local copies, waits for them, and re-layouts  3.15 us
    ppermute x2, starting transfers between devices, exchange(): lax.ppermute(m2, axis, both(odd))  1.31 us
  transfers between devices with their start and end apart: 8, of which 4 were waited for; matrix products, arithmetic and copies ran while one was open for 1% of the time, Pallas kernels for 4%

profile of v1, /device:TPU:0, one launch (start us, length us, event | category | flops | bytes accessed | tf_op | source)
XLA Modules:
  0.0 47.9 jit_solution(864165449763299415)
XLA Ops:
  0.7 0.8 %copy.17 = s32[1,1,81,128]{3,2,1,0:T(8,128)S(1)} copy(s32[1,1,81,128]{3,1,2,0:T(1,128)} %param.12) | data formatting | bytes 82944
  1.5 0.1 stack.81.flags
  1.6 0.7 %copy-done.3 = s32[32,256]{1,0:T(8,128)S(1)} copy-done((s32[32,256]{1,0:T(8,128)S(1)}, s32[32,256]{1,0:T(8,128)}, u32[]{:S(2)}) %copy-start.3) | copy-done | bytes 32792
  2.3 1.0 %copy-done.2 = bf16[32,256,24]{1,2,0:T(8,128)(2,1)S(1)} copy-done((bf16[32,256,24]{1,2,0:T(8,128)(2,1)S(1)}, bf16[32,256,24]{1,2,0:T(8,128)(2,1)}, u32[]{:S(2)}) %copy-start.2) | copy-done | bytes 393240
  3.3 2.7 %shard_map.129 = (f32[512,256]{1,0:T(8,128)S(1)}, bf16[8,64,256]{2,1,0:T(8,128)(2,1)S(1)}, f32[64,128]{1,0:T(8,128)S(1)}, bf16[288,256]{1,0:T(8,128)(2,1)S(1)}, bf16[288,256]{1,0:T(8,128)(2,1)S(1)}) custom-call(s32[17]{0:T(128)S(1)} %stack.81.flags, bf16[32,24,256]{2,1,0:T(8,128)(2,1)S(1)} %bitcast.52, bf16[384,256]{1,0:T(8,128)(2,1)S(1)} %copy-done, ...), custom_call_target="tpu_custom_call" | custom-call | flops 1000000 | bytes 1000000 | tf_op jit(solution)/shard_map/pallas_call | solution.py:477
  6.0 0.5 %collective-permute-start = (bf16[288,256]{1,0:T(8,128)(2,1)S(1)}, bf16[288,256]{1,0:T(8,128)(2,1)S(1)}, u32[]{:S(2)}, u32[]{:S(2)}) collective-permute-start(bf16[288,256]{1,0:T(8,128)(2,1)S(1)} %get-tuple-element.22), channel_id=1, source_target_pairs={{0,1},{2,3},{1,0},{3,2},{4,5},{6,7},{5,4},{7,6},{8,9},{10,11},{9,8... | collective-permute-start | bytes 442376 | tf_op jit(solution)/shard_map/ppermute | solution.py:495
  6.5 0.7 %collective-permute-start.1 = (bf16[288,256]{1,0:T(8,128)(2,1)S(1)}, bf16[288,256]{1,0:T(8,128)(2,1)S(1)}, u32[]{:S(2)}, u32[]{:S(2)}) collective-permute-start(bf16[288,256]{1,0:T(8,128)(2,1)S(1)} %get-tuple-element.23), channel_id=1, source_target_pairs={{1,2},{2,1},{5,6},{6,5},{9,10},{10,9},{13,14},{14,13},{17,18},{18,... | collective-permute-start | bytes 442376 | tf_op jit(solution)/shard_map/ppermute | solution.py:495
  7.3 0.6 %copy-done.7 = f32[880]{0:T(1024)S(1)} copy-done((f32[880]{0:T(1024)S(1)}, f32[880]{0:T(1024)}, u32[]{:S(2)}) %copy-start.7) | copy-done | bytes 3544
  7.9 0.6 %shard_map.130 = (bf16[80,256]{1,0:T(8,128)(2,1)S(1)}, bf16[80,256]{1,0:T(8,128)(2,1)S(1)}) custom-call(s32[17]{0:T(128)S(1)} %stack.81.flags, bf16[8,64,256]{2,1,0:T(8,128)(2,1)S(1)} %get-tuple-element.20.act, f32[64,128]{1,0:T(8,128)S(1)} %get-tuple-element.21.bm, bf16[288,256]{1,0:T(8,128)(2,1)S(1)} %collective-permute-done.p1, ...), custom_call_target="tpu_custom_call" | custom-call | flops 1000000 | bytes 1000000 | tf_op jit(solution)/shard_map/pallas_call | solution.py:477
  8.5 2.7 %collective-permute-start.2 = (bf16[80,256]{1,0:T(8,128)(2,1)S(1)}, bf16[80,256]{1,0:T(8,128)(2,1)S(1)}, u32[]{:S(2)}, u32[]{:S(2)}) collective-permute-start(bf16[80,256]{1,0:T(8,128)(2,1)S(1)} %get-tuple-element.24), channel_id=1, source_target_pairs={{0,4},{8,12},{4,0},{12,8},{1,5},{9,13},{5,1},{13,9},{2,6},{10,14},... | collective-permute-start | bytes 122888 | tf_op jit(solution)/shard_map/ppermute | solution.py:495
  11.2 0.7 %collective-permute-start.3 = (bf16[80,256]{1,0:T(8,128)(2,1)S(1)}, bf16[80,256]{1,0:T(8,128)(2,1)S(1)}, u32[]{:S(2)}, u32[]{:S(2)}) collective-permute-start(bf16[80,256]{1,0:T(8,128)(2,1)S(1)} %get-tuple-element.25), channel_id=1, source_target_pairs={{4,8},{8,4},{5,9},{9,5},{6,10},{10,6},{7,11},{11,7},{20,24},{24,20... | collective-permute-start | bytes 122888 | tf_op jit(solution)/shard_map/ppermute | solution.py:495
  12.1 0.2 shard_map.134
  12.3 0.9 %collective-permute-done.2.t1 = bf16[80,256]{1,0:T(8,128)(2,1)S(1)} collective-permute-done((bf16[80,256]{1,0:T(8,128)(2,1)S(1)}, bf16[80,256]{1,0:T(8,128)(2,1)S(1)}, u32[]{:S(2)}, u32[]{:S(2)}) %collective-permute-start.2) | collective-permute-done | bytes 40992 | tf_op jit(solution)/shard_map/ppermute | solution.py:495
  13.2 5.9 %shard_map.131 = (f32[14,72,256]{2,1,0:T(8,128)S(1)}, f32[12,72,256]{2,1,0:T(8,128)S(1)}, f32[64,128]{1,0:T(8,128)S(1)}, f32[16,128]{1,0:T(8,128)S(1)}) custom-call(s32[17]{0:T(128)S(1)} %stack.81.flags, bf16[8,64,256]{2,1,0:T(8,128)(2,1)S(1)} %get-tuple-element.20.act, f32[64,128]{1,0:T(8,128)S(1)} %get-tuple-element.21.bm, ...), custom_call_target="tpu_custom_call" | custom-call | flops 1000000 | bytes 1000000 | tf_op jit(solution)/shard_map/pallas_call | solution.py:477
  19.1 5.1 %collective-permute-start.4 = (f32[1,16,128]{2,1,0:T(8,128)S(1)}, f32[1,16,128]{2,1,0:T(8,128)S(1)}, u32[]{:S(2)}, u32[]{:S(2)}) collective-permute-start(f32[1,16,128]{2,1,0:T(8,128)S(1)} %bitcast.54), channel_id=1, source_target_pairs={{0,1},{1,0},{2,3},{3,2},{4,5},{5,4},{6,7},{7,6},{8,9},{9,8},{10,11... | collective-permute-start | bytes 24584 | tf_op jit(solution)/shard_map/ppermute | solution.py:582
  24.2 0.4 shard_map.133.slope_mix
  24.6 1.4 %shard_map.132 = (f32[12,72,256]{2,1,0:T(8,128)S(1)}, f32[32,256]{1,0:T(8,128)}) custom-call(f32[12,72,256]{2,1,0:T(8,128)S(1)} %get-tuple-element.26.src, f32[64,128]{1,0:T(8,128)S(1)} %get-tuple-element.27.pred, s32[32,256]{1,0:T(8,128)S(1)} %copy-done.3), custom_call_target="tpu_custom_call" | custom-call | flops 1000000 | bytes 1000000 | tf_op jit(solution)/shard_map/pallas_call | solution.py:477
  26.0 2.0 %collective-permute-start.5 = (f32[2,16,128]{2,1,0:T(8,128)S(1)}, f32[2,16,128]{2,1,0:T(8,128)S(1)}, u32[]{:S(2)}, u32[]{:S(2)}) collective-permute-start(f32[2,16,128]{2,1,0:T(8,128)S(1)} %pad_maximum_fusion.2), channel_id=1, source_target_pairs={{0,2},{1,3},{2,0},{3,1},{4,6},{5,7},{6,4},{7,5},{8,10},{9,11},{10,... | collective-permute-start | bytes 49160 | tf_op jit(solution)/shard_map/ppermute | solution.py:582
  28.0 1.8 %collective-permute-done.5 = f32[2,16,128]{2,1,0:T(8,128)S(1)} collective-permute-done((f32[2,16,128]{2,1,0:T(8,128)S(1)}, f32[2,16,128]{2,1,0:T(8,128)S(1)}, u32[]{:S(2)}, u32[]{:S(2)}) %collective-permute-start.5) | collective-permute-done | bytes 16416 | tf_op jit(solution)/shard_map/ppermute | solution.py:582
  29.7 4.5 %collective-permute-start.6 = (f32[4,16,128]{2,1,0:T(8,128)S(1)}, f32[4,16,128]{2,1,0:T(8,128)S(1)}, u32[]{:S(2)}, u32[]{:S(2)}) collective-permute-start(f32[4,16,128]{2,1,0:T(8,128)S(1)} %pad_maximum_fusion.1), channel_id=1, source_target_pairs={{0,4},{4,0},{8,12},{12,8},{1,5},{5,1},{9,13},{13,9},{2,6},{6,2},{1... | collective-permute-start | bytes 98312 | tf_op jit(solution)/shard_map/ppermute | solution.py:582
  34.3 1.9 %collective-permute-done.6 = f32[4,16,128]{2,1,0:T(8,128)S(1)} collective-permute-done((f32[4,16,128]{2,1,0:T(8,128)S(1)}, f32[4,16,128]{2,1,0:T(8,128)S(1)}, u32[]{:S(2)}, u32[]{:S(2)}) %collective-permute-start.6) | collective-permute-done | bytes 32800 | tf_op jit(solution)/shard_map/ppermute | solution.py:582
  36.2 3.5 %collective-permute-start.7 = (f32[8,16,128]{2,1,0:T(8,128)S(1)}, f32[8,16,128]{2,1,0:T(8,128)S(1)}, u32[]{:S(2)}, u32[]{:S(2)}) collective-permute-start(f32[8,16,128]{2,1,0:T(8,128)S(1)} %pad_maximum_fusion), channel_id=1, source_target_pairs={{0,8},{4,12},{8,0},{12,4},{1,9},{5,13},{9,1},{13,5},{2,10},{6,14},... | collective-permute-start | bytes 196616 | tf_op jit(solution)/shard_map/ppermute | solution.py:582
  39.6 2.2 %collective-permute-done.7 = f32[8,16,128]{2,1,0:T(8,128)S(1)} collective-permute-done((f32[8,16,128]{2,1,0:T(8,128)S(1)}, f32[8,16,128]{2,1,0:T(8,128)S(1)}, u32[]{:S(2)}, u32[]{:S(2)}) %collective-permute-start.7) | collective-permute-done | bytes 65568 | tf_op jit(solution)/shard_map/ppermute | solution.py:582
  41.9 6.0 %shard_map.135 = (f32[8,128]{1,0:T(8,128)}, f32[1,1]{1,0:T(1,128)}, bf16[32,24,256]{2,1,0:T(8,128)(2,1)}) custom-call(s32[17]{0:T(128)S(1)} %stack.81.flags, f32[16,16,128]{2,1,0:T(8,128)S(1)} %constant_dynamic-update-slice_fusion.msgs, f32[64,128]{1,0:T(8,128)S(1)} %get-tuple-element.21.bm, bf16[288,256]{1,0:T(8,128)(2,1)S(1)} %collective-permute-done.p1, ...), custom_call_target="tpu_custom_call" | custom-call | flops 1000000 | bytes 1000000 | tf_op jit(solution)/shard_map/pallas_call | solution.py:477
  (39 shorter events, 0.3 us)
Async XLA Ops:
  0.6 1.0 %copy-start = (bf16[384,256]{1,0:T(8,128)(2,1)S(1)}, bf16[384,256]{1,0:T(8,128)(2,1)}, u32[]{:S(2)}) copy-start(bf16[384,256]{1,0:T(8,128)(2,1)} %w_embed.3) | copy-start | bytes 589828
  1.5 0.8 %copy-start.3 = (s32[32,256]{1,0:T(8,128)S(1)}, s32[32,256]{1,0:T(8,128)}, u32[]{:S(2)}) copy-start(s32[32,256]{1,0:T(8,128)} %land.3) | copy-start | bytes 98308
  2.3 1.0 %copy-start.2 = (bf16[32,256,24]{1,2,0:T(8,128)(2,1)S(1)}, bf16[32,256,24]{1,2,0:T(8,128)(2,1)}, u32[]{:S(2)}) copy-start(bf16[32,256,24]{1,2,0:T(8,128)(2,1)} %param.10) | copy-start | bytes 1179652
  3.3 3.9 %copy-start.6 = (bf16[256,16]{0,1:T(8,128)(2,1)S(1)}, bf16[256,16]{0,1:T(8,128)(2,1)}, u32[]{:S(2)}) copy-start(bf16[256,16]{0,1:T(8,128)(2,1)} %param.19) | copy-start | bytes 24580
  6.0 1.2 %copy-start.8 = (s32[1,1,81]{2,1,0:T(1,128)S(1)}, s32[1,1,81]{2,1,0:T(1,128)}, u32[]{:S(2)}) copy-start(s32[1,1,81]{2,1,0:T(1,128)} %param.13) | copy-start | bytes 976
  6.0 1.9 %collective-permute-start = (bf16[288,256]{1,0:T(8,128)(2,1)S(1)}, bf16[288,256]{1,0:T(8,128)(2,1)S(1)}, u32[]{:S(2)}, u32[]{:S(2)}) collective-permute-start(bf16[288,256]{1,0:T(8,128)(2,1)S(1)} %get-tuple-element.22), channel_id=1, source_target_pairs={{0,1},{2,3},{1,0},{3,2},{4,5},{6,7},{5,4},{7,6},{8,9},{10,11},{9,8... | collective-permute-start | bytes 442376 | tf_op jit(solution)/shard_map/ppermute | solution.py:495
  6.5 1.4 %collective-permute-start.1 = (bf16[288,256]{1,0:T(8,128)(2,1)S(1)}, bf16[288,256]{1,0:T(8,128)(2,1)S(1)}, u32[]{:S(2)}, u32[]{:S(2)}) collective-permute-start(bf16[288,256]{1,0:T(8,128)(2,1)S(1)} %get-tuple-element.23), channel_id=1, source_target_pairs={{1,2},{2,1},{5,6},{6,5},{9,10},{10,9},{13,14},{14,13},{17,18},{18,... | collective-permute-start | bytes 442376 | tf_op jit(solution)/shard_map/ppermute | solution.py:495
  7.2 0.7 %copy-start.7 = (f32[880]{0:T(1024)S(1)}, f32[880]{0:T(1024)}, u32[]{:S(2)}) copy-start(f32[880]{0:T(1024)} %param.14) | copy-start | bytes 10564
  8.5 4.6 %collective-permute-start.2 = (bf16[80,256]{1,0:T(8,128)(2,1)S(1)}, bf16[80,256]{1,0:T(8,128)(2,1)S(1)}, u32[]{:S(2)}, u32[]{:S(2)}) collective-permute-start(bf16[80,256]{1,0:T(8,128)(2,1)S(1)} %get-tuple-element.24), channel_id=1, source_target_pairs={{0,4},{8,12},{4,0},{12,8},{1,5},{9,13},{5,1},{13,9},{2,6},{10,14},... | collective-permute-start | bytes 122888 | tf_op jit(solution)/shard_map/ppermute | solution.py:495
  11.2 2.0 %collective-permute-start.3 = (bf16[80,256]{1,0:T(8,128)(2,1)S(1)}, bf16[80,256]{1,0:T(8,128)(2,1)S(1)}, u32[]{:S(2)}, u32[]{:S(2)}) collective-permute-start(bf16[80,256]{1,0:T(8,128)(2,1)S(1)} %get-tuple-element.25), channel_id=1, source_target_pairs={{4,8},{8,4},{5,9},{9,5},{6,10},{10,6},{7,11},{11,7},{20,24},{24,20... | collective-permute-start | bytes 122888 | tf_op jit(solution)/shard_map/ppermute | solution.py:495
  12.1 1.1 %copy-start.1 = (bf16[256,256]{1,0:T(8,128)(2,1)S(1)}, bf16[256,256]{1,0:T(8,128)(2,1)}, u32[]{:S(2)}) copy-start(bf16[256,256]{1,0:T(8,128)(2,1)} %w_mix.3) | copy-start | bytes 393220
  12.1 1.1 %copy-start.4 = (bf16[9,256]{1,0:T(8,128)(2,1)S(1)}, bf16[9,256]{1,0:T(8,128)(2,1)}, u32[]{:S(2)}) copy-start(bf16[9,256]{1,0:T(8,128)(2,1)} %k_first.3) | copy-start | bytes 13828
  12.1 1.1 %copy-start.5 = (bf16[9,256]{1,0:T(8,128)(2,1)S(1)}, bf16[9,256]{1,0:T(8,128)(2,1)}, u32[]{:S(2)}) copy-start(bf16[9,256]{1,0:T(8,128)(2,1)} %k_deep.3) | copy-start | bytes 13828
  19.1 6.9 %collective-permute-start.4 = (f32[1,16,128]{2,1,0:T(8,128)S(1)}, f32[1,16,128]{2,1,0:T(8,128)S(1)}, u32[]{:S(2)}, u32[]{:S(2)}) collective-permute-start(f32[1,16,128]{2,1,0:T(8,128)S(1)} %bitcast.54), channel_id=1, source_target_pairs={{0,1},{1,0},{2,3},{3,2},{4,5},{5,4},{6,7},{7,6},{8,9},{9,8},{10,11... | collective-permute-start | bytes 24584 | tf_op jit(solution)/shard_map/ppermute | solution.py:582
  26.0 3.7 %collective-permute-start.5 = (f32[2,16,128]{2,1,0:T(8,128)S(1)}, f32[2,16,128]{2,1,0:T(8,128)S(1)}, u32[]{:S(2)}, u32[]{:S(2)}) collective-permute-start(f32[2,16,128]{2,1,0:T(8,128)S(1)} %pad_maximum_fusion.2), channel_id=1, source_target_pairs={{0,2},{1,3},{2,0},{3,1},{4,6},{5,7},{6,4},{7,5},{8,10},{9,11},{10,... | collective-permute-start | bytes 49160 | tf_op jit(solution)/shard_map/ppermute | solution.py:582
  29.7 6.4 %collective-permute-start.6 = (f32[4,16,128]{2,1,0:T(8,128)S(1)}, f32[4,16,128]{2,1,0:T(8,128)S(1)}, u32[]{:S(2)}, u32[]{:S(2)}) collective-permute-start(f32[4,16,128]{2,1,0:T(8,128)S(1)} %pad_maximum_fusion.1), channel_id=1, source_target_pairs={{0,4},{4,0},{8,12},{12,8},{1,5},{5,1},{9,13},{13,9},{2,6},{6,2},{1... | collective-permute-start | bytes 98312 | tf_op jit(solution)/shard_map/ppermute | solution.py:582
  36.2 5.7 %collective-permute-start.7 = (f32[8,16,128]{2,1,0:T(8,128)S(1)}, f32[8,16,128]{2,1,0:T(8,128)S(1)}, u32[]{:S(2)}, u32[]{:S(2)}) collective-permute-start(f32[8,16,128]{2,1,0:T(8,128)S(1)} %pad_maximum_fusion), channel_id=1, source_target_pairs={{0,8},{4,12},{8,0},{12,4},{1,9},{5,13},{9,1},{13,5},{2,10},{6,14},... | collective-permute-start | bytes 196616 | tf_op jit(solution)/shard_map/ppermute | solution.py:582

commit v2 on v1

--- a/solution.py
+++ b/solution.py
@@ -61,14 +61,51 @@
     return jnp.concatenate(parts, axis=0).astype(BF16)
 
 
+def parity(axis):
+    return lax.axis_index(axis) % 2
+
+
 def embed_kernel(
-    flags, feat, w_embed, land, blocks, pre_out, act_out, bm_out, m1_out, m2_out, hot_a, hot_b
+    feat_hbm, w_hbm, land_hbm, blocks_hbm, pre_out, act_out, bm_out, m1_out, m2_out, w_out,
+    feat, w_embed, land, blocks, hot_a, hot_b, sems,
 ):
+    pairs = ((blocks_hbm, blocks), (land_hbm, land), (feat_hbm, feat), (w_hbm, w_embed))
+    copies = [pltpu.make_async_copy(src, dst, sems.at[n]) for n, (src, dst) in enumerate(pairs)]
+    for copy in copies:
+        copy.start()
     rows, c_in, cols = feat.shape
     c_pad = 32
     crows, ccols = rows // 4, cols // 4
     nblk = blocks.shape[0]
     spread = spread_matrix(cols)
+
+    copies[0].wait()
+    shift_row = cols.bit_length() - 1
+    chunk = hot_a.shape[1] // LANES
+    total = jnp.zeros((ccols, LANES), F32)
+    sub_a = iota((LANES, LANES), 0)
+    sub_b = iota((ccols, LANES), 0)
+    for first in range(0, nblk, chunk):
+        for step in range(chunk):
+            k = first + step
+            cell = blocks[k]
+            named = cell < rows * cols
+            q = jnp.where(named, (cell & 3) * rows + (cell >> shift_row), -1)
+            j = (cell & (cols - 1)) >> 2
+            span = slice(step * LANES, (step + 1) * LANES)
+            hot_a[:, span] = jnp.where(sub_a == q, 1.0, 0.0).astype(BF16)
+            hot_b[:, span] = jnp.where(sub_b == j, float(k + 1), 0.0).astype(BF16)
+        total = total + dot_nt(hot_b[...], hot_a[...])
+    copies[1].wait()
+    land_moved = dot_nt(spread, land[...].astype(F32).astype(BF16))
+    land_q = jnp.concatenate(
+        [land_moved[b * ccols : (b + 1) * ccols, :] for b in range(4)], axis=1
+    )
+    bm = total * land_q
+    bm_out[...] = bm
+
+    copies[2].wait()
+    copies[3].wait()
     field = feat[...].astype(F32)
     field = jnp.concatenate([field, jnp.zeros((rows, c_pad - c_in, cols), F32)], axis=1)
     field = field.reshape(rows * c_pad, cols).astype(BF16)
@@ -87,45 +124,24 @@
         ],
         axis=0,
     )
-    pre = dot(lhs, padded_embed(w_embed, c_in, c_pad))
+    weights = padded_embed(w_embed, c_in, c_pad)
+    w_out[...] = weights
+    pre = dot(lhs, weights)
+    chan = pre.shape[1]
     pre_out[...] = pre
-    act_out[...] = gelu_exact(pre).astype(BF16).reshape(crows, ccols, pre.shape[1])
-
-    shift_row = cols.bit_length() - 1
-    chunk = next(c for c in (9, 8, 7, 6, 5, 4, 3, 2, 1) if nblk % c == 0)
-    total = jnp.zeros((ccols, LANES), F32)
-    sub_a = iota((LANES, LANES), 0)
-    sub_b = iota((ccols, LANES), 0)
-    for first in range(0, nblk, chunk):
-        for step in range(chunk):
-            k = first + step
-            cell = blocks[k : k + 1, :]
-            named = cell < rows * cols
-            q = jnp.where(named, (cell & 3) * rows + (cell >> shift_row), -1)
-            j = (cell & (cols - 1)) >> 2
-            span = slice(step * LANES, (step + 1) * LANES)
-            hot_a[:, span] = jnp.where(sub_a == q, 1.0, 0.0).astype(BF16)
-            hot_b[:, span] = jnp.where(sub_b == j, float(k + 1), 0.0).astype(BF16)
-        total = total + dot_nt(hot_b[...], hot_a[...])
-    land_moved = dot_nt(spread, land[...].astype(F32).astype(BF16))
-    land_q = jnp.concatenate(
-        [land_moved[b * ccols : (b + 1) * ccols, :] for b in range(4)], axis=1
-    )
-    bm = total * land_q
-    bm_out[...] = bm
+    act_out[...] = gelu_exact(pre).astype(BF16).reshape(crows, ccols, chan)
     half = ccols // 2
     bm_wide = jnp.concatenate([bm[:half], bm[half:]], axis=1).astype(BF16)
-    chan = pre.shape[1]
-    odd = flags[0]
+    odd = parity("band")
     for out, start in ((m1_out, (1 - odd) * (crows - HALO)), (m2_out, odd * (crows - HALO))):
         out[0 : HALO * ccols] = act_out[pl.ds(start, HALO)].reshape(HALO * ccols, chan)
         out[HALO * ccols :] = bm_wide
 
 
-def edges_kernel(flags, act, bm, p1, p2, m1_out, m2_out):
+def edges_kernel(act, bm, p1, p2, m1_out, m2_out):
     crows, ccols, chan = act.shape
-    odd_b = flags[0] == 1
-    odd_t = flags[1] == 1
+    odd_b = parity("band") == 1
+    odd_t = parity("tile") == 1
     n = HALO * ccols
     up = jnp.where(odd_b, p1[...].astype(F32), p2[...].astype(F32))
     down = jnp.where(odd_b, p2[...].astype(F32), p1[...].astype(F32))
@@ -182,95 +198,170 @@
         lax.fori_loop(0, count, body, (zero, zero))
 
 
+def halo_rows(act, p1, p2, t1, t2):
+    crows, ccols, chan = act.shape
+    odd_b = parity("band") == 1
+    odd_t = parity("tile") == 1
+
+    def edge(first, second, odd, at, n):
+        return jnp.where(odd, first[at : at + n].astype(F32), second[at : at + n].astype(F32))
+
+    def row(r):
+        if r < HALO:
+            own = edge(p1, p2, odd_b, r * ccols, ccols)
+        elif r < HALO + crows:
+            own = act[r - HALO].astype(F32)
+        else:
+            own = edge(p2, p1, odd_b, (r - HALO - crows) * ccols, ccols)
+        base = HALO * r // 16 * 16
+        at = HALO * r - base
+        left = edge(t1, t2, odd_t, base, 16)[at : at + HALO]
+        right = edge(t2, t1, odd_t, base, 16)[at : at + HALO]
+        return own, jnp.concatenate([right, left], axis=0)
+
+    return row
+
+
+def inside_columns(shape, ccols):
+    tile = lax.axis_index("tile")
+    first = tile == 0
+    last = tile == lax.axis_size("tile") - 1
+    col = iota(shape, len(shape) - 2)
+    low = jnp.where(last, ccols, ccols + HALO)
+    high = jnp.where(first, ccols + 2 * HALO, ccols + HALO)
+    return (col < low) | (col >= high)
+
+
+def mix_pair(pair, base, weights, ok):
+    _, width, chan = pair.shape
+    pre = dot(pair.reshape(2 * width, chan).astype(BF16), weights).reshape(2, width, chan)
+    pre = jnp.where(ok, pre, OUTSIDE)
+    return pre, rounded(base + gelu_exact(pre))
+
+
 def forward_kernel(
-    flags, act, bm, p1, p2, t1, t2, w_mix, k_first, k_deep, wall, msg_in,
-    pre_mix, pre_deep, pred_out, msg_out, field, mixed,
+    act, bm, p1, p2, t1, t2, w_mix, k_first, k_deep, wall, msg_in,
+    field, act_mix, pre_mix, pre_deep, pred_out, msg_out, mixed,
 ):
     crows, ccols, chan = act.shape
     width = ccols + 2 * HALO
-    odd_b = flags[0] == 1
-    odd_t = flags[1] == 1
-    nrow = crows + 2 * HALO
-    n = HALO * ccols
-    up = jnp.where(odd_b, p1[0:n].astype(F32), p2[0:n].astype(F32))
-    down = jnp.where(odd_b, p2[0:n].astype(F32), p1[0:n].astype(F32))
-    m = HALO * nrow
-    left = jnp.where(odd_t, t1[0:m].astype(F32), t2[0:m].astype(F32))
-    right = jnp.where(odd_t, t2[0:m].astype(F32), t1[0:m].astype(F32))
-    for r in range(nrow):
-        if r < HALO:
-            row = up[r * ccols : (r + 1) * ccols]
-        elif r < HALO + crows:
-            row = act[r - HALO].astype(F32)
-        else:
-            row = down[(r - HALO - crows) * ccols : (r - HALO - crows + 1) * ccols]
-        field[r, 0:ccols, :] = row
-        field[r, ccols:, :] = jnp.concatenate(
-            [right[HALO * r : HALO * (r + 1)], left[HALO * r : HALO * (r + 1)]], axis=0
-        )
+    row = halo_rows(act, p1, p2, t1, t2)
+    for r in range(crows + 4):
+        own, edge = row(r + 2)
+        field[r, 0:ccols, :] = own
+        field[r, ccols:, :] = edge
 
     def keep_mixed(r, span, value):
         mixed[r, :, span] = value
 
-    conv_pass(field, nrow, k_first[...].astype(F32), keep_mixed, chan)
-
-    col = iota((1, width, chan), 1)
-    col_ok = (col < ccols) | ((col < ccols + HALO) & (flags[5] == 0)) | (
-        (col >= ccols + HALO) & (flags[4] == 0)
-    )
-    first_row = flags[2] * (HALO - 1)
-    last_row = nrow - 2 - flags[3] * (HALO - 1)
+    conv_pass(field, crows + 4, k_first[...].astype(F32), keep_mixed, chan)
+
+    shape = (2, width, chan)
+    col_ok = inside_columns(shape, ccols)
+    band = lax.axis_index("band")
+    first_row = jnp.where(band == 0, 1, 0)
+    last_row = jnp.where(band == lax.axis_size("band") - 1, crows + 1, crows + 2)
     weights = w_mix[...]
-
-    def mix(g, carry):
-        pair = mixed[pl.ds(2 * g, 2)].reshape(2 * width, chan).astype(BF16)
-        pre = dot(pair, weights).reshape(2, width, chan)
-        row = iota((2, width, chan), 0) + 2 * g
-        ok = col_ok & (row >= first_row) & (row < last_row)
-        pre = jnp.where(ok, pre, OUTSIDE)
-        pre_mix[pl.ds(2 * g, 2)] = pre
-        mixed[pl.ds(2 * g, 2)] = rounded(field[pl.ds(2 * g + 1, 2)] + gelu_exact(pre))
-        return carry
-
-    lax.fori_loop(0, (nrow - 2) // 2, mix, 0)
+    for g in range((crows + 2) // 2):
+        at = iota(shape, 0) + 2 * g
+        ok = col_ok & (at >= first_row) & (at < last_row)
+        pair = slice(2 * g, 2 * g + 2)
+        pre, post = mix_pair(mixed[pair], field[2 * g + 1 : 2 * g + 3], weights, ok)
+        pre_mix[pair] = pre
+        act_mix[pair] = post
 
     def keep_deep(r, span, value):
         pre_deep[r, :, span] = value
 
-    conv_pass(mixed, nrow - 2, k_deep[...].astype(F32), keep_deep, chan)
+    conv_pass(act_mix, crows + 2, k_deep[...].astype(F32), keep_deep, chan)
 
     head = wall[...]
     head_row = (iota(head.shape, 0) % (4 * crows)) // 4
-
-    def deep(i, pred):
-        pre = pre_deep[i + 2, 0:ccols, :]
-        out = (mixed[i + 3, 0:ccols, :] + gelu_exact(pre)).astype(BF16)
-        return pred + dot_nt(out, jnp.where(head_row == i, head, 0.0).astype(BF16))
-
-    pred = lax.fori_loop(0, crows, deep, jnp.zeros((ccols, LANES), F32))
+    pred = jnp.zeros((ccols, LANES), F32)
+    for i in range(crows):
+        out = act_mix[i + 1, 0:ccols, :] + gelu_exact(pre_deep[i, 0:ccols, :])
+        pred = pred + dot_nt(
+            out.astype(BF16), jnp.where(head_row == i, head, 0.0).astype(BF16)
+        )
     pred_out[...] = pred
 
     maps = bm[...]
     slots = iota((LANES, LANES), 0).astype(F32)[:88]
     sums = jnp.zeros((88, LANES), F32)
+    for j in range(ccols):
+        sums = sums + jnp.where(maps[j : j + 1, :] == slots, pred[j : j + 1, :], 0.0)
+    msg_out[...] = msg_in[...]
+    msg_out[0:1, :] = across_lanes(sums)
+
+
+def across_lanes(acc):
+    rest = jnp.zeros((LANES - acc.shape[0], LANES), F32)
+    turned = jnp.concatenate([acc, rest], axis=0).T
+    total = jnp.sum(turned, axis=0, keepdims=True)
+    return jnp.where(iota((1, LANES), 1) > 0, total, 0.0)
+
+
+def count_kernel(pre_first, bm, msg_in, slope_first, msg_out):
+    slope_first[...] = gelu_slope(pre_first[...])
+    maps = bm[...]
+    slots = iota((LANES, LANES), 0).astype(F32)[:88]
     counts = jnp.zeros((88, LANES), F32)
-    for j in range(ccols):
-        hit = maps[j : j + 1, :] == slots
-        sums = sums + jnp.where(hit, pred[j : j + 1, :], 0.0)
-        counts = counts + jnp.where(hit, 1.0, 0.0)
+    for j in range(maps.shape[0]):
+        counts = counts + jnp.where(maps[j : j + 1, :] == slots, 1.0, 0.0)
     msg_out[...] = msg_in[...]
-    used = iota((1, LANES), 1) > 0
-    rest = jnp.zeros((LANES - 88, LANES), F32)
-    for at, acc in enumerate((sums, counts)):
-        across = jnp.concatenate([acc, rest], axis=0).T
-        msg_out[at : at + 1, :] = jnp.where(used, jnp.sum(across, axis=0, keepdims=True), 0.0)
-
-
-def slope_kernel(src, out):
+    msg_out[1:2, :] = across_lanes(counts)
+
+
+def rim_kernel(
+    after, act, p1, p2, t1, t2, w_mix, k_first, k_deep, field, act_mix, slope_rim,
+    ext, mixed,
+):
+    del after
+    crows, ccols, chan = act.shape
+    width = ccols + 2 * HALO
+    row = halo_rows(act, p1, p2, t1, t2)
+    first, second = k_first[...].astype(F32), k_deep[...].astype(F32)
+    weights = w_mix[...]
+    shape = (2, width, chan)
+    col_ok = inside_columns(shape, ccols)
+    band = lax.axis_index("band")
+    for side in range(2):
+        outer = (0, 1) if side == 0 else (crows + 6, crows + 7)
+        inner = (0, 1) if side == 0 else (crows + 2, crows + 3)
+        spots = (0, 1) if side == 0 else (2, 3)
+        for r, at in zip(outer, spots):
+            own, edge = row(r)
+            ext[at, 0:ccols, :] = own
+            ext[at, ccols:, :] = edge
+        for r, at in zip(inner, (2, 3) if side == 0 else (0, 1)):
+            ext[at] = field[r]
+
+        def keep_mixed(r, span, value):
+            mixed[r, :, span] = value
+
+        conv_pass(ext, 4, first, keep_mixed, chan)
+        edge_band = 0 if side == 0 else lax.axis_size("band") - 1
+        ok = col_ok & (band != edge_band)
+        _, post = mix_pair(mixed[...], ext[1:3], weights, ok)
+        have = (0, 1) if side == 0 else (crows, crows + 1)
+        for n in range(2):
+            ext[spots[n]] = post[n]
+            ext[(2, 3)[n] if side == 0 else n] = act_mix[have[n]]
+
+        def keep_deep(r, span, value):
+            mixed[r, :, span] = value
+
+        conv_pass(ext, 4, second, keep_deep, chan)
+        slope_rim[2 * side : 2 * side + 2] = gelu_slope(mixed[...])
+
+
+def slope_kernel(after, src, out):
+    del after
     out[...] = gelu_slope(src[...])
 
 
-def slope_pred_kernel(src, pred, land, out, cells):
+def slope_pred_kernel(after, src, pred, land, out, cells):
+    del after
     rows, cols = land.shape
     out[...] = gelu_slope(src[...])
     turned = pred[...].T
@@ -282,17 +373,25 @@
 
 
 def backward_kernel(
-    flags, msgs, bm, p1, p2, t1, t2, slope_deep, slope_mix, slope_first,
-    w_mix, k_first, k_deep, wall, w_embed,
+    msgs, bm, p1, p2, t1, t2, slope_deep, slope_rim, slope_mix, slope_first,
+    w_mix, k_first, k_deep, wall, w_wide,
     mean_out, loss_out, grad_out,
-    targets, table, grads, field, mixing, proj, share_rows, share, count, loss_scale, c_in,
+    targets, table, grads, field, mixing, proj, share_rows, share, loss_scale, c_in,
 ):
     ndev = msgs.shape[0]
     crows = slope_first.shape[0]
     ccols = slope_first.shape[1]
     chan = slope_first.shape[2]
     width = ccols + 2 * HALO
-    me = flags[6]
+    band, tile = lax.axis_index("band"), lax.axis_index("tile")
+    bands, tiles = lax.axis_size("band"), lax.axis_size("tile")
+    me = tile * bands + band
+
+    def slot_of(v, t):
+        other_band, other_tile = band + v, tile + t
+        ok = (other_band >= 0) & (other_band < bands) & (other_tile >= 0) & (other_tile < tiles)
+        return jnp.where(ok, (other_tile * bands + other_band) ^ me, 0)
+
     height = ndev * share_rows
     chunk = min(16, ndev)
     first_target = msgs.shape[1] - share_rows
@@ -353,8 +452,8 @@
 
     n = HALO * ccols
     half = ccols // 2
-    odd_b = flags[0] == 1
-    odd_t = flags[1] == 1
+    odd_b = parity("band") == 1
+    odd_t = parity("tile") == 1
     up = jnp.where(odd_b, p1[n:].astype(F32), p2[n:].astype(F32))
     down = jnp.where(odd_b, p2[n:].astype(F32), p1[n:].astype(F32))
     m = HALO * (crows + 2 * HALO)
@@ -368,9 +467,9 @@
     cells = []
     gap = jnp.zeros((4, LANES), F32)
     for v in range(3):
-        mid = block_grads(flags[8 + 3 * v + 1])
-        lo = block_grads(flags[8 + 3 * v])
-        hi = block_grads(flags[8 + 3 * v + 2])
+        mid = block_grads(slot_of(v - 1, 0))
+        lo = block_grads(slot_of(v - 1, -1))
+        hi = block_grads(slot_of(v - 1, 1))
         source = jnp.broadcast_to(mid, (8, LANES))
         parts = [
             jnp.take_along_axis(source, maps[v][at : at + 8].astype(jnp.int32), axis=1)
@@ -394,7 +493,8 @@
         weights = jnp.where(head_row == i, head, 0.0).astype(BF16)
         deep = rounded(dot(cells[v], weights))
         mixing[r] = deep
-        field[r] = deep * slope_deep[r]
+        slope = slope_rim[r] if v == 0 else slope_deep[i] if v == 1 else slope_rim[r - crows]
+        field[r] = deep * slope
 
     def keep_mix(r, span, value):
         mixing[r + 1, :, span] = rounded(mixing[r + 1, :, span] + value)
@@ -431,14 +531,11 @@
     first_pass()
     weights = w_mix[...]
 
-    def unmix(g, carry):
-        pre = (mixing[pl.ds(2 * g + 1, 2)] * slope_mix[pl.ds(2 * g + 2, 2)]).reshape(
+    for g in range((nrow - 2) // 2):
+        pre = (mixing[2 * g + 1 : 2 * g + 3] * slope_mix[2 * g : 2 * g + 2]).reshape(
             2 * width, chan
         )
-        field[pl.ds(2 * g, 2)] = dot_nt(pre.astype(BF16), weights).reshape(2, width, chan)
-        return carry
-
-    lax.fori_loop(0, (nrow - 2) // 2, unmix, 0)
+        field[2 * g : 2 * g + 2] = dot_nt(pre.astype(BF16), weights).reshape(2, width, chan)
 
     def keep_first(r, span, value):
         total = mixing[r + 2, 0:ccols, span] + value[0:ccols]
@@ -447,9 +544,7 @@
     conv_pass(field, nrow - 2, reversed_taps(k_first), keep_first, chan)
 
     c_pad = 32
-    out = dot_nt(
-        padded_embed(w_embed, c_in, c_pad), proj[...].reshape(crows * ccols, chan)
-    ).astype(BF16)
+    out = dot_nt(w_wide[...], proj[...].reshape(crows * ccols, chan)).astype(BF16)
     wide = 4 * c_pad
     lhs = jnp.concatenate(
         [
@@ -469,19 +564,23 @@
         grad_out[r] = fine[r * c_pad : r * c_pad + c_in].astype(BF16)
 
 
-def call(kernel, outs, scratch=(), flops=10**6, smem=True):
+def call(kernel, outs, scratch=(), hbm=0):
     def run(*args):
-        space = [pl.BlockSpec(memory_space=pltpu.VMEM)] * len(args)
-        if smem:
-            space[0] = pl.BlockSpec(memory_space=pltpu.SMEM)
+        space = [pl.BlockSpec(memory_space=pl.ANY)] * hbm
+        space += [pl.BlockSpec(memory_space=pltpu.VMEM)] * (len(args) - hbm)
         return pl.pallas_call(
             kernel,
             out_shape=[jax.ShapeDtypeStruct(s, d) for s, d in outs],
             in_specs=space,
             out_specs=[pl.BlockSpec(memory_space=pltpu.VMEM)] * len(outs),
-            scratch_shapes=[pltpu.VMEM(s, d) for s, d in scratch],
+            scratch_shapes=[
+                pltpu.SemaphoreType.DMA(s) if d is None else pltpu.VMEM(s, d)
+                for s, d in scratch
+            ],
             compiler_params=pltpu.CompilerParams(vmem_limit_bytes=VMEM_LIMIT),
-            cost_estimate=pl.CostEstimate(flops=flops, bytes_accessed=10**6, transcendentals=0),
+            cost_estimate=pl.CostEstimate(
+                flops=10**6, bytes_accessed=10**6, transcendentals=0
+            ),
         )(*args)
 
     return run
@@ -505,25 +604,10 @@
     width = ccols + 2 * HALO
     nblk = cell_blocks.shape[-2]
     bands, tiles = lax.axis_size("band"), lax.axis_size("tile")
-    band, tile = lax.axis_index("band"), lax.axis_index("tile")
     ndev = bands * tiles
     share = targets.shape[0]
     share_rows = pl.next_power_of_2(pl.cdiv(share, LANES))
     msg_rows = pl.cdiv(4 + share_rows, 8) * 8
-    me = tile * bands + band
-
-    slots = []
-    for v in (-1, 0, 1):
-        for t in (-1, 0, 1):
-            nb, nt = band + v, tile + t
-            ok = (nb >= 0) & (nb < bands) & (nt >= 0) & (nt < tiles)
-            slots.append(jnp.where(ok, (nt * bands + nb) ^ me, 0))
-    flags = jnp.stack(
-        [
-            band % 2, tile % 2, band == 0, band == bands - 1, tile == 0, tile == tiles - 1, me, me,
-        ]
-        + slots
-    ).astype(jnp.int32)
 
     rid = region_ids.reshape(1, nblk)
     owner, place = rid // share, rid % share
@@ -542,7 +626,8 @@
 
     feat = features.transpose(0, 2, 1)
     msg1 = HALO * ccols + ccols // 2
-    pre_first, act, bm, m1, m2 = call(
+    chunk = next(c for c in (9, 8, 7, 6, 5, 4, 3, 2, 1) if nblk % c == 0)
+    pre_first, act, bm, m1, m2, w_wide = call(
         embed_kernel,
         [
             ((crows * ccols, chan), F32),
@@ -550,38 +635,79 @@
             ((ccols, LANES), F32),
             ((msg1, chan), BF16),
             ((msg1, chan), BF16),
+            ((512, chan), BF16),
         ],
-        [((LANES, 9 * LANES), BF16), ((ccols, 9 * LANES), BF16)],
-    )(flags, feat, w_embed, land_mask, cell_blocks.reshape(nblk, LANES))
+        [
+            ((rows, c_in, cols), BF16),
+            ((16 * c_in, chan), BF16),
+            ((rows, cols), jnp.int32),
+            ((nblk, 1, LANES), jnp.int32),
+            ((LANES, chunk * LANES), BF16),
+            ((ccols, chunk * LANES), BF16),
+            ((4,), None),
+        ],
+        hbm=4,
+    )(
+        *(
+            pltpu.with_memory_space_constraint(x, pltpu.HBM)
+            for x in (feat, w_embed, land_mask, cell_blocks.reshape(nblk, 1, LANES))
+        )
+    )
     p1, p2 = exchange(m1, m2, "band")
     msg2 = HALO * (crows + 2 * HALO) + 16
-    m1, m2 = call(edges_kernel, [((msg2, chan), BF16)] * 2)(flags, act, bm, p1, p2)
+    m1, m2 = call(edges_kernel, [((msg2, chan), BF16)] * 2)(act, bm, p1, p2)
     t1, t2 = exchange(m1, m2, "tile")
+    slope_first, msg_in = call(
+        count_kernel, [((crows * ccols, chan), F32), ((msg_rows, LANES), F32)]
+    )(pre_first, bm, msg_in)
     nrow = crows + 2 * HALO
-    pre_mix, pre_deep, pred, msg = call(
+    field, act_mix, pre_mix, pre_deep, pred, msg = call(
         forward_kernel,
         [
-            ((nrow - 2, width, chan), F32),
-            ((nrow - 4, width, chan), F32),
+            ((crows + 4, width, chan), F32),
+            ((crows + 2, width, chan), F32),
+            ((crows + 2, width, chan), F32),
+            ((crows, width, chan), F32),
             ((ccols, LANES), F32),
             ((msg_rows, LANES), F32),
         ],
-        [((nrow, width, chan), F32), ((nrow - 2, width, chan), F32)],
-    )(flags, act, bm, p1, p2, t1, t2, w_mix, k_first, k_deep, wall, msg_in)
-
-    (slope_first,) = call(slope_kernel, [((crows * ccols, chan), F32)], smem=False)(pre_first)
-    (slope_mix,) = call(slope_kernel, [((nrow - 2, width, chan), F32)], smem=False)(pre_mix)
-    slope_deep, cell_pred = call(
-        slope_pred_kernel, [((nrow - 4, width, chan), F32), ((rows, cols), F32)], smem=False
-    )(pre_deep, pred, land_mask)
-
+        [((crows + 2, width, chan), F32)],
+    )(act, bm, p1, p2, t1, t2, w_mix, k_first, k_deep, wall, msg_in)
+
+    def slopes_mix(after):
+        return call(slope_kernel, [((crows + 2, width, chan), F32)], hbm=1)(after, pre_mix)
+
+    def slopes_deep(after):
+        return call(
+            slope_pred_kernel,
+            [((crows, width, chan), F32), ((rows, cols), F32)],
+            hbm=1,
+        )(after, pre_deep, pred, land_mask)
+
+    def slopes_rim(after):
+        return call(
+            rim_kernel,
+            [((4, width, chan), F32)],
+            [((4, width, chan), F32), ((2, width, chan), F32)],
+            hbm=1,
+        )(after, act, p1, p2, t1, t2, w_mix, k_first, k_deep, field, act_mix)
+
+    beside = {1: slopes_mix, 2: slopes_deep, 3: slopes_rim}
+    made = {}
     msgs = msg[None]
+    at = 0
     for axis, size in (("band", bands), ("tile", tiles)):
         step = 1
         while step < size:
+            if at in beside:
+                made[at] = beside[at](msgs)
             other = lax.ppermute(msgs, axis, [(i, i ^ step) for i in range(size)])
             msgs = jnp.concatenate([msgs, other], axis=0)
             step *= 2
+            at += 1
+    (slope_mix,) = made[1]
+    slope_deep, cell_pred = made[2]
+    (slope_rim,) = made[3]
 
     height = ndev * share_rows
     mean, loss, grad = call(
@@ -589,7 +715,6 @@
             backward_kernel,
             share_rows=share_rows,
             share=share,
-            count=ndev,
             loss_scale=1.0 / (2.0 * rows * cols * ndev),
             c_in=c_in,
         ),
@@ -603,8 +728,8 @@
             ((crows, ccols, chan), BF16),
         ],
     )(
-        flags, msgs, bm, p1, p2, t1, t2, slope_deep, slope_mix,
-        slope_first.reshape(crows, ccols, chan), w_mix, k_first, k_deep, wall, w_embed,
+        msgs, bm, p1, p2, t1, t2, slope_deep, slope_rim, slope_mix,
+        slope_first.reshape(crows, ccols, chan), w_mix, k_first, k_deep, wall, w_wide,
     )
     return (
         cell_pred,

time: 48.2 us -> 40.4 us (0.84)
  Pallas kernels: 17.1 us -> 14.4 us
  waiting for transfers between devices: 6.77 us -> 4.09 us
  local copies, waits for them, and re-layouts: 3.36 us -> 0.79 us
    pallas_call x7 -> x8, Pallas kernels: 17.1 us -> 14.4 us  [run(): pl.pallas_call(kernel, out_shape=[jax.ShapeDtypeStruct(s, d) for s, d in...]
    unnamed x23 -> x18, local copies, waits for them, and re-layouts: 3.15 us -> 0.67 us
    ppermute x4, waiting for transfers between devices: 5.9 us -> 3.65 us  [per_device(): other = lax.ppermute(msgs, axis, [(i, i ^ step) for i in range(size)])]
  transfers between devices with their start and end apart: 8 -> 8, of which waited for: 4 -> 5; matrix products, arithmetic and copies ran while one was open for 1% -> 1% of each run, Pallas kernels for 4% -> 9%
where the time goes in v2:
time: 40.4 us; the launch traced here: 40.2 us
  starting transfers between devices  19.9 us (49%)
  Pallas kernels  14.4 us (36%)
  waiting for transfers between devices  4.09 us (10%)
  between operations  0.81 us (2%)
  local copies, waits for them, and re-layouts  0.79 us (2%)
    ppermute x4, starting transfers between devices, per_device(): other = lax.ppermute(msgs, axis, [(i, i ^ step) for i in range(size)])  15.4 us
    pallas_call x8, Pallas kernels, run(): pl.pallas_call(kernel, out_shape=[jax.ShapeDtypeStruct(s, d) for s, d in...  14.4 us
    ppermute x4, waiting for transfers between devices, per_device(): other = lax.ppermute(msgs, axis, [(i, i ^ step) for i in range(size)])  3.65 us
    ppermute x2, starting transfers between devices, exchange(): lax.ppermute(m1, axis, both(even))  3.06 us
    ppermute x2, starting transfers between devices, exchange(): lax.ppermute(m2, axis, both(odd))  1.44 us
  transfers between devices with their start and end apart: 8, of which 5 were waited for; matrix products, arithmetic and copies ran while one was open for 1% of the time, Pallas kernels for 9%

profile of v2, /device:TPU:0, one launch (start us, length us, event | category | flops | bytes accessed | tf_op | source)
XLA Modules:
  0.0 40.2 jit_solution(4213033177841199534)
XLA Ops:
  0.6 3.4 %shard_map.129 = (f32[512,256]{1,0:T(8,128)S(1)}, bf16[8,64,256]{2,1,0:T(8,128)(2,1)S(1)}, f32[64,128]{1,0:T(8,128)S(1)}, bf16[288,256]{1,0:T(8,128)(2,1)S(1)}, ...) custom-call(bf16[32,24,256]{2,1,0:T(8,128)(2,1)} %bitcast.39, bf16[384,256]{1,0:T(8,128)(2,1)} %w_hbm.1, ...), custom_call_target="tpu_custom_call" | custom-call | flops 1000000 | bytes 1000000 | tf_op jit(solution)/shard_map/pallas_call | solution.py:571
  4.1 0.5 %collective-permute-start = (bf16[288,256]{1,0:T(8,128)(2,1)S(1)}, bf16[288,256]{1,0:T(8,128)(2,1)S(1)}, u32[]{:S(2)}, u32[]{:S(2)}) collective-permute-start(bf16[288,256]{1,0:T(8,128)(2,1)S(1)} %get-tuple-element.27), channel_id=1, source_target_pairs={{0,1},{2,3},{1,0},{3,2},{4,5},{6,7},{5,4},{7,6},{8,9},{10,11},{9,8... | collective-permute-start | bytes 442376 | tf_op jit(solution)/shard_map/ppermute | solution.py:594
  4.6 0.8 %collective-permute-start.1 = (bf16[288,256]{1,0:T(8,128)(2,1)S(1)}, bf16[288,256]{1,0:T(8,128)(2,1)S(1)}, u32[]{:S(2)}, u32[]{:S(2)}) collective-permute-start(bf16[288,256]{1,0:T(8,128)(2,1)S(1)} %get-tuple-element.28), channel_id=1, source_target_pairs={{1,2},{2,1},{5,6},{6,5},{9,10},{10,9},{13,14},{14,13},{17,18},{18,... | collective-permute-start | bytes 442376 | tf_op jit(solution)/shard_map/ppermute | solution.py:594
  5.4 0.0 copy-start.5
  5.5 0.6 %copy-done.5 = f32[880]{0:T(1024)S(1)} copy-done((f32[880]{0:T(1024)S(1)}, f32[880]{0:T(1024)}, u32[]{:S(2)}) %copy-start.5) | copy-done | bytes 3544
  6.2 2.5 %collective-permute-start.2 = (bf16[80,256]{1,0:T(8,128)(2,1)S(1)}, bf16[80,256]{1,0:T(8,128)(2,1)S(1)}, u32[]{:S(2)}, u32[]{:S(2)}) collective-permute-start(bf16[80,256]{1,0:T(8,128)(2,1)S(1)} %get-tuple-element.29), channel_id=1, source_target_pairs={{0,4},{8,12},{4,0},{12,8},{1,5},{9,13},{5,1},{13,9},{2,6},{10,14},... | collective-permute-start | bytes 122888 | tf_op jit(solution)/shard_map/ppermute | solution.py:594
  8.7 0.7 %collective-permute-start.3 = (bf16[80,256]{1,0:T(8,128)(2,1)S(1)}, bf16[80,256]{1,0:T(8,128)(2,1)S(1)}, u32[]{:S(2)}, u32[]{:S(2)}) collective-permute-start(bf16[80,256]{1,0:T(8,128)(2,1)S(1)} %get-tuple-element.30), channel_id=1, source_target_pairs={{4,8},{8,4},{5,9},{9,5},{6,10},{10,6},{7,11},{11,7},{20,24},{24,20... | collective-permute-start | bytes 122888 | tf_op jit(solution)/shard_map/ppermute | solution.py:594
  9.4 0.1 pad_convert_fusion
  9.6 0.0 copy-start.3
  9.6 0.6 %shard_map.131 = (f32[512,256]{1,0:T(8,128)S(1)}, f32[16,128]{1,0:T(8,128)S(1)}) custom-call(f32[512,256]{1,0:T(8,128)S(1)} %get-tuple-element.31.pre_first, f32[64,128]{1,0:T(8,128)S(1)} %get-tuple-element.26.bm, f32[16,128]{1,0:T(8,128)S(1)} %concatenate.22.msg_in), custom_call_target="tpu_custom_call" | custom-call | flops 1000000 | bytes 1000000 | tf_op jit(solution)/shard_map/pallas_call | solution.py:571
  10.3 0.4 %collective-permute-done.2.t1 = bf16[80,256]{1,0:T(8,128)(2,1)S(1)} collective-permute-done((bf16[80,256]{1,0:T(8,128)(2,1)S(1)}, bf16[80,256]{1,0:T(8,128)(2,1)S(1)}, u32[]{:S(2)}, u32[]{:S(2)}) %collective-permute-start.2) | collective-permute-done | bytes 40992 | tf_op jit(solution)/shard_map/ppermute | solution.py:594
  10.7 2.6 %shard_map.132 = (f32[12,72,256]{2,1,0:T(8,128)S(1)}, f32[10,72,256]{2,1,0:T(8,128)S(1)}, f32[10,72,256]{2,1,0:T(8,128)S(1)}, f32[8,72,256]{2,1,0:T(8,128)S(1)},...) custom-call(bf16[8,64,256]{2,1,0:T(8,128)(2,1)S(1)} %get-tuple-element.25.act, f32[64,128]{1,0:T(8,128)S(1)} %get-tuple-element.26.bm, ...), custom_call_target="tpu_custom_call" | custom-call | flops 1000000 | bytes 1000000 | tf_op jit(solution)/shard_map/pallas_call | solution.py:571
  13.3 5.2 %collective-permute-start.4 = (f32[1,16,128]{2,1,0:T(8,128)S(1)}, f32[1,16,128]{2,1,0:T(8,128)S(1)}, u32[]{:S(2)}, u32[]{:S(2)}) collective-permute-start(f32[1,16,128]{2,1,0:T(8,128)S(1)} %bitcast.35), channel_id=1, source_target_pairs={{0,1},{1,0},{2,3},{3,2},{4,5},{5,4},{6,7},{7,6},{8,9},{9,8},{10,11... | collective-permute-start | bytes 24584 | tf_op jit(solution)/shard_map/ppermute | solution.py:704
  18.5 0.8 %collective-permute-done.4 = f32[1,16,128]{2,1,0:T(8,128)S(1)} collective-permute-done((f32[1,16,128]{2,1,0:T(8,128)S(1)}, f32[1,16,128]{2,1,0:T(8,128)S(1)}, u32[]{:S(2)}, u32[]{:S(2)}) %collective-permute-start.4) | collective-permute-done | bytes 8224 | tf_op jit(solution)/shard_map/ppermute | solution.py:704
  19.4 2.2 %collective-permute-start.5 = (f32[2,16,128]{2,1,0:T(8,128)S(1)}, f32[2,16,128]{2,1,0:T(8,128)S(1)}, u32[]{:S(2)}, u32[]{:S(2)}) collective-permute-start(f32[2,16,128]{2,1,0:T(8,128)S(1)} %pad_maximum_fusion.2.after), channel_id=1, source_target_pairs={{0,2},{1,3},{2,0},{3,1},{4,6},{5,7},{6,4},{7,5},{8,10},{9,11},{10,... | collective-permute-start | bytes 49160 | tf_op jit(solution)/shard_map/ppermute | solution.py:704
  21.5 0.3 shard_map.135.slope_mix
  21.8 1.4 %collective-permute-done.5 = f32[2,16,128]{2,1,0:T(8,128)S(1)} collective-permute-done((f32[2,16,128]{2,1,0:T(8,128)S(1)}, f32[2,16,128]{2,1,0:T(8,128)S(1)}, u32[]{:S(2)}, u32[]{:S(2)}) %collective-permute-start.5) | collective-permute-done | bytes 16416 | tf_op jit(solution)/shard_map/ppermute | solution.py:704
  23.3 4.6 %collective-permute-start.6 = (f32[4,16,128]{2,1,0:T(8,128)S(1)}, f32[4,16,128]{2,1,0:T(8,128)S(1)}, u32[]{:S(2)}, u32[]{:S(2)}) collective-permute-start(f32[4,16,128]{2,1,0:T(8,128)S(1)} %pad_maximum_fusion.1.after), channel_id=1, source_target_pairs={{0,4},{4,0},{8,12},{12,8},{1,5},{5,1},{9,13},{13,9},{2,6},{6,2},{1... | collective-permute-start | bytes 98312 | tf_op jit(solution)/shard_map/ppermute | solution.py:704
  27.8 1.1 %shard_map.133 = (f32[8,72,256]{2,1,0:T(8,128)S(1)}, f32[32,256]{1,0:T(8,128)}) custom-call(f32[4,16,128]{2,1,0:T(8,128)S(1)} %pad_maximum_fusion.1.after, f32[8,72,256]{2,1,0:T(8,128)S(1)} %get-tuple-element.34.src, f32[64,128]{1,0:T(8,128)S(1)} %get-tuple-element.35.pred, s32[32,256]{1,0:T(8,128)S(1)} %copy-done.1), custom_call_target="tpu_custom_call" | custom-call | flops 1000000 | bytes 1000000 | tf_op jit(solution)/shard_map/pallas_call | solution.py:571
  29.0 0.7 %collective-permute-done.6 = f32[4,16,128]{2,1,0:T(8,128)S(1)} collective-permute-done((f32[4,16,128]{2,1,0:T(8,128)S(1)}, f32[4,16,128]{2,1,0:T(8,128)S(1)}, u32[]{:S(2)}, u32[]{:S(2)}) %collective-permute-start.6) | collective-permute-done | bytes 32800 | tf_op jit(solution)/shard_map/ppermute | solution.py:704
  29.7 3.5 %collective-permute-start.7 = (f32[8,16,128]{2,1,0:T(8,128)S(1)}, f32[8,16,128]{2,1,0:T(8,128)S(1)}, u32[]{:S(2)}, u32[]{:S(2)}) collective-permute-start(f32[8,16,128]{2,1,0:T(8,128)S(1)} %pad_maximum_fusion.after), channel_id=1, source_target_pairs={{0,8},{4,12},{8,0},{12,4},{1,9},{5,13},{9,1},{13,5},{2,10},{6,14},... | collective-permute-start | bytes 196616 | tf_op jit(solution)/shard_map/ppermute | solution.py:704
  33.2 1.6 %shard_map.134.slope_rim = f32[4,72,256]{2,1,0:T(8,128)S(1)} custom-call(f32[8,16,128]{2,1,0:T(8,128)S(1)} %pad_maximum_fusion.after, bf16[8,64,256]{2,1,0:T(8,128)(2,1)S(1)} %get-tuple-element.25.act, bf16[288,256]{1,0:T(8,128)(2,1)S(1)} %collective-permute-done.p1, bf16[288,256]{1,0:T(8,128)(2,1)S(1)} %collective-permute-done.1.p2, ...), custom_call_target="tpu_custom_call" | custom-call | flops 1000000 | bytes 1000000 | tf_op jit(solution)/shard_map/pallas_call | solution.py:571
  34.8 0.6 %collective-permute-done.7 = f32[8,16,128]{2,1,0:T(8,128)S(1)} collective-permute-done((f32[8,16,128]{2,1,0:T(8,128)S(1)}, f32[8,16,128]{2,1,0:T(8,128)S(1)}, u32[]{:S(2)}, u32[]{:S(2)}) %collective-permute-start.7) | collective-permute-done | bytes 65568 | tf_op jit(solution)/shard_map/ppermute | solution.py:704
  35.5 4.7 %shard_map.136 = (f32[8,128]{1,0:T(8,128)}, f32[1,1]{1,0:T(1,128)}, bf16[32,24,256]{2,1,0:T(8,128)(2,1)}) custom-call(f32[16,16,128]{2,1,0:T(8,128)S(1)} %constant_dynamic-update-slice_fusion.msgs, f32[64,128]{1,0:T(8,128)S(1)} %get-tuple-element.26.bm, bf16[288,256]{1,0:T(8,128)(2,1)S(1)} %collective-permute-done.p1, ...), custom_call_target="tpu_custom_call" | custom-call | flops 1000000 | bytes 1000000 | tf_op jit(solution)/shard_map/pallas_call | solution.py:571
  (34 shorter events, 0.3 us)
Async XLA Ops:
  0.6 4.8 %copy-start.4 = (bf16[256,16]{0,1:T(8,128)(2,1)S(1)}, bf16[256,16]{0,1:T(8,128)(2,1)}, u32[]{:S(2)}) copy-start(bf16[256,16]{0,1:T(8,128)(2,1)} %param.19) | copy-start | bytes 24580
  4.1 2.1 %collective-permute-start = (bf16[288,256]{1,0:T(8,128)(2,1)S(1)}, bf16[288,256]{1,0:T(8,128)(2,1)S(1)}, u32[]{:S(2)}, u32[]{:S(2)}) collective-permute-start(bf16[288,256]{1,0:T(8,128)(2,1)S(1)} %get-tuple-element.27), channel_id=1, source_target_pairs={{0,1},{2,3},{1,0},{3,2},{4,5},{6,7},{5,4},{7,6},{8,9},{10,11},{9,8... | collective-permute-start | bytes 442376 | tf_op jit(solution)/shard_map/ppermute | solution.py:594
  4.6 0.8 %copy-start.6 = (s32[1,1,81]{2,1,0:T(1,128)S(1)}, s32[1,1,81]{2,1,0:T(1,128)}, u32[]{:S(2)}) copy-start(s32[1,1,81]{2,1,0:T(1,128)} %param.13) | copy-start | bytes 976
  4.6 1.5 %collective-permute-start.1 = (bf16[288,256]{1,0:T(8,128)(2,1)S(1)}, bf16[288,256]{1,0:T(8,128)(2,1)S(1)}, u32[]{:S(2)}, u32[]{:S(2)}) collective-permute-start(bf16[288,256]{1,0:T(8,128)(2,1)S(1)} %get-tuple-element.28), channel_id=1, source_target_pairs={{1,2},{2,1},{5,6},{6,5},{9,10},{10,9},{13,14},{14,13},{17,18},{18,... | collective-permute-start | bytes 442376 | tf_op jit(solution)/shard_map/ppermute | solution.py:594
  5.4 0.7 %copy-start.5 = (f32[880]{0:T(1024)S(1)}, f32[880]{0:T(1024)}, u32[]{:S(2)}) copy-start(f32[880]{0:T(1024)} %param.14) | copy-start | bytes 10564
  6.2 4.5 %collective-permute-start.2 = (bf16[80,256]{1,0:T(8,128)(2,1)S(1)}, bf16[80,256]{1,0:T(8,128)(2,1)S(1)}, u32[]{:S(2)}, u32[]{:S(2)}) collective-permute-start(bf16[80,256]{1,0:T(8,128)(2,1)S(1)} %get-tuple-element.29), channel_id=1, source_target_pairs={{0,4},{8,12},{4,0},{12,8},{1,5},{9,13},{5,1},{13,9},{2,6},{10,14},... | collective-permute-start | bytes 122888 | tf_op jit(solution)/shard_map/ppermute | solution.py:594
  8.7 2.0 %collective-permute-start.3 = (bf16[80,256]{1,0:T(8,128)(2,1)S(1)}, bf16[80,256]{1,0:T(8,128)(2,1)S(1)}, u32[]{:S(2)}, u32[]{:S(2)}) collective-permute-start(bf16[80,256]{1,0:T(8,128)(2,1)S(1)} %get-tuple-element.30), channel_id=1, source_target_pairs={{4,8},{8,4},{5,9},{9,5},{6,10},{10,6},{7,11},{11,7},{20,24},{24,20... | collective-permute-start | bytes 122888 | tf_op jit(solution)/shard_map/ppermute | solution.py:594
  9.6 1.1 %copy-start = (bf16[256,256]{1,0:T(8,128)(2,1)S(1)}, bf16[256,256]{1,0:T(8,128)(2,1)}, u32[]{:S(2)}) copy-start(bf16[256,256]{1,0:T(8,128)(2,1)} %w_mix.5) | copy-start | bytes 393220
  9.6 1.1 %copy-start.2 = (bf16[9,256]{1,0:T(8,128)(2,1)S(1)}, bf16[9,256]{1,0:T(8,128)(2,1)}, u32[]{:S(2)}) copy-start(bf16[9,256]{1,0:T(8,128)(2,1)} %k_first.5) | copy-start | bytes 13828
  9.6 1.1 %copy-start.3 = (bf16[9,256]{1,0:T(8,128)(2,1)S(1)}, bf16[9,256]{1,0:T(8,128)(2,1)}, u32[]{:S(2)}) copy-start(bf16[9,256]{1,0:T(8,128)(2,1)} %k_deep.5) | copy-start | bytes 13828
  13.3 6.1 %collective-permute-start.4 = (f32[1,16,128]{2,1,0:T(8,128)S(1)}, f32[1,16,128]{2,1,0:T(8,128)S(1)}, u32[]{:S(2)}, u32[]{:S(2)}) collective-permute-start(f32[1,16,128]{2,1,0:T(8,128)S(1)} %bitcast.35), channel_id=1, source_target_pairs={{0,1},{1,0},{2,3},{3,2},{4,5},{5,4},{6,7},{7,6},{8,9},{9,8},{10,11... | collective-permute-start | bytes 24584 | tf_op jit(solution)/shard_map/ppermute | solution.py:704
  19.4 3.9 %collective-permute-start.5 = (f32[2,16,128]{2,1,0:T(8,128)S(1)}, f32[2,16,128]{2,1,0:T(8,128)S(1)}, u32[]{:S(2)}, u32[]{:S(2)}) collective-permute-start(f32[2,16,128]{2,1,0:T(8,128)S(1)} %pad_maximum_fusion.2.after), channel_id=1, source_target_pairs={{0,2},{1,3},{2,0},{3,1},{4,6},{5,7},{6,4},{7,5},{8,10},{9,11},{10,... | collective-permute-start | bytes 49160 | tf_op jit(solution)/shard_map/ppermute | solution.py:704
  23.3 4.6 %copy-start.1 = (s32[32,256]{1,0:T(8,128)S(1)}, s32[32,256]{1,0:T(8,128)}, u32[]{:S(2)}) copy-start(s32[32,256]{1,0:T(8,128)} %land.1) | copy-start | bytes 98308
  23.3 6.5 %collective-permute-start.6 = (f32[4,16,128]{2,1,0:T(8,128)S(1)}, f32[4,16,128]{2,1,0:T(8,128)S(1)}, u32[]{:S(2)}, u32[]{:S(2)}) collective-permute-start(f32[4,16,128]{2,1,0:T(8,128)S(1)} %pad_maximum_fusion.1.after), channel_id=1, source_target_pairs={{0,4},{4,0},{8,12},{12,8},{1,5},{5,1},{9,13},{13,9},{2,6},{6,2},{1... | collective-permute-start | bytes 98312 | tf_op jit(solution)/shard_map/ppermute | solution.py:704
  29.7 5.7 %collective-permute-start.7 = (f32[8,16,128]{2,1,0:T(8,128)S(1)}, f32[8,16,128]{2,1,0:T(8,128)S(1)}, u32[]{:S(2)}, u32[]{:S(2)}) collective-permute-start(f32[8,16,128]{2,1,0:T(8,128)S(1)} %pad_maximum_fusion.after), channel_id=1, source_target_pairs={{0,8},{4,12},{8,0},{12,4},{1,9},{5,13},{9,1},{13,5},{2,10},{6,14},... | collective-permute-start | bytes 196616 | tf_op jit(solution)/shard_map/ppermute | solution.py:704

commit v3 on v2

--- a/solution.py
+++ b/solution.py
@@ -67,36 +67,45 @@
 
 def embed_kernel(
     feat_hbm, w_hbm, land_hbm, blocks_hbm, pre_out, act_out, bm_out, m1_out, m2_out, w_out,
-    feat, w_embed, land, blocks, hot_a, hot_b, sems,
+    feat, w_embed, land, blocks, sems,
 ):
-    pairs = ((blocks_hbm, blocks), (land_hbm, land), (feat_hbm, feat), (w_hbm, w_embed))
+    rows, c_in, cols = feat.shape
+    part = rows // 4
+    pairs = [(blocks_hbm, blocks), (land_hbm, land), (w_hbm, w_embed)]
+    pairs += [
+        (feat_hbm.at[pl.ds(part * n, part)], feat.at[pl.ds(part * n, part)]) for n in range(4)
+    ]
     copies = [pltpu.make_async_copy(src, dst, sems.at[n]) for n, (src, dst) in enumerate(pairs)]
     for copy in copies:
         copy.start()
-    rows, c_in, cols = feat.shape
     c_pad = 32
     crows, ccols = rows // 4, cols // 4
     nblk = blocks.shape[0]
     spread = spread_matrix(cols)
 
-    copies[0].wait()
+    for copy in copies:
+        copy.wait()
     shift_row = cols.bit_length() - 1
-    chunk = hot_a.shape[1] // LANES
+    chunk = next(c for c in (9, 8, 7, 6, 5, 4, 3, 2, 1) if nblk % c == 0)
     total = jnp.zeros((ccols, LANES), F32)
-    sub_a = iota((LANES, LANES), 0)
-    sub_b = iota((ccols, LANES), 0)
+    sub_a = iota((LANES, LANES), 0).astype(F32).astype(BF16)
+    sub_b = iota((ccols, LANES), 0).astype(F32).astype(BF16)
+    one, none = jnp.ones((), BF16), jnp.zeros((), BF16)
     for first in range(0, nblk, chunk):
+        hot_q, hot_j = [], []
         for step in range(chunk):
             k = first + step
             cell = blocks[k]
             named = cell < rows * cols
             q = jnp.where(named, (cell & 3) * rows + (cell >> shift_row), -1)
             j = (cell & (cols - 1)) >> 2
-            span = slice(step * LANES, (step + 1) * LANES)
-            hot_a[:, span] = jnp.where(sub_a == q, 1.0, 0.0).astype(BF16)
-            hot_b[:, span] = jnp.where(sub_b == j, float(k + 1), 0.0).astype(BF16)
-        total = total + dot_nt(hot_b[...], hot_a[...])
-    copies[1].wait()
+            hot_q.append(jnp.where(sub_a == q.astype(F32).astype(BF16), one, none))
+            hot_j.append(
+                jnp.where(sub_b == j.astype(F32).astype(BF16), jnp.array(k + 1, BF16), none)
+            )
+        total = total + dot_nt(
+            jnp.concatenate(hot_j, axis=1), jnp.concatenate(hot_q, axis=1)
+        )
     land_moved = dot_nt(spread, land[...].astype(F32).astype(BF16))
     land_q = jnp.concatenate(
         [land_moved[b * ccols : (b + 1) * ccols, :] for b in range(4)], axis=1
@@ -104,8 +113,6 @@
     bm = total * land_q
     bm_out[...] = bm
 
-    copies[2].wait()
-    copies[3].wait()
     field = feat[...].astype(F32)
     field = jnp.concatenate([field, jnp.zeros((rows, c_pad - c_in, cols), F32)], axis=1)
     field = field.reshape(rows * c_pad, cols).astype(BF16)
@@ -314,56 +321,43 @@
 
 def rim_kernel(
     after, act, p1, p2, t1, t2, w_mix, k_first, k_deep, field, act_mix, slope_rim,
-    ext, mixed,
+    ext, mixed, side,
 ):
     del after
     crows, ccols, chan = act.shape
     width = ccols + 2 * HALO
     row = halo_rows(act, p1, p2, t1, t2)
-    first, second = k_first[...].astype(F32), k_deep[...].astype(F32)
-    weights = w_mix[...]
-    shape = (2, width, chan)
-    col_ok = inside_columns(shape, ccols)
-    band = lax.axis_index("band")
-    for side in range(2):
-        outer = (0, 1) if side == 0 else (crows + 6, crows + 7)
-        inner = (0, 1) if side == 0 else (crows + 2, crows + 3)
-        spots = (0, 1) if side == 0 else (2, 3)
-        for r, at in zip(outer, spots):
-            own, edge = row(r)
-            ext[at, 0:ccols, :] = own
-            ext[at, ccols:, :] = edge
-        for r, at in zip(inner, (2, 3) if side == 0 else (0, 1)):
-            ext[at] = field[r]
-
-        def keep_mixed(r, span, value):
-            mixed[r, :, span] = value
-
-        conv_pass(ext, 4, first, keep_mixed, chan)
-        edge_band = 0 if side == 0 else lax.axis_size("band") - 1
-        ok = col_ok & (band != edge_band)
-        _, post = mix_pair(mixed[...], ext[1:3], weights, ok)
-        have = (0, 1) if side == 0 else (crows, crows + 1)
-        for n in range(2):
-            ext[spots[n]] = post[n]
-            ext[(2, 3)[n] if side == 0 else n] = act_mix[have[n]]
-
-        def keep_deep(r, span, value):
-            mixed[r, :, span] = value
-
-        conv_pass(ext, 4, second, keep_deep, chan)
-        slope_rim[2 * side : 2 * side + 2] = gelu_slope(mixed[...])
-
-
-def slope_kernel(after, src, out):
+    outer = (0, 1) if side == 0 else (crows + 6, crows + 7)
+    inner = (0, 1) if side == 0 else (crows + 2, crows + 3)
+    near = (2, 3) if side == 0 else (0, 1)
+    far = (0, 1) if side == 0 else (2, 3)
+    for r, at in zip(outer, far):
+        own, edge = row(r)
+        ext[at, 0:ccols, :] = own
+        ext[at, ccols:, :] = edge
+    for r, at in zip(inner, near):
+        ext[at] = field[r]
+
+    def keep(r, span, value):
+        mixed[r, :, span] = value
+
+    conv_pass(ext, 4, k_first[...].astype(F32), keep, chan)
+    edge_band = 0 if side == 0 else lax.axis_size("band") - 1
+    ok = inside_columns((2, width, chan), ccols) & (lax.axis_index("band") != edge_band)
+    _, post = mix_pair(mixed[...], ext[1:3], w_mix[...], ok)
+    have = (0, 1) if side == 0 else (crows, crows + 1)
+    for n in range(2):
+        ext[far[n]] = post[n]
+        ext[near[n]] = act_mix[have[n]]
+    conv_pass(ext, 4, k_deep[...].astype(F32), keep, chan)
+    slope_rim[...] = gelu_slope(mixed[...])
+
+
+def slope_kernel(after, mix, deep, pred, land, slope_mix, slope_deep, cells):
     del after
-    out[...] = gelu_slope(src[...])
-
-
-def slope_pred_kernel(after, src, pred, land, out, cells):
-    del after
+    slope_mix[...] = gelu_slope(mix[...])
+    slope_deep[...] = gelu_slope(deep[...])
     rows, cols = land.shape
-    out[...] = gelu_slope(src[...])
     turned = pred[...].T
     wide = jnp.concatenate([turned[b * rows : (b + 1) * rows] for b in range(4)], axis=1)
     high = wide.astype(BF16)
@@ -373,12 +367,13 @@
 
 
 def backward_kernel(
-    msgs, bm, p1, p2, t1, t2, slope_deep, slope_rim, slope_mix, slope_first,
+    gathered, bm, p1, p2, t1, t2, slope_deep, rim_above, rim_below, slope_mix,
+    slope_first,
     w_mix, k_first, k_deep, wall, w_wide,
     mean_out, loss_out, grad_out,
     targets, table, grads, field, mixing, proj, share_rows, share, loss_scale, c_in,
 ):
-    ndev = msgs.shape[0]
+    ndev = gathered.shape[0]
     crows = slope_first.shape[0]
     ccols = slope_first.shape[1]
     chan = slope_first.shape[2]
@@ -386,30 +381,36 @@
     band, tile = lax.axis_index("band"), lax.axis_index("tile")
     bands, tiles = lax.axis_size("band"), lax.axis_size("tile")
     me = tile * bands + band
+    masks = hop_masks(bands, tiles)
+
+    def slot_at(owner):
+        apart = owner ^ me
+        return sum(jnp.where(apart & mask > 0, 2**n, 0) for n, mask in enumerate(masks))
 
     def slot_of(v, t):
         other_band, other_tile = band + v, tile + t
         ok = (other_band >= 0) & (other_band < bands) & (other_tile >= 0) & (other_tile < tiles)
-        return jnp.where(ok, (other_tile * bands + other_band) ^ me, 0)
+        return jnp.where(ok, slot_at(other_tile * bands + other_band), 0)
 
     height = ndev * share_rows
     chunk = min(16, ndev)
-    first_target = msgs.shape[1] - share_rows
-    sub = iota((height, LANES), 0).astype(F32)
-    sub_lo = iota((LANES, LANES), 0).astype(F32)
+    first_target = gathered.shape[1] - share_rows
+    sub = iota((height, LANES), 0).astype(F32).astype(BF16)
+    sub_lo = iota((LANES, LANES), 0).astype(F32).astype(BF16)
+    one, none = jnp.ones((), BF16), jnp.zeros((), BF16)
 
     def gather_chunk(c, acc):
         hot_hi, hot_lo = [], []
         for o in range(chunk):
             owner = c * chunk + o
-            m = msgs[owner ^ me]
-            hot_hi.append(jnp.where(sub == m[2:3], 1.0, 0.0).astype(BF16))
-            low_hit = sub_lo == m[3:4]
+            m = gathered[slot_at(owner)]
+            hot_hi.append(jnp.where(sub == m[2:3].astype(BF16), one, none))
+            low_hit = sub_lo == m[3:4].astype(BF16)
             high = rounded(m[0:1])
             parts = [high, m[0:1] - high, m[1:2]]
             hot_lo.append(
                 jnp.concatenate(
-                    [jnp.where(low_hit, part, 0.0).astype(BF16) for part in parts], axis=0
+                    [jnp.where(low_hit, part.astype(BF16), none) for part in parts], axis=0
                 )
             )
             targets[pl.ds(owner * share_rows, share_rows)] = m[first_target:]
@@ -441,7 +442,7 @@
     sub8 = iota((8, LANES), 0).astype(F32)
 
     def block_grads(slot):
-        m = msgs[slot]
+        m = gathered[slot]
         low = jnp.broadcast_to(jnp.maximum(m[3:4], 0.0), (8, LANES)).astype(jnp.int32)
         high = m[2:3]
         total = jnp.zeros((8, LANES), F32)
@@ -493,7 +494,7 @@
         weights = jnp.where(head_row == i, head, 0.0).astype(BF16)
         deep = rounded(dot(cells[v], weights))
         mixing[r] = deep
-        slope = slope_rim[r] if v == 0 else slope_deep[i] if v == 1 else slope_rim[r - crows]
+        slope = rim_above[r] if v == 0 else slope_deep[i] if v == 1 else rim_below[r - crows - 2]
         field[r] = deep * slope
 
     def keep_mix(r, span, value):
@@ -546,22 +547,25 @@
     c_pad = 32
     out = dot_nt(w_wide[...], proj[...].reshape(crows * ccols, chan)).astype(BF16)
     wide = 4 * c_pad
-    lhs = jnp.concatenate(
-        [
-            jnp.concatenate(
-                [
-                    out[b * wide : (b + 1) * wide, i * ccols : (i + 1) * ccols]
-                    for b in range(4)
-                ],
-                axis=1,
-            )
-            for i in range(crows)
-        ],
-        axis=0,
-    )
-    fine = dot(lhs, spread_matrix(4 * ccols))
-    for r in range(4 * crows):
-        grad_out[r] = fine[r * c_pad : r * c_pad + c_in].astype(BF16)
+    spread = spread_matrix(4 * ccols)
+    group = crows // 4
+    for g in range(4):
+        lhs = jnp.concatenate(
+            [
+                jnp.concatenate(
+                    [
+                        out[b * wide : (b + 1) * wide, i * ccols : (i + 1) * ccols]
+                        for b in range(4)
+                    ],
+                    axis=1,
+                )
+                for i in range(g * group, (g + 1) * group)
+            ],
+            axis=0,
+        )
+        fine = dot(lhs, spread)
+        for r in range(4 * group):
+            grad_out[4 * group * g + r] = fine[r * c_pad : r * c_pad + c_in].astype(BF16)
 
 
 def call(kernel, outs, scratch=(), hbm=0):
@@ -586,6 +590,10 @@
     return run
 
 
+def hop_masks(bands, tiles):
+    return [2**n for n in range((bands * tiles).bit_length() - 2, -1, -1)]
+
+
 def exchange(m1, m2, axis):
     size = lax.axis_size(axis)
     even = [(i, i + 1) for i in range(0, size - 1, 2)]
@@ -626,7 +634,6 @@
 
     feat = features.transpose(0, 2, 1)
     msg1 = HALO * ccols + ccols // 2
-    chunk = next(c for c in (9, 8, 7, 6, 5, 4, 3, 2, 1) if nblk % c == 0)
     pre_first, act, bm, m1, m2, w_wide = call(
         embed_kernel,
         [
@@ -642,9 +649,7 @@
             ((16 * c_in, chan), BF16),
             ((rows, cols), jnp.int32),
             ((nblk, 1, LANES), jnp.int32),
-            ((LANES, chunk * LANES), BF16),
-            ((ccols, chunk * LANES), BF16),
-            ((4,), None),
+            ((7,), None),
         ],
         hbm=4,
     )(
@@ -674,40 +679,38 @@
         [((crows + 2, width, chan), F32)],
     )(act, bm, p1, p2, t1, t2, w_mix, k_first, k_deep, wall, msg_in)
 
-    def slopes_mix(after):
-        return call(slope_kernel, [((crows + 2, width, chan), F32)], hbm=1)(after, pre_mix)
-
-    def slopes_deep(after):
+    def slopes(after):
         return call(
-            slope_pred_kernel,
-            [((crows, width, chan), F32), ((rows, cols), F32)],
+            slope_kernel,
+            [
+                ((crows + 2, width, chan), F32),
+                ((crows, width, chan), F32),
+                ((rows, cols), F32),
+            ],
             hbm=1,
-        )(after, pre_deep, pred, land_mask)
-
-    def slopes_rim(after):
+        )(after, pre_mix, pre_deep, pred, land_mask)
+
+    def rim(side, after):
         return call(
-            rim_kernel,
-            [((4, width, chan), F32)],
+            functools.partial(rim_kernel, side=side),
+            [((2, width, chan), F32)],
             [((4, width, chan), F32), ((2, width, chan), F32)],
             hbm=1,
         )(after, act, p1, p2, t1, t2, w_mix, k_first, k_deep, field, act_mix)
 
-    beside = {1: slopes_mix, 2: slopes_deep, 3: slopes_rim}
-    made = {}
+    def send(x, mask):
+        pairs = [(n, n ^ mask) for n in range(ndev)]
+        return lax.ppermute(x, ("tile", "band"), pairs)
+
+    masks = hop_masks(bands, tiles)
+    beside = [slopes, functools.partial(rim, 0), functools.partial(rim, 1)]
+    made = []
     msgs = msg[None]
-    at = 0
-    for axis, size in (("band", bands), ("tile", tiles)):
-        step = 1
-        while step < size:
-            if at in beside:
-                made[at] = beside[at](msgs)
-            other = lax.ppermute(msgs, axis, [(i, i ^ step) for i in range(size)])
-            msgs = jnp.concatenate([msgs, other], axis=0)
-            step *= 2
-            at += 1
-    (slope_mix,) = made[1]
-    slope_deep, cell_pred = made[2]
-    (slope_rim,) = made[3]
+    for n, mask in enumerate(masks):
+        if n < len(beside):
+            made.append(beside[n](msgs))
+        msgs = jnp.concatenate([msgs, send(msgs, mask)], axis=0)
+    (slope_mix, slope_deep, cell_pred), (rim_above,), (rim_below,) = made
 
     height = ndev * share_rows
     mean, loss, grad = call(
@@ -728,7 +731,7 @@
             ((crows, ccols, chan), BF16),
         ],
     )(
-        msgs, bm, p1, p2, t1, t2, slope_deep, slope_rim, slope_mix,
+        msgs, bm, p1, p2, t1, t2, slope_deep, rim_above, rim_below, slope_mix,
         slope_first.reshape(crows, ccols, chan), w_mix, k_first, k_deep, wall, w_wide,
     )
     return (

time: 40.4 us -> 39.2 us (0.970)
  starting transfers between devices: 19.9 us -> 19 us
    ppermute x4, starting transfers between devices: 15.4 us -> 14.5 us  [send(): return lax.ppermute(x, ('tile', 'band'), pairs)]
    pallas_call x8, Pallas kernels: 14.4 us -> 14 us  [run(): pl.pallas_call(kernel, out_shape=[jax.ShapeDtypeStruct(s, d) for s, d in...]
  transfers between devices with their start and end apart: 8 -> 8, of which waited for: 5 -> 4; matrix products, arithmetic and copies ran while one was open for 1% -> 1% of each run, Pallas kernels for 9% -> 10%
where the time goes in v3:
time: 39.2 us; the launch traced here: 39 us
  starting transfers between devices  19 us (48%)
  Pallas kernels  14 us (36%)
  waiting for transfers between devices  4.25 us (11%)
  between operations  0.84 us (2%)
  local copies, waits for them, and re-layouts  0.81 us (2%)
    ppermute x4, starting transfers between devices, send(): return lax.ppermute(x, ('tile', 'band'), pairs)  14.5 us
    pallas_call x8, Pallas kernels, run(): pl.pallas_call(kernel, out_shape=[jax.ShapeDtypeStruct(s, d) for s, d in...  14 us
    ppermute x4, waiting for transfers between devices, send(): return lax.ppermute(x, ('tile', 'band'), pairs)  3.81 us
    ppermute x2, starting transfers between devices, exchange(): lax.ppermute(m1, axis, both(even))  3.18 us
    ppermute x2, starting transfers between devices, exchange(): lax.ppermute(m2, axis, both(odd))  1.31 us
  transfers between devices with their start and end apart: 8, of which 4 were waited for; matrix products, arithmetic and copies ran while one was open for 1% of the time, Pallas kernels for 10%

profile of v3, /device:TPU:0, one launch (start us, length us, event | category | flops | bytes accessed | tf_op | source)
XLA Modules:
  0.0 39.0 jit_solution(16682367729031385325)
XLA Ops:
  0.6 2.8 %shard_map.129 = (f32[512,256]{1,0:T(8,128)S(1)}, bf16[8,64,256]{2,1,0:T(8,128)(2,1)S(1)}, f32[64,128]{1,0:T(8,128)S(1)}, bf16[288,256]{1,0:T(8,128)(2,1)S(1)}, ...) custom-call(bf16[32,24,256]{2,1,0:T(8,128)(2,1)} %bitcast.40, bf16[384,256]{1,0:T(8,128)(2,1)} %w_hbm.1, ...), custom_call_target="tpu_custom_call" | custom-call | flops 1000000 | bytes 1000000 | tf_op jit(solution)/shard_map/pallas_call | solution.py:575
  3.5 0.0 copy-start.6
  3.5 0.5 %collective-permute-start = (bf16[288,256]{1,0:T(8,128)(2,1)S(1)}, bf16[288,256]{1,0:T(8,128)(2,1)S(1)}, u32[]{:S(2)}, u32[]{:S(2)}) collective-permute-start(bf16[288,256]{1,0:T(8,128)(2,1)S(1)} %get-tuple-element.28), channel_id=1, source_target_pairs={{0,1},{2,3},{1,0},{3,2},{4,5},{6,7},{5,4},{7,6},{8,9},{10,11},{9,8... | collective-permute-start | bytes 442376 | tf_op jit(solution)/shard_map/ppermute | solution.py:602
  4.0 0.7 %collective-permute-start.1 = (bf16[288,256]{1,0:T(8,128)(2,1)S(1)}, bf16[288,256]{1,0:T(8,128)(2,1)S(1)}, u32[]{:S(2)}, u32[]{:S(2)}) collective-permute-start(bf16[288,256]{1,0:T(8,128)(2,1)S(1)} %get-tuple-element.29), channel_id=1, source_target_pairs={{1,2},{2,1},{5,6},{6,5},{9,10},{10,9},{13,14},{14,13},{17,18},{18,... | collective-permute-start | bytes 442376 | tf_op jit(solution)/shard_map/ppermute | solution.py:602
  4.7 0.0 copy-start.5
  4.7 0.6 %copy-done.5 = f32[880]{0:T(1024)S(1)} copy-done((f32[880]{0:T(1024)S(1)}, f32[880]{0:T(1024)}, u32[]{:S(2)}) %copy-start.5) | copy-done | bytes 3544
  5.5 2.7 %collective-permute-start.2 = (bf16[80,256]{1,0:T(8,128)(2,1)S(1)}, bf16[80,256]{1,0:T(8,128)(2,1)S(1)}, u32[]{:S(2)}, u32[]{:S(2)}) collective-permute-start(bf16[80,256]{1,0:T(8,128)(2,1)S(1)} %get-tuple-element.30), channel_id=1, source_target_pairs={{0,4},{8,12},{4,0},{12,8},{1,5},{9,13},{5,1},{13,9},{2,6},{10,14},... | collective-permute-start | bytes 122888 | tf_op jit(solution)/shard_map/ppermute | solution.py:602
  8.1 0.7 %collective-permute-start.3 = (bf16[80,256]{1,0:T(8,128)(2,1)S(1)}, bf16[80,256]{1,0:T(8,128)(2,1)S(1)}, u32[]{:S(2)}, u32[]{:S(2)}) collective-permute-start(bf16[80,256]{1,0:T(8,128)(2,1)S(1)} %get-tuple-element.31), channel_id=1, source_target_pairs={{4,8},{8,4},{5,9},{9,5},{6,10},{10,6},{7,11},{11,7},{20,24},{24,20... | collective-permute-start | bytes 122888 | tf_op jit(solution)/shard_map/ppermute | solution.py:602
  8.8 0.1 pad_convert_fusion
  9.0 0.6 %shard_map.131 = (f32[512,256]{1,0:T(8,128)S(1)}, f32[16,128]{1,0:T(8,128)S(1)}) custom-call(f32[512,256]{1,0:T(8,128)S(1)} %get-tuple-element.32.pre_first, f32[64,128]{1,0:T(8,128)S(1)} %get-tuple-element.27.bm, f32[16,128]{1,0:T(8,128)S(1)} %concatenate.22.msg_in), custom_call_target="tpu_custom_call" | custom-call | flops 1000000 | bytes 1000000 | tf_op jit(solution)/shard_map/pallas_call | solution.py:575
  9.7 0.4 %collective-permute-done.2.t1 = bf16[80,256]{1,0:T(8,128)(2,1)S(1)} collective-permute-done((bf16[80,256]{1,0:T(8,128)(2,1)S(1)}, bf16[80,256]{1,0:T(8,128)(2,1)S(1)}, u32[]{:S(2)}, u32[]{:S(2)}) %collective-permute-start.2) | collective-permute-done | bytes 40992 | tf_op jit(solution)/shard_map/ppermute | solution.py:602
  10.1 0.0 copy-start.3
  10.1 2.6 %shard_map.132 = (f32[12,72,256]{2,1,0:T(8,128)S(1)}, f32[10,72,256]{2,1,0:T(8,128)S(1)}, f32[10,72,256]{2,1,0:T(8,128)S(1)}, f32[8,72,256]{2,1,0:T(8,128)S(1)},...) custom-call(bf16[8,64,256]{2,1,0:T(8,128)(2,1)S(1)} %get-tuple-element.26.act, f32[64,128]{1,0:T(8,128)S(1)} %get-tuple-element.27.bm, ...), custom_call_target="tpu_custom_call" | custom-call | flops 1000000 | bytes 1000000 | tf_op jit(solution)/shard_map/pallas_call | solution.py:575
  12.7 6.5 %collective-permute-start.4 = (f32[1,16,128]{2,1,0:T(8,128)S(1)}, f32[1,16,128]{2,1,0:T(8,128)S(1)}, u32[]{:S(2)}, u32[]{:S(2)}) collective-permute-start(f32[1,16,128]{2,1,0:T(8,128)S(1)} %bitcast.35), channel_id=1, source_target_pairs={{0,8},{1,9},{2,10},{3,11},{4,12},{5,13},{6,14},{7,15},{8,0},{9,1},... | collective-permute-start | bytes 24584 | tf_op jit(solution)/shard_map/ppermute | solution.py:703
  19.3 1.6 %shard_map.133 = (f32[10,72,256]{2,1,0:T(8,128)S(1)}, f32[8,72,256]{2,1,0:T(8,128)S(1)}, f32[32,256]{1,0:T(8,128)}) custom-call(f32[1,16,128]{2,1,0:T(8,128)S(1)} %bitcast.36, f32[10,72,256]{2,1,0:T(8,128)S(1)} %get-tuple-element.35.mix, f32[8,72,256]{2,1,0:T(8,128)S(1)} %get-tuple-element.36.deep, f32[64,128]{1,0:T(8,128)S(1)} %get-tuple-element.37.pred, ...), custom_call_target="tpu_custom_call" | custom-call | flops 1000000 | bytes 1000000 | tf_op jit(solution)/shard_map/pallas_call | solution.py:575
  20.9 0.0 collective-permute-done.4
  20.9 1.5 %collective-permute-start.5 = (f32[2,16,128]{2,1,0:T(8,128)S(1)}, f32[2,16,128]{2,1,0:T(8,128)S(1)}, u32[]{:S(2)}, u32[]{:S(2)}) collective-permute-start(f32[2,16,128]{2,1,0:T(8,128)S(1)} %pad_maximum_fusion.2.after), channel_id=1, source_target_pairs={{0,4},{1,5},{2,6},{3,7},{4,0},{5,1},{6,2},{7,3},{8,12},{9,13},{10,... | collective-permute-start | bytes 49160 | tf_op jit(solution)/shard_map/ppermute | solution.py:703
  22.4 0.8 %shard_map.134.rim_above = f32[2,72,256]{2,1,0:T(8,128)S(1)} custom-call(f32[2,16,128]{2,1,0:T(8,128)S(1)} %pad_maximum_fusion.2.after, bf16[8,64,256]{2,1,0:T(8,128)(2,1)S(1)} %get-tuple-element.26.act, bf16[288,256]{1,0:T(8,128)(2,1)S(1)} %collective-permute-done.p1, bf16[288,256]{1,0:T(8,128)(2,1)S(1)} %collective-permute-done.1.p2, ...), custom_call_target="tpu_custom_call" | custom-call | flops 1000000 | bytes 1000000 | tf_op jit(solution)/shard_map/pallas_call | solution.py:575
  23.2 1.5 %collective-permute-done.5 = f32[2,16,128]{2,1,0:T(8,128)S(1)} collective-permute-done((f32[2,16,128]{2,1,0:T(8,128)S(1)}, f32[2,16,128]{2,1,0:T(8,128)S(1)}, u32[]{:S(2)}, u32[]{:S(2)}) %collective-permute-start.5) | collective-permute-done | bytes 16416 | tf_op jit(solution)/shard_map/ppermute | solution.py:703
  24.6 6.5 %collective-permute-start.6 = (f32[4,16,128]{2,1,0:T(8,128)S(1)}, f32[4,16,128]{2,1,0:T(8,128)S(1)}, u32[]{:S(2)}, u32[]{:S(2)}) collective-permute-start(f32[4,16,128]{2,1,0:T(8,128)S(1)} %pad_maximum_fusion.1.after), channel_id=1, source_target_pairs={{0,2},{1,3},{2,0},{3,1},{4,6},{5,7},{6,4},{7,5},{8,10},{9,11},{10,... | collective-permute-start | bytes 98312 | tf_op jit(solution)/shard_map/ppermute | solution.py:703
  31.2 0.8 %shard_map.135.rim_below = f32[2,72,256]{2,1,0:T(8,128)S(1)} custom-call(f32[4,16,128]{2,1,0:T(8,128)S(1)} %pad_maximum_fusion.1.after, bf16[8,64,256]{2,1,0:T(8,128)(2,1)S(1)} %get-tuple-element.26.act, bf16[288,256]{1,0:T(8,128)(2,1)S(1)} %collective-permute-done.p1, bf16[288,256]{1,0:T(8,128)(2,1)S(1)} %collective-permute-done.1.p2, ...), custom_call_target="tpu_custom_call" | custom-call | flops 1000000 | bytes 1000000 | tf_op jit(solution)/shard_map/pallas_call | solution.py:575
  32.0 1.1 %collective-permute-done.6 = f32[4,16,128]{2,1,0:T(8,128)S(1)} collective-permute-done((f32[4,16,128]{2,1,0:T(8,128)S(1)}, f32[4,16,128]{2,1,0:T(8,128)S(1)}, u32[]{:S(2)}, u32[]{:S(2)}) %collective-permute-start.6) | collective-permute-done | bytes 32800 | tf_op jit(solution)/shard_map/ppermute | solution.py:703
  33.1 1.2 %collective-permute-done.7 = f32[8,16,128]{2,1,0:T(8,128)S(1)} collective-permute-done((f32[8,16,128]{2,1,0:T(8,128)S(1)}, f32[8,16,128]{2,1,0:T(8,128)S(1)}, u32[]{:S(2)}, u32[]{:S(2)}) %collective-permute-start.7) | collective-permute-done | bytes 65568 | tf_op jit(solution)/shard_map/ppermute | solution.py:703
  34.3 4.7 %shard_map.136 = (f32[8,128]{1,0:T(8,128)}, f32[1,1]{1,0:T(1,128)}, bf16[32,24,256]{2,1,0:T(8,128)(2,1)}) custom-call(f32[16,16,128]{2,1,0:T(8,128)S(1)} %constant_dynamic-update-slice_fusion.gathered, f32[64,128]{1,0:T(8,128)S(1)} %get-tuple-element.27.bm, bf16[288,256]{1,0:T(8,128)(2,1)S(1)} %collective-permute-done.p1, ...), custom_call_target="tpu_custom_call" | custom-call | flops 1000000 | bytes 1000000 | tf_op jit(solution)/shard_map/pallas_call | solution.py:575
  (34 shorter events, 0.3 us)
Async XLA Ops:
  0.6 4.1 %copy-start.4 = (bf16[256,16]{0,1:T(8,128)(2,1)S(1)}, bf16[256,16]{0,1:T(8,128)(2,1)}, u32[]{:S(2)}) copy-start(bf16[256,16]{0,1:T(8,128)(2,1)} %param.19) | copy-start | bytes 24580
  3.5 1.2 %copy-start.6 = (s32[1,1,81]{2,1,0:T(1,128)S(1)}, s32[1,1,81]{2,1,0:T(1,128)}, u32[]{:S(2)}) copy-start(s32[1,1,81]{2,1,0:T(1,128)} %param.13) | copy-start | bytes 976
  3.5 1.9 %collective-permute-start = (bf16[288,256]{1,0:T(8,128)(2,1)S(1)}, bf16[288,256]{1,0:T(8,128)(2,1)S(1)}, u32[]{:S(2)}, u32[]{:S(2)}) collective-permute-start(bf16[288,256]{1,0:T(8,128)(2,1)S(1)} %get-tuple-element.28), channel_id=1, source_target_pairs={{0,1},{2,3},{1,0},{3,2},{4,5},{6,7},{5,4},{7,6},{8,9},{10,11},{9,8... | collective-permute-start | bytes 442376 | tf_op jit(solution)/shard_map/ppermute | solution.py:602
  4.0 1.4 %collective-permute-start.1 = (bf16[288,256]{1,0:T(8,128)(2,1)S(1)}, bf16[288,256]{1,0:T(8,128)(2,1)S(1)}, u32[]{:S(2)}, u32[]{:S(2)}) collective-permute-start(bf16[288,256]{1,0:T(8,128)(2,1)S(1)} %get-tuple-element.29), channel_id=1, source_target_pairs={{1,2},{2,1},{5,6},{6,5},{9,10},{10,9},{13,14},{14,13},{17,18},{18,... | collective-permute-start | bytes 442376 | tf_op jit(solution)/shard_map/ppermute | solution.py:602
  4.7 0.7 %copy-start.5 = (f32[880]{0:T(1024)S(1)}, f32[880]{0:T(1024)}, u32[]{:S(2)}) copy-start(f32[880]{0:T(1024)} %param.14) | copy-start | bytes 10564
  5.5 4.6 %collective-permute-start.2 = (bf16[80,256]{1,0:T(8,128)(2,1)S(1)}, bf16[80,256]{1,0:T(8,128)(2,1)S(1)}, u32[]{:S(2)}, u32[]{:S(2)}) collective-permute-start(bf16[80,256]{1,0:T(8,128)(2,1)S(1)} %get-tuple-element.30), channel_id=1, source_target_pairs={{0,4},{8,12},{4,0},{12,8},{1,5},{9,13},{5,1},{13,9},{2,6},{10,14},... | collective-permute-start | bytes 122888 | tf_op jit(solution)/shard_map/ppermute | solution.py:602
  8.1 2.0 %collective-permute-start.3 = (bf16[80,256]{1,0:T(8,128)(2,1)S(1)}, bf16[80,256]{1,0:T(8,128)(2,1)S(1)}, u32[]{:S(2)}, u32[]{:S(2)}) collective-permute-start(bf16[80,256]{1,0:T(8,128)(2,1)S(1)} %get-tuple-element.31), channel_id=1, source_target_pairs={{4,8},{8,4},{5,9},{9,5},{6,10},{10,6},{7,11},{11,7},{20,24},{24,20... | collective-permute-start | bytes 122888 | tf_op jit(solution)/shard_map/ppermute | solution.py:602
  9.0 1.1 %copy-start = (bf16[256,256]{1,0:T(8,128)(2,1)S(1)}, bf16[256,256]{1,0:T(8,128)(2,1)}, u32[]{:S(2)}) copy-start(bf16[256,256]{1,0:T(8,128)(2,1)} %w_mix.7) | copy-start | bytes 393220
  9.0 1.1 %copy-start.1 = (bf16[9,256]{1,0:T(8,128)(2,1)S(1)}, bf16[9,256]{1,0:T(8,128)(2,1)}, u32[]{:S(2)}) copy-start(bf16[9,256]{1,0:T(8,128)(2,1)} %k_first.7) | copy-start | bytes 13828
  9.0 1.1 %copy-start.2 = (bf16[9,256]{1,0:T(8,128)(2,1)S(1)}, bf16[9,256]{1,0:T(8,128)(2,1)}, u32[]{:S(2)}) copy-start(bf16[9,256]{1,0:T(8,128)(2,1)} %k_deep.7) | copy-start | bytes 13828
  10.1 9.1 %copy-start.3 = (s32[32,256]{1,0:T(8,128)S(1)}, s32[32,256]{1,0:T(8,128)}, u32[]{:S(2)}) copy-start(s32[32,256]{1,0:T(8,128)} %land.1) | copy-start | bytes 98308
  12.7 8.2 %collective-permute-start.4 = (f32[1,16,128]{2,1,0:T(8,128)S(1)}, f32[1,16,128]{2,1,0:T(8,128)S(1)}, u32[]{:S(2)}, u32[]{:S(2)}) collective-permute-start(f32[1,16,128]{2,1,0:T(8,128)S(1)} %bitcast.35), channel_id=1, source_target_pairs={{0,8},{1,9},{2,10},{3,11},{4,12},{5,13},{6,14},{7,15},{8,0},{9,1},... | collective-permute-start | bytes 24584 | tf_op jit(solution)/shard_map/ppermute | solution.py:703
  20.9 3.7 %collective-permute-start.5 = (f32[2,16,128]{2,1,0:T(8,128)S(1)}, f32[2,16,128]{2,1,0:T(8,128)S(1)}, u32[]{:S(2)}, u32[]{:S(2)}) collective-permute-start(f32[2,16,128]{2,1,0:T(8,128)S(1)} %pad_maximum_fusion.2.after), channel_id=1, source_target_pairs={{0,4},{1,5},{2,6},{3,7},{4,0},{5,1},{6,2},{7,3},{8,12},{9,13},{10,... | collective-permute-start | bytes 49160 | tf_op jit(solution)/shard_map/ppermute | solution.py:703
  24.6 8.4 %collective-permute-start.6 = (f32[4,16,128]{2,1,0:T(8,128)S(1)}, f32[4,16,128]{2,1,0:T(8,128)S(1)}, u32[]{:S(2)}, u32[]{:S(2)}) collective-permute-start(f32[4,16,128]{2,1,0:T(8,128)S(1)} %pad_maximum_fusion.1.after), channel_id=1, source_target_pairs={{0,2},{1,3},{2,0},{3,1},{4,6},{5,7},{6,4},{7,5},{8,10},{9,11},{10,... | collective-permute-start | bytes 98312 | tf_op jit(solution)/shard_map/ppermute | solution.py:703
  33.1 1.3 %collective-permute-start.7 = (f32[8,16,128]{2,1,0:T(8,128)S(1)}, f32[8,16,128]{2,1,0:T(8,128)S(1)}, u32[]{:S(2)}, u32[]{:S(2)}) collective-permute-start(f32[8,16,128]{2,1,0:T(8,128)S(1)} %pad_maximum_fusion), channel_id=1, source_target_pairs={{0,1},{1,0},{2,3},{3,2},{4,5},{5,4},{6,7},{7,6},{8,9},{9,8},{10,11... | collective-permute-start | bytes 196616 | tf_op jit(solution)/shard_map/ppermute | solution.py:703

commit v4 on v3

--- a/solution.py
+++ b/solution.py
@@ -66,7 +66,7 @@
 
 
 def embed_kernel(
-    feat_hbm, w_hbm, land_hbm, blocks_hbm, pre_out, act_out, bm_out, m1_out, m2_out, w_out,
+    feat_hbm, w_hbm, land_hbm, blocks_hbm, pre_out, act_out, bm_out, m2_out, w_out,
     feat, w_embed, land, blocks, sems,
 ):
     rows, c_in, cols = feat.shape
@@ -137,15 +137,22 @@
     chan = pre.shape[1]
     pre_out[...] = pre
     act_out[...] = gelu_exact(pre).astype(BF16).reshape(crows, ccols, chan)
+    pack(act_out, bm, parity("band"), m2_out)
+
+
+def pack(act, bm, low, out):
+    crows, ccols, chan = act.shape
     half = ccols // 2
-    bm_wide = jnp.concatenate([bm[:half], bm[half:]], axis=1).astype(BF16)
-    odd = parity("band")
-    for out, start in ((m1_out, (1 - odd) * (crows - HALO)), (m2_out, odd * (crows - HALO))):
-        out[0 : HALO * ccols] = act_out[pl.ds(start, HALO)].reshape(HALO * ccols, chan)
-        out[HALO * ccols :] = bm_wide
-
-
-def edges_kernel(act, bm, p1, p2, m1_out, m2_out):
+    start = low * (crows - HALO)
+    out[0 : HALO * ccols] = act[pl.ds(start, HALO)].reshape(HALO * ccols, chan)
+    out[HALO * ccols :] = jnp.concatenate([bm[:half], bm[half:]], axis=1).astype(BF16)
+
+
+def pack_kernel(act, bm, m1_out):
+    pack(act, bm[...], 1 - parity("band"), m1_out)
+
+
+def edges_kernel(act, bm, p1, p2, out, second):
     crows, ccols, chan = act.shape
     odd_b = parity("band") == 1
     odd_t = parity("tile") == 1
@@ -179,8 +186,8 @@
 
     left = message(left, bm_left)
     right = message(right, bm_right)
-    m1_out[...] = jnp.where(odd_t, left, right).astype(BF16)
-    m2_out[...] = jnp.where(odd_t, right, left).astype(BF16)
+    low = ~odd_t if second else odd_t
+    out[...] = jnp.where(low, left, right).astype(BF16)
 
 
 def conv_pass(src, count, kernel, emit, chan):
@@ -188,21 +195,17 @@
     for h in range(0, chan, LANES):
         span = slice(h, h + LANES)
         taps = [kernel[t : t + 1, span] for t in range(9)]
-
-        def body(r, carry, span=span, taps=taps):
-            older, newer = carry
+        sums = [None] * (count - 2)
+        for r in range(count):
             x = src[r, :, span]
             before = pltpu.roll(x, 1, 0)
             after = pltpu.roll(x, width - 1, 0)
-            parts = [
-                taps[3 * a] * before + taps[3 * a + 1] * x + taps[3 * a + 2] * after
-                for a in range(3)
-            ]
-            emit(jnp.maximum(r - 2, 0), span, older + parts[2])
-            return newer + parts[1], parts[0]
-
-        zero = jnp.zeros((width, LANES), F32)
-        lax.fori_loop(0, count, body, (zero, zero))
+            for a in range(3):
+                if 0 <= r - a < count - 2:
+                    part = taps[3 * a] * before + taps[3 * a + 1] * x + taps[3 * a + 2] * after
+                    sums[r - a] = part if a == 0 else sums[r - a] + part
+            if r >= 2:
+                emit(r - 2, span, sums[r - 2])
 
 
 def halo_rows(act, p1, p2, t1, t2):
@@ -504,32 +507,7 @@
         k = k[...].astype(F32)
         return jnp.concatenate([k[t : t + 1] for t in range(8, -1, -1)], axis=0)
 
-    def first_pass():
-        kernel = reversed_taps(k_deep)
-        for h in range(0, chan, LANES):
-            span = slice(h, h + LANES)
-            taps = [kernel[t : t + 1, span] for t in range(9)]
-
-            def parts_of(r):
-                x = field[r, :, span]
-                before = pltpu.roll(x, 1, 0)
-                after = pltpu.roll(x, width - 1, 0)
-                return [
-                    taps[3 * a] * before + taps[3 * a + 1] * x + taps[3 * a + 2] * after
-                    for a in range(3)
-                ]
-
-            def body(r, carry):
-                older, newer = carry
-                p = parts_of(r)
-                keep_mix(r - 2, span, older + p[2])
-                return newer + p[1], p[0]
-
-            a = parts_of(0)
-            b = parts_of(1)
-            lax.fori_loop(2, nrow, body, (a[0] + b[1], b[0]))
-
-    first_pass()
+    conv_pass(field, nrow, reversed_taps(k_deep), keep_mix, chan)
     weights = w_mix[...]
 
     for g in range((nrow - 2) // 2):
@@ -594,12 +572,13 @@
     return [2**n for n in range((bands * tiles).bit_length() - 2, -1, -1)]
 
 
-def exchange(m1, m2, axis):
+def exchange(first, second, axis):
     size = lax.axis_size(axis)
-    even = [(i, i + 1) for i in range(0, size - 1, 2)]
-    odd = [(i, i + 1) for i in range(1, size - 1, 2)]
-    both = lambda pairs: pairs + [(j, i) for i, j in pairs]
-    return lax.ppermute(m1, axis, both(even)), lax.ppermute(m2, axis, both(odd))
+    results = []
+    for message, start in ((second, 1), (first, 0)):
+        pairs = [(i, i + 1) for i in range(start, size - 1, 2)]
+        results.append(lax.ppermute(message(), axis, pairs + [(j, i) for i, j in pairs]))
+    return results[1], results[0]
 
 
 def per_device(
@@ -634,13 +613,12 @@
 
     feat = features.transpose(0, 2, 1)
     msg1 = HALO * ccols + ccols // 2
-    pre_first, act, bm, m1, m2, w_wide = call(
+    pre_first, act, bm, m2, w_wide = call(
         embed_kernel,
         [
             ((crows * ccols, chan), F32),
             ((crows, ccols, chan), BF16),
             ((ccols, LANES), F32),
-            ((msg1, chan), BF16),
             ((msg1, chan), BF16),
             ((512, chan), BF16),
         ],
@@ -658,10 +636,17 @@
             for x in (feat, w_embed, land_mask, cell_blocks.reshape(nblk, 1, LANES))
         )
     )
-    p1, p2 = exchange(m1, m2, "band")
+    def pack_first():
+        return call(pack_kernel, [((msg1, chan), BF16)])(act, bm)[0]
+
+    p1, p2 = exchange(pack_first, lambda: m2, "band")
     msg2 = HALO * (crows + 2 * HALO) + 16
-    m1, m2 = call(edges_kernel, [((msg2, chan), BF16)] * 2)(act, bm, p1, p2)
-    t1, t2 = exchange(m1, m2, "tile")
+
+    def edges(second):
+        kernel = functools.partial(edges_kernel, second=second)
+        return call(kernel, [((msg2, chan), BF16)])(act, bm, p1, p2)[0]
+
+    t1, t2 = exchange(lambda: edges(False), lambda: edges(True), "tile")
     slope_first, msg_in = call(
         count_kernel, [((crows * ccols, chan), F32), ((msg_rows, LANES), F32)]
     )(pre_first, bm, msg_in)

time: 39.2 us -> 37.8 us (0.964)
  Pallas kernels: 14 us -> 11.8 us
  waiting for transfers between devices: 4.25 us -> 6.22 us
  starting transfers between devices: 19 us -> 17.8 us
    ppermute x4, starting transfers between devices: 14.5 us -> 10.5 us  [send(): return lax.ppermute(x, ('tile', 'band'), pairs)]
    ppermute x4, starting transfers between devices: 4.49 us -> 7.33 us  [exchange(): lax.ppermute(message(), axis, pairs + [(j, i) for i, j in pairs])]
    pallas_call x8 -> x10, Pallas kernels: 14 us -> 11.8 us  [run(): pl.pallas_call(kernel, out_shape=[jax.ShapeDtypeStruct(s, d) for s, d in...]
    ppermute x4, waiting for transfers between devices: 3.81 us -> 5.13 us  [send(): return lax.ppermute(x, ('tile', 'band'), pairs)]
    ppermute x4, waiting for transfers between devices: 0.44 us -> 1.1 us  [exchange(): lax.ppermute(message(), axis, pairs + [(j, i) for i, j in pairs])]
  transfers between devices with their start and end apart: 8 -> 8, of which waited for: 4 -> 5; matrix products, arithmetic and copies ran while one was open for 1% -> 1% of each run, Pallas kernels for 10% -> 8%
where the time goes in v4:
time: 37.8 us; the launch traced here: 37.6 us
  starting transfers between devices  17.8 us (47%)
  Pallas kernels  11.8 us (31%)
  waiting for transfers between devices  6.22 us (16%)
  between operations  0.84 us (2%)
  local copies, waits for them, and re-layouts  0.81 us (2%)
    pallas_call x10, Pallas kernels, run(): pl.pallas_call(kernel, out_shape=[jax.ShapeDtypeStruct(s, d) for s, d in...  11.8 us
    ppermute x4, starting transfers between devices, send(): return lax.ppermute(x, ('tile', 'band'), pairs)  10.5 us
    ppermute x4, starting transfers between devices, exchange(): lax.ppermute(message(), axis, pairs + [(j, i) for i, j in pairs])  7.33 us
    ppermute x4, waiting for transfers between devices, send(): return lax.ppermute(x, ('tile', 'band'), pairs)  5.13 us
    ppermute x4, waiting for transfers between devices, exchange(): lax.ppermute(message(), axis, pairs + [(j, i) for i, j in pairs])  1.1 us
  transfers between devices with their start and end apart: 8, of which 5 were waited for; matrix products, arithmetic and copies ran while one was open for 1% of the time, Pallas kernels for 8%

profile of v4, /device:TPU:0, one launch (start us, length us, event | category | flops | bytes accessed | tf_op | source)
XLA Modules:
  0.0 37.6 jit_solution(10443429070782729102)
XLA Ops:
  0.6 2.8 %shard_map.129 = (f32[512,256]{1,0:T(8,128)S(1)}, bf16[8,64,256]{2,1,0:T(8,128)(2,1)S(1)}, f32[64,128]{1,0:T(8,128)S(1)}, bf16[288,256]{1,0:T(8,128)(2,1)S(1)}, bf16[512,256]{1,0:T(8,128)(2,1)S(1)}) custom-call(bf16[32,24,256]{2,1,0:T(8,128)(2,1)} %bitcast.40, bf16[384,256]{1,0:T(8,128)(2,1)} %w_hbm.1, s32[32,256]{1,0:T(8,128)} %land.1, s32[81,1,128]{2,1,0:T(1,128)} %bitcast.42), custom_call_target="tpu_custom_call" | custom-call | flops 1000000 | bytes 1000000 | tf_op jit(solution)/shard_map/pallas_call | solution.py:553
  3.5 0.5 %collective-permute-start = (bf16[288,256]{1,0:T(8,128)(2,1)S(1)}, bf16[288,256]{1,0:T(8,128)(2,1)S(1)}, u32[]{:S(2)}, u32[]{:S(2)}) collective-permute-start(bf16[288,256]{1,0:T(8,128)(2,1)S(1)} %shard_map.130), channel_id=1, source_target_pairs={{0,1},{2,3},{1,0},{3,2},{4,5},{6,7},{5,4},{7,6},{8,9},{10,11},{9,8... | collective-permute-start | bytes 442376 | tf_op jit(solution)/shard_map/ppermute | solution.py:580
  4.0 0.7 %collective-permute-start.1 = (bf16[288,256]{1,0:T(8,128)(2,1)S(1)}, bf16[288,256]{1,0:T(8,128)(2,1)S(1)}, u32[]{:S(2)}, u32[]{:S(2)}) collective-permute-start(bf16[288,256]{1,0:T(8,128)(2,1)S(1)} %get-tuple-element.25), channel_id=1, source_target_pairs={{1,2},{2,1},{5,6},{6,5},{9,10},{10,9},{13,14},{14,13},{17,18},{18,... | collective-permute-start | bytes 442376 | tf_op jit(solution)/shard_map/ppermute | solution.py:580
  4.7 0.0 copy-start.5
  4.8 0.6 %copy-done.5 = f32[880]{0:T(1024)S(1)} copy-done((f32[880]{0:T(1024)S(1)}, f32[880]{0:T(1024)}, u32[]{:S(2)}) %copy-start.5) | copy-done | bytes 3544
  5.5 0.7 %collective-permute-start.3 = (bf16[80,256]{1,0:T(8,128)(2,1)S(1)}, bf16[80,256]{1,0:T(8,128)(2,1)S(1)}, u32[]{:S(2)}, u32[]{:S(2)}) collective-permute-start(bf16[80,256]{1,0:T(8,128)(2,1)S(1)} %shard_map.132), channel_id=1, source_target_pairs={{4,8},{8,4},{5,9},{9,5},{6,10},{10,6},{7,11},{11,7},{20,24},{24,20... | collective-permute-start | bytes 122888 | tf_op jit(solution)/shard_map/ppermute | solution.py:580
  6.2 5.5 %collective-permute-start.2 = (bf16[80,256]{1,0:T(8,128)(2,1)S(1)}, bf16[80,256]{1,0:T(8,128)(2,1)S(1)}, u32[]{:S(2)}, u32[]{:S(2)}) collective-permute-start(bf16[80,256]{1,0:T(8,128)(2,1)S(1)} %shard_map.131), channel_id=1, source_target_pairs={{0,4},{8,12},{4,0},{12,8},{1,5},{9,13},{5,1},{13,9},{2,6},{10,14},... | collective-permute-start | bytes 122888 | tf_op jit(solution)/shard_map/ppermute | solution.py:580
  11.7 0.1 pad_convert_fusion
  11.9 0.0 copy-start.1
  11.9 0.0 copy-start.2
  11.9 0.6 %shard_map.133 = (f32[512,256]{1,0:T(8,128)S(1)}, f32[16,128]{1,0:T(8,128)S(1)}) custom-call(f32[512,256]{1,0:T(8,128)S(1)} %get-tuple-element.26.pre_first, f32[64,128]{1,0:T(8,128)S(1)} %get-tuple-element.24.bm, f32[16,128]{1,0:T(8,128)S(1)} %concatenate.22.msg_in), custom_call_target="tpu_custom_call" | custom-call | flops 1000000 | bytes 1000000 | tf_op jit(solution)/shard_map/pallas_call | solution.py:553
  12.6 1.1 %collective-permute-done.2.t1 = bf16[80,256]{1,0:T(8,128)(2,1)S(1)} collective-permute-done((bf16[80,256]{1,0:T(8,128)(2,1)S(1)}, bf16[80,256]{1,0:T(8,128)(2,1)S(1)}, u32[]{:S(2)}, u32[]{:S(2)}) %collective-permute-start.2) | collective-permute-done | bytes 40992 | tf_op jit(solution)/shard_map/ppermute | solution.py:580
  13.7 2.0 %shard_map.134 = (f32[12,72,256]{2,1,0:T(8,128)S(1)}, f32[10,72,256]{2,1,0:T(8,128)S(1)}, f32[10,72,256]{2,1,0:T(8,128)S(1)}, f32[8,72,256]{2,1,0:T(8,128)S(1)},...) custom-call(bf16[8,64,256]{2,1,0:T(8,128)(2,1)S(1)} %get-tuple-element.23.act, f32[64,128]{1,0:T(8,128)S(1)} %get-tuple-element.24.bm, ...), custom_call_target="tpu_custom_call" | custom-call | flops 1000000 | bytes 1000000 | tf_op jit(solution)/shard_map/pallas_call | solution.py:553
  15.7 2.0 %collective-permute-start.4 = (f32[1,16,128]{2,1,0:T(8,128)S(1)}, f32[1,16,128]{2,1,0:T(8,128)S(1)}, u32[]{:S(2)}, u32[]{:S(2)}) collective-permute-start(f32[1,16,128]{2,1,0:T(8,128)S(1)} %bitcast.35), channel_id=1, source_target_pairs={{0,8},{1,9},{2,10},{3,11},{4,12},{5,13},{6,14},{7,15},{8,0},{9,1},... | collective-permute-start | bytes 24584 | tf_op jit(solution)/shard_map/ppermute | solution.py:688
  17.6 1.6 %shard_map.135 = (f32[10,72,256]{2,1,0:T(8,128)S(1)}, f32[8,72,256]{2,1,0:T(8,128)S(1)}, f32[32,256]{1,0:T(8,128)}) custom-call(f32[1,16,128]{2,1,0:T(8,128)S(1)} %bitcast.36, f32[10,72,256]{2,1,0:T(8,128)S(1)} %get-tuple-element.29.mix, f32[8,72,256]{2,1,0:T(8,128)S(1)} %get-tuple-element.30.deep, f32[64,128]{1,0:T(8,128)S(1)} %get-tuple-element.31.pred, ...), custom_call_target="tpu_custom_call" | custom-call | flops 1000000 | bytes 1000000 | tf_op jit(solution)/shard_map/pallas_call | solution.py:553
  19.3 1.0 %collective-permute-done.4 = f32[1,16,128]{2,1,0:T(8,128)S(1)} collective-permute-done((f32[1,16,128]{2,1,0:T(8,128)S(1)}, f32[1,16,128]{2,1,0:T(8,128)S(1)}, u32[]{:S(2)}, u32[]{:S(2)}) %collective-permute-start.4) | collective-permute-done | bytes 8224 | tf_op jit(solution)/shard_map/ppermute | solution.py:688
  20.3 2.0 %collective-permute-start.5 = (f32[2,16,128]{2,1,0:T(8,128)S(1)}, f32[2,16,128]{2,1,0:T(8,128)S(1)}, u32[]{:S(2)}, u32[]{:S(2)}) collective-permute-start(f32[2,16,128]{2,1,0:T(8,128)S(1)} %pad_maximum_fusion.2.after), channel_id=1, source_target_pairs={{0,4},{1,5},{2,6},{3,7},{4,0},{5,1},{6,2},{7,3},{8,12},{9,13},{10,... | collective-permute-start | bytes 49160 | tf_op jit(solution)/shard_map/ppermute | solution.py:688
  22.3 0.4 %shard_map.136.rim_above = f32[2,72,256]{2,1,0:T(8,128)S(1)} custom-call(f32[2,16,128]{2,1,0:T(8,128)S(1)} %pad_maximum_fusion.2.after, bf16[8,64,256]{2,1,0:T(8,128)(2,1)S(1)} %get-tuple-element.23.act, bf16[288,256]{1,0:T(8,128)(2,1)S(1)} %collective-permute-done.p1, bf16[288,256]{1,0:T(8,128)(2,1)S(1)} %collective-permute-done.1.p2, ...), custom_call_target="tpu_custom_call" | custom-call | flops 1000000 | bytes 1000000 | tf_op jit(solution)/shard_map/pallas_call | solution.py:553
  22.7 1.4 %collective-permute-done.5 = f32[2,16,128]{2,1,0:T(8,128)S(1)} collective-permute-done((f32[2,16,128]{2,1,0:T(8,128)S(1)}, f32[2,16,128]{2,1,0:T(8,128)S(1)}, u32[]{:S(2)}, u32[]{:S(2)}) %collective-permute-start.5) | collective-permute-done | bytes 16416 | tf_op jit(solution)/shard_map/ppermute | solution.py:688
  24.1 6.5 %collective-permute-start.6 = (f32[4,16,128]{2,1,0:T(8,128)S(1)}, f32[4,16,128]{2,1,0:T(8,128)S(1)}, u32[]{:S(2)}, u32[]{:S(2)}) collective-permute-start(f32[4,16,128]{2,1,0:T(8,128)S(1)} %pad_maximum_fusion.1.after), channel_id=1, source_target_pairs={{0,2},{1,3},{2,0},{3,1},{4,6},{5,7},{6,4},{7,5},{8,10},{9,11},{10,... | collective-permute-start | bytes 98312 | tf_op jit(solution)/shard_map/ppermute | solution.py:688
  30.6 0.4 %shard_map.137.rim_below = f32[2,72,256]{2,1,0:T(8,128)S(1)} custom-call(f32[4,16,128]{2,1,0:T(8,128)S(1)} %pad_maximum_fusion.1.after, bf16[8,64,256]{2,1,0:T(8,128)(2,1)S(1)} %get-tuple-element.23.act, bf16[288,256]{1,0:T(8,128)(2,1)S(1)} %collective-permute-done.p1, bf16[288,256]{1,0:T(8,128)(2,1)S(1)} %collective-permute-done.1.p2, ...), custom_call_target="tpu_custom_call" | custom-call | flops 1000000 | bytes 1000000 | tf_op jit(solution)/shard_map/pallas_call | solution.py:553
  31.1 1.5 %collective-permute-done.6 = f32[4,16,128]{2,1,0:T(8,128)S(1)} collective-permute-done((f32[4,16,128]{2,1,0:T(8,128)S(1)}, f32[4,16,128]{2,1,0:T(8,128)S(1)}, u32[]{:S(2)}, u32[]{:S(2)}) %collective-permute-start.6) | collective-permute-done | bytes 32800 | tf_op jit(solution)/shard_map/ppermute | solution.py:688
  32.6 1.2 %collective-permute-done.7 = f32[8,16,128]{2,1,0:T(8,128)S(1)} collective-permute-done((f32[8,16,128]{2,1,0:T(8,128)S(1)}, f32[8,16,128]{2,1,0:T(8,128)S(1)}, u32[]{:S(2)}, u32[]{:S(2)}) %collective-permute-start.7) | collective-permute-done | bytes 65568 | tf_op jit(solution)/shard_map/ppermute | solution.py:688
  33.8 3.8 %shard_map.138 = (f32[8,128]{1,0:T(8,128)}, f32[1,1]{1,0:T(1,128)}, bf16[32,24,256]{2,1,0:T(8,128)(2,1)}) custom-call(f32[16,16,128]{2,1,0:T(8,128)S(1)} %constant_dynamic-update-slice_fusion.gathered, f32[64,128]{1,0:T(8,128)S(1)} %get-tuple-element.24.bm, bf16[288,256]{1,0:T(8,128)(2,1)S(1)} %collective-permute-done.p1, ...), custom_call_target="tpu_custom_call" | custom-call | flops 1000000 | bytes 1000000 | tf_op jit(solution)/shard_map/pallas_call | solution.py:553
  (36 shorter events, 0.3 us)
Async XLA Ops:
  3.4 1.3 %copy-start.4 = (bf16[256,16]{0,1:T(8,128)(2,1)S(1)}, bf16[256,16]{0,1:T(8,128)(2,1)}, u32[]{:S(2)}) copy-start(bf16[256,16]{0,1:T(8,128)(2,1)} %param.19) | copy-start | bytes 24580
  3.5 1.2 %copy-start.6 = (s32[1,1,81]{2,1,0:T(1,128)S(1)}, s32[1,1,81]{2,1,0:T(1,128)}, u32[]{:S(2)}) copy-start(s32[1,1,81]{2,1,0:T(1,128)} %param.13) | copy-start | bytes 976
  3.5 1.9 %collective-permute-start = (bf16[288,256]{1,0:T(8,128)(2,1)S(1)}, bf16[288,256]{1,0:T(8,128)(2,1)S(1)}, u32[]{:S(2)}, u32[]{:S(2)}) collective-permute-start(bf16[288,256]{1,0:T(8,128)(2,1)S(1)} %shard_map.130), channel_id=1, source_target_pairs={{0,1},{2,3},{1,0},{3,2},{4,5},{6,7},{5,4},{7,6},{8,9},{10,11},{9,8... | collective-permute-start | bytes 442376 | tf_op jit(solution)/shard_map/ppermute | solution.py:580
  4.0 1.4 %collective-permute-start.1 = (bf16[288,256]{1,0:T(8,128)(2,1)S(1)}, bf16[288,256]{1,0:T(8,128)(2,1)S(1)}, u32[]{:S(2)}, u32[]{:S(2)}) collective-permute-start(bf16[288,256]{1,0:T(8,128)(2,1)S(1)} %get-tuple-element.25), channel_id=1, source_target_pairs={{1,2},{2,1},{5,6},{6,5},{9,10},{10,9},{13,14},{14,13},{17,18},{18,... | collective-permute-start | bytes 442376 | tf_op jit(solution)/shard_map/ppermute | solution.py:580
  4.7 0.7 %copy-start.5 = (f32[880]{0:T(1024)S(1)}, f32[880]{0:T(1024)}, u32[]{:S(2)}) copy-start(f32[880]{0:T(1024)} %param.14) | copy-start | bytes 10564
  5.5 7.1 %collective-permute-start.3 = (bf16[80,256]{1,0:T(8,128)(2,1)S(1)}, bf16[80,256]{1,0:T(8,128)(2,1)S(1)}, u32[]{:S(2)}, u32[]{:S(2)}) collective-permute-start(bf16[80,256]{1,0:T(8,128)(2,1)S(1)} %shard_map.132), channel_id=1, source_target_pairs={{4,8},{8,4},{5,9},{9,5},{6,10},{10,6},{7,11},{11,7},{20,24},{24,20... | collective-permute-start | bytes 122888 | tf_op jit(solution)/shard_map/ppermute | solution.py:580
  6.2 7.5 %collective-permute-start.2 = (bf16[80,256]{1,0:T(8,128)(2,1)S(1)}, bf16[80,256]{1,0:T(8,128)(2,1)S(1)}, u32[]{:S(2)}, u32[]{:S(2)}) collective-permute-start(bf16[80,256]{1,0:T(8,128)(2,1)S(1)} %shard_map.131), channel_id=1, source_target_pairs={{0,4},{8,12},{4,0},{12,8},{1,5},{9,13},{5,1},{13,9},{2,6},{10,14},... | collective-permute-start | bytes 122888 | tf_op jit(solution)/shard_map/ppermute | solution.py:580
  11.9 1.8 %copy-start = (bf16[256,256]{1,0:T(8,128)(2,1)S(1)}, bf16[256,256]{1,0:T(8,128)(2,1)}, u32[]{:S(2)}) copy-start(bf16[256,256]{1,0:T(8,128)(2,1)} %w_mix.7) | copy-start | bytes 393220
  11.9 1.8 %copy-start.1 = (bf16[9,256]{1,0:T(8,128)(2,1)S(1)}, bf16[9,256]{1,0:T(8,128)(2,1)}, u32[]{:S(2)}) copy-start(bf16[9,256]{1,0:T(8,128)(2,1)} %k_first.7) | copy-start | bytes 13828
  11.9 1.7 %copy-start.2 = (bf16[9,256]{1,0:T(8,128)(2,1)S(1)}, bf16[9,256]{1,0:T(8,128)(2,1)}, u32[]{:S(2)}) copy-start(bf16[9,256]{1,0:T(8,128)(2,1)} %k_deep.7) | copy-start | bytes 13828
  13.7 4.0 %copy-start.3 = (s32[32,256]{1,0:T(8,128)S(1)}, s32[32,256]{1,0:T(8,128)}, u32[]{:S(2)}) copy-start(s32[32,256]{1,0:T(8,128)} %land.1) | copy-start | bytes 98308
  15.7 4.6 %collective-permute-start.4 = (f32[1,16,128]{2,1,0:T(8,128)S(1)}, f32[1,16,128]{2,1,0:T(8,128)S(1)}, u32[]{:S(2)}, u32[]{:S(2)}) collective-permute-start(f32[1,16,128]{2,1,0:T(8,128)S(1)} %bitcast.35), channel_id=1, source_target_pairs={{0,8},{1,9},{2,10},{3,11},{4,12},{5,13},{6,14},{7,15},{8,0},{9,1},... | collective-permute-start | bytes 24584 | tf_op jit(solution)/shard_map/ppermute | solution.py:688
  20.3 3.8 %collective-permute-start.5 = (f32[2,16,128]{2,1,0:T(8,128)S(1)}, f32[2,16,128]{2,1,0:T(8,128)S(1)}, u32[]{:S(2)}, u32[]{:S(2)}) collective-permute-start(f32[2,16,128]{2,1,0:T(8,128)S(1)} %pad_maximum_fusion.2.after), channel_id=1, source_target_pairs={{0,4},{1,5},{2,6},{3,7},{4,0},{5,1},{6,2},{7,3},{8,12},{9,13},{10,... | collective-permute-start | bytes 49160 | tf_op jit(solution)/shard_map/ppermute | solution.py:688
  24.1 8.4 %collective-permute-start.6 = (f32[4,16,128]{2,1,0:T(8,128)S(1)}, f32[4,16,128]{2,1,0:T(8,128)S(1)}, u32[]{:S(2)}, u32[]{:S(2)}) collective-permute-start(f32[4,16,128]{2,1,0:T(8,128)S(1)} %pad_maximum_fusion.1.after), channel_id=1, source_target_pairs={{0,2},{1,3},{2,0},{3,1},{4,6},{5,7},{6,4},{7,5},{8,10},{9,11},{10,... | collective-permute-start | bytes 98312 | tf_op jit(solution)/shard_map/ppermute | solution.py:688
  32.5 1.3 %collective-permute-start.7 = (f32[8,16,128]{2,1,0:T(8,128)S(1)}, f32[8,16,128]{2,1,0:T(8,128)S(1)}, u32[]{:S(2)}, u32[]{:S(2)}) collective-permute-start(f32[8,16,128]{2,1,0:T(8,128)S(1)} %pad_maximum_fusion), channel_id=1, source_target_pairs={{0,1},{1,0},{2,3},{3,2},{4,5},{5,4},{6,7},{7,6},{8,9},{9,8},{10,11... | collective-permute-start | bytes 196616 | tf_op jit(solution)/shard_map/ppermute | solution.py:688

commit v5 on v4

--- a/solution.py
+++ b/solution.py
@@ -91,18 +91,17 @@
     sub_a = iota((LANES, LANES), 0).astype(F32).astype(BF16)
     sub_b = iota((ccols, LANES), 0).astype(F32).astype(BF16)
     one, none = jnp.ones((), BF16), jnp.zeros((), BF16)
+    cells = blocks[...].reshape(nblk, LANES)
+    named = cells < rows * cols
+    all_q = jnp.where(named, (cells & 3) * rows + (cells >> shift_row), -1).astype(F32)
+    all_j = ((cells & (cols - 1)) >> 2).astype(F32)
     for first in range(0, nblk, chunk):
         hot_q, hot_j = [], []
-        for step in range(chunk):
-            k = first + step
-            cell = blocks[k]
-            named = cell < rows * cols
-            q = jnp.where(named, (cell & 3) * rows + (cell >> shift_row), -1)
-            j = (cell & (cols - 1)) >> 2
-            hot_q.append(jnp.where(sub_a == q.astype(F32).astype(BF16), one, none))
-            hot_j.append(
-                jnp.where(sub_b == j.astype(F32).astype(BF16), jnp.array(k + 1, BF16), none)
-            )
+        for k in range(first, first + chunk):
+            q = all_q[k : k + 1].astype(BF16)
+            j = all_j[k : k + 1].astype(BF16)
+            hot_q.append(jnp.where(sub_a == q, one, none))
+            hot_j.append(jnp.where(sub_b == j, jnp.array(k + 1, BF16), none))
         total = total + dot_nt(
             jnp.concatenate(hot_j, axis=1), jnp.concatenate(hot_q, axis=1)
         )
@@ -523,7 +522,7 @@
     conv_pass(field, nrow - 2, reversed_taps(k_first), keep_first, chan)
 
     c_pad = 32
-    out = dot_nt(w_wide[...], proj[...].reshape(crows * ccols, chan)).astype(BF16)
+    out = dot_nt(w_wide[...], proj[...].reshape(crows * ccols, chan))
     wide = 4 * c_pad
     spread = spread_matrix(4 * ccols)
     group = crows // 4
@@ -541,7 +540,7 @@
             ],
             axis=0,
         )
-        fine = dot(lhs, spread)
+        fine = dot(lhs.astype(BF16), spread)
         for r in range(4 * group):
             grad_out[4 * group * g + r] = fine[r * c_pad : r * c_pad + c_in].astype(BF16)
 

time: 37.8 us -> 37.8 us (level)
  no operation moved by 1% of the time
where the time goes in v5:
time: 37.8 us; the launch traced here: 37.6 us
  starting transfers between devices  17.8 us (47%)
  Pallas kernels  11.7 us (31%)
  waiting for transfers between devices  6.22 us (16%)
  between operations  0.84 us (2%)
  local copies, waits for them, and re-layouts  0.81 us (2%)
    pallas_call x10, Pallas kernels, run(): pl.pallas_call(kernel, out_shape=[jax.ShapeDtypeStruct(s, d) for s, d in...  11.7 us
    ppermute x4, starting transfers between devices, send(): return lax.ppermute(x, ('tile', 'band'), pairs)  10.5 us
    ppermute x4, starting transfers between devices, exchange(): lax.ppermute(message(), axis, pairs + [(j, i) for i, j in pairs])  7.33 us
    ppermute x4, waiting for transfers between devices, send(): return lax.ppermute(x, ('tile', 'band'), pairs)  5.13 us
    ppermute x4, waiting for transfers between devices, exchange(): lax.ppermute(message(), axis, pairs + [(j, i) for i, j in pairs])  1.1 us
  transfers between devices with their start and end apart: 8, of which 5 were waited for; matrix products, arithmetic and copies ran while one was open for 1% of the time, Pallas kernels for 8%

profile of v5, /device:TPU:0, one launch (start us, length us, event | category | flops | bytes accessed | tf_op | source)
XLA Modules:
  0.0 37.6 jit_solution(16774074058624476571)
XLA Ops:
  0.6 2.8 %shard_map.129 = (f32[512,256]{1,0:T(8,128)S(1)}, bf16[8,64,256]{2,1,0:T(8,128)(2,1)S(1)}, f32[64,128]{1,0:T(8,128)S(1)}, bf16[288,256]{1,0:T(8,128)(2,1)S(1)}, bf16[512,256]{1,0:T(8,128)(2,1)S(1)}) custom-call(bf16[32,24,256]{2,1,0:T(8,128)(2,1)} %bitcast.40, bf16[384,256]{1,0:T(8,128)(2,1)} %w_hbm.1, s32[32,256]{1,0:T(8,128)} %land.1, s32[81,1,128]{2,1,0:T(1,128)} %bitcast.42), custom_call_target="tpu_custom_call" | custom-call | flops 1000000 | bytes 1000000 | tf_op jit(solution)/shard_map/pallas_call | solution.py:552
  3.4 0.0 copy-start.4
  3.5 0.0 copy-start.6
  3.5 0.5 %collective-permute-start = (bf16[288,256]{1,0:T(8,128)(2,1)S(1)}, bf16[288,256]{1,0:T(8,128)(2,1)S(1)}, u32[]{:S(2)}, u32[]{:S(2)}) collective-permute-start(bf16[288,256]{1,0:T(8,128)(2,1)S(1)} %shard_map.130), channel_id=1, source_target_pairs={{0,1},{2,3},{1,0},{3,2},{4,5},{6,7},{5,4},{7,6},{8,9},{10,11},{9,8... | collective-permute-start | bytes 442376 | tf_op jit(solution)/shard_map/ppermute | solution.py:579
  4.0 0.7 %collective-permute-start.1 = (bf16[288,256]{1,0:T(8,128)(2,1)S(1)}, bf16[288,256]{1,0:T(8,128)(2,1)S(1)}, u32[]{:S(2)}, u32[]{:S(2)}) collective-permute-start(bf16[288,256]{1,0:T(8,128)(2,1)S(1)} %get-tuple-element.25), channel_id=1, source_target_pairs={{1,2},{2,1},{5,6},{6,5},{9,10},{10,9},{13,14},{14,13},{17,18},{18,... | collective-permute-start | bytes 442376 | tf_op jit(solution)/shard_map/ppermute | solution.py:579
  4.8 0.6 %copy-done.5 = f32[880]{0:T(1024)S(1)} copy-done((f32[880]{0:T(1024)S(1)}, f32[880]{0:T(1024)}, u32[]{:S(2)}) %copy-start.5) | copy-done | bytes 3544
  5.5 0.7 %collective-permute-start.3 = (bf16[80,256]{1,0:T(8,128)(2,1)S(1)}, bf16[80,256]{1,0:T(8,128)(2,1)S(1)}, u32[]{:S(2)}, u32[]{:S(2)}) collective-permute-start(bf16[80,256]{1,0:T(8,128)(2,1)S(1)} %shard_map.132), channel_id=1, source_target_pairs={{4,8},{8,4},{5,9},{9,5},{6,10},{10,6},{7,11},{11,7},{20,24},{24,20... | collective-permute-start | bytes 122888 | tf_op jit(solution)/shard_map/ppermute | solution.py:579
  6.2 5.5 %collective-permute-start.2 = (bf16[80,256]{1,0:T(8,128)(2,1)S(1)}, bf16[80,256]{1,0:T(8,128)(2,1)S(1)}, u32[]{:S(2)}, u32[]{:S(2)}) collective-permute-start(bf16[80,256]{1,0:T(8,128)(2,1)S(1)} %shard_map.131), channel_id=1, source_target_pairs={{0,4},{8,12},{4,0},{12,8},{1,5},{9,13},{5,1},{13,9},{2,6},{10,14},... | collective-permute-start | bytes 122888 | tf_op jit(solution)/shard_map/ppermute | solution.py:579
  11.7 0.1 pad_convert_fusion
  11.9 0.6 %shard_map.133 = (f32[512,256]{1,0:T(8,128)S(1)}, f32[16,128]{1,0:T(8,128)S(1)}) custom-call(f32[512,256]{1,0:T(8,128)S(1)} %get-tuple-element.26.pre_first, f32[64,128]{1,0:T(8,128)S(1)} %get-tuple-element.24.bm, f32[16,128]{1,0:T(8,128)S(1)} %concatenate.22.msg_in), custom_call_target="tpu_custom_call" | custom-call | flops 1000000 | bytes 1000000 | tf_op jit(solution)/shard_map/pallas_call | solution.py:552
  12.6 1.1 %collective-permute-done.2.t1 = bf16[80,256]{1,0:T(8,128)(2,1)S(1)} collective-permute-done((bf16[80,256]{1,0:T(8,128)(2,1)S(1)}, bf16[80,256]{1,0:T(8,128)(2,1)S(1)}, u32[]{:S(2)}, u32[]{:S(2)}) %collective-permute-start.2) | collective-permute-done | bytes 40992 | tf_op jit(solution)/shard_map/ppermute | solution.py:579
  13.7 0.0 copy-start.3
  13.7 2.0 %shard_map.134 = (f32[12,72,256]{2,1,0:T(8,128)S(1)}, f32[10,72,256]{2,1,0:T(8,128)S(1)}, f32[10,72,256]{2,1,0:T(8,128)S(1)}, f32[8,72,256]{2,1,0:T(8,128)S(1)},...) custom-call(bf16[8,64,256]{2,1,0:T(8,128)(2,1)S(1)} %get-tuple-element.23.act, f32[64,128]{1,0:T(8,128)S(1)} %get-tuple-element.24.bm, ...), custom_call_target="tpu_custom_call" | custom-call | flops 1000000 | bytes 1000000 | tf_op jit(solution)/shard_map/pallas_call | solution.py:552
  15.7 2.0 %collective-permute-start.4 = (f32[1,16,128]{2,1,0:T(8,128)S(1)}, f32[1,16,128]{2,1,0:T(8,128)S(1)}, u32[]{:S(2)}, u32[]{:S(2)}) collective-permute-start(f32[1,16,128]{2,1,0:T(8,128)S(1)} %bitcast.35), channel_id=1, source_target_pairs={{0,8},{1,9},{2,10},{3,11},{4,12},{5,13},{6,14},{7,15},{8,0},{9,1},... | collective-permute-start | bytes 24584 | tf_op jit(solution)/shard_map/ppermute | solution.py:687
  17.6 1.6 %shard_map.135 = (f32[10,72,256]{2,1,0:T(8,128)S(1)}, f32[8,72,256]{2,1,0:T(8,128)S(1)}, f32[32,256]{1,0:T(8,128)}) custom-call(f32[1,16,128]{2,1,0:T(8,128)S(1)} %bitcast.36, f32[10,72,256]{2,1,0:T(8,128)S(1)} %get-tuple-element.29.mix, f32[8,72,256]{2,1,0:T(8,128)S(1)} %get-tuple-element.30.deep, f32[64,128]{1,0:T(8,128)S(1)} %get-tuple-element.31.pred, ...), custom_call_target="tpu_custom_call" | custom-call | flops 1000000 | bytes 1000000 | tf_op jit(solution)/shard_map/pallas_call | solution.py:552
  19.3 1.0 %collective-permute-done.4 = f32[1,16,128]{2,1,0:T(8,128)S(1)} collective-permute-done((f32[1,16,128]{2,1,0:T(8,128)S(1)}, f32[1,16,128]{2,1,0:T(8,128)S(1)}, u32[]{:S(2)}, u32[]{:S(2)}) %collective-permute-start.4) | collective-permute-done | bytes 8224 | tf_op jit(solution)/shard_map/ppermute | solution.py:687
  20.3 2.0 %collective-permute-start.5 = (f32[2,16,128]{2,1,0:T(8,128)S(1)}, f32[2,16,128]{2,1,0:T(8,128)S(1)}, u32[]{:S(2)}, u32[]{:S(2)}) collective-permute-start(f32[2,16,128]{2,1,0:T(8,128)S(1)} %pad_maximum_fusion.2.after), channel_id=1, source_target_pairs={{0,4},{1,5},{2,6},{3,7},{4,0},{5,1},{6,2},{7,3},{8,12},{9,13},{10,... | collective-permute-start | bytes 49160 | tf_op jit(solution)/shard_map/ppermute | solution.py:687
  22.3 0.4 %shard_map.136.rim_above = f32[2,72,256]{2,1,0:T(8,128)S(1)} custom-call(f32[2,16,128]{2,1,0:T(8,128)S(1)} %pad_maximum_fusion.2.after, bf16[8,64,256]{2,1,0:T(8,128)(2,1)S(1)} %get-tuple-element.23.act, bf16[288,256]{1,0:T(8,128)(2,1)S(1)} %collective-permute-done.p1, bf16[288,256]{1,0:T(8,128)(2,1)S(1)} %collective-permute-done.1.p2, ...), custom_call_target="tpu_custom_call" | custom-call | flops 1000000 | bytes 1000000 | tf_op jit(solution)/shard_map/pallas_call | solution.py:552
  22.7 1.4 %collective-permute-done.5 = f32[2,16,128]{2,1,0:T(8,128)S(1)} collective-permute-done((f32[2,16,128]{2,1,0:T(8,128)S(1)}, f32[2,16,128]{2,1,0:T(8,128)S(1)}, u32[]{:S(2)}, u32[]{:S(2)}) %collective-permute-start.5) | collective-permute-done | bytes 16416 | tf_op jit(solution)/shard_map/ppermute | solution.py:687
  24.1 6.5 %collective-permute-start.6 = (f32[4,16,128]{2,1,0:T(8,128)S(1)}, f32[4,16,128]{2,1,0:T(8,128)S(1)}, u32[]{:S(2)}, u32[]{:S(2)}) collective-permute-start(f32[4,16,128]{2,1,0:T(8,128)S(1)} %pad_maximum_fusion.1.after), channel_id=1, source_target_pairs={{0,2},{1,3},{2,0},{3,1},{4,6},{5,7},{6,4},{7,5},{8,10},{9,11},{10,... | collective-permute-start | bytes 98312 | tf_op jit(solution)/shard_map/ppermute | solution.py:687
  30.6 0.4 %shard_map.137.rim_below = f32[2,72,256]{2,1,0:T(8,128)S(1)} custom-call(f32[4,16,128]{2,1,0:T(8,128)S(1)} %pad_maximum_fusion.1.after, bf16[8,64,256]{2,1,0:T(8,128)(2,1)S(1)} %get-tuple-element.23.act, bf16[288,256]{1,0:T(8,128)(2,1)S(1)} %collective-permute-done.p1, bf16[288,256]{1,0:T(8,128)(2,1)S(1)} %collective-permute-done.1.p2, ...), custom_call_target="tpu_custom_call" | custom-call | flops 1000000 | bytes 1000000 | tf_op jit(solution)/shard_map/pallas_call | solution.py:552
  31.1 1.5 %collective-permute-done.6 = f32[4,16,128]{2,1,0:T(8,128)S(1)} collective-permute-done((f32[4,16,128]{2,1,0:T(8,128)S(1)}, f32[4,16,128]{2,1,0:T(8,128)S(1)}, u32[]{:S(2)}, u32[]{:S(2)}) %collective-permute-start.6) | collective-permute-done | bytes 32800 | tf_op jit(solution)/shard_map/ppermute | solution.py:687
  32.6 1.2 %collective-permute-done.7 = f32[8,16,128]{2,1,0:T(8,128)S(1)} collective-permute-done((f32[8,16,128]{2,1,0:T(8,128)S(1)}, f32[8,16,128]{2,1,0:T(8,128)S(1)}, u32[]{:S(2)}, u32[]{:S(2)}) %collective-permute-start.7) | collective-permute-done | bytes 65568 | tf_op jit(solution)/shard_map/ppermute | solution.py:687
  33.8 3.8 %shard_map.138 = (f32[8,128]{1,0:T(8,128)}, f32[1,1]{1,0:T(1,128)}, bf16[32,24,256]{2,1,0:T(8,128)(2,1)}) custom-call(f32[16,16,128]{2,1,0:T(8,128)S(1)} %constant_dynamic-update-slice_fusion.gathered, f32[64,128]{1,0:T(8,128)S(1)} %get-tuple-element.24.bm, bf16[288,256]{1,0:T(8,128)(2,1)S(1)} %collective-permute-done.p1, ...), custom_call_target="tpu_custom_call" | custom-call | flops 1000000 | bytes 1000000 | tf_op jit(solution)/shard_map/pallas_call | solution.py:552
  (36 shorter events, 0.3 us)
Async XLA Ops:
  3.4 1.3 %copy-start.4 = (bf16[256,16]{0,1:T(8,128)(2,1)S(1)}, bf16[256,16]{0,1:T(8,128)(2,1)}, u32[]{:S(2)}) copy-start(bf16[256,16]{0,1:T(8,128)(2,1)} %param.19) | copy-start | bytes 24580
  3.5 1.2 %copy-start.6 = (s32[1,1,81]{2,1,0:T(1,128)S(1)}, s32[1,1,81]{2,1,0:T(1,128)}, u32[]{:S(2)}) copy-start(s32[1,1,81]{2,1,0:T(1,128)} %param.13) | copy-start | bytes 976
  3.5 1.9 %collective-permute-start = (bf16[288,256]{1,0:T(8,128)(2,1)S(1)}, bf16[288,256]{1,0:T(8,128)(2,1)S(1)}, u32[]{:S(2)}, u32[]{:S(2)}) collective-permute-start(bf16[288,256]{1,0:T(8,128)(2,1)S(1)} %shard_map.130), channel_id=1, source_target_pairs={{0,1},{2,3},{1,0},{3,2},{4,5},{6,7},{5,4},{7,6},{8,9},{10,11},{9,8... | collective-permute-start | bytes 442376 | tf_op jit(solution)/shard_map/ppermute | solution.py:579
  4.0 1.4 %collective-permute-start.1 = (bf16[288,256]{1,0:T(8,128)(2,1)S(1)}, bf16[288,256]{1,0:T(8,128)(2,1)S(1)}, u32[]{:S(2)}, u32[]{:S(2)}) collective-permute-start(bf16[288,256]{1,0:T(8,128)(2,1)S(1)} %get-tuple-element.25), channel_id=1, source_target_pairs={{1,2},{2,1},{5,6},{6,5},{9,10},{10,9},{13,14},{14,13},{17,18},{18,... | collective-permute-start | bytes 442376 | tf_op jit(solution)/shard_map/ppermute | solution.py:579
  4.7 0.7 %copy-start.5 = (f32[880]{0:T(1024)S(1)}, f32[880]{0:T(1024)}, u32[]{:S(2)}) copy-start(f32[880]{0:T(1024)} %param.14) | copy-start | bytes 10564
  5.5 7.1 %collective-permute-start.3 = (bf16[80,256]{1,0:T(8,128)(2,1)S(1)}, bf16[80,256]{1,0:T(8,128)(2,1)S(1)}, u32[]{:S(2)}, u32[]{:S(2)}) collective-permute-start(bf16[80,256]{1,0:T(8,128)(2,1)S(1)} %shard_map.132), channel_id=1, source_target_pairs={{4,8},{8,4},{5,9},{9,5},{6,10},{10,6},{7,11},{11,7},{20,24},{24,20... | collective-permute-start | bytes 122888 | tf_op jit(solution)/shard_map/ppermute | solution.py:579
  6.2 7.5 %collective-permute-start.2 = (bf16[80,256]{1,0:T(8,128)(2,1)S(1)}, bf16[80,256]{1,0:T(8,128)(2,1)S(1)}, u32[]{:S(2)}, u32[]{:S(2)}) collective-permute-start(bf16[80,256]{1,0:T(8,128)(2,1)S(1)} %shard_map.131), channel_id=1, source_target_pairs={{0,4},{8,12},{4,0},{12,8},{1,5},{9,13},{5,1},{13,9},{2,6},{10,14},... | collective-permute-start | bytes 122888 | tf_op jit(solution)/shard_map/ppermute | solution.py:579
  11.9 1.8 %copy-start = (bf16[256,256]{1,0:T(8,128)(2,1)S(1)}, bf16[256,256]{1,0:T(8,128)(2,1)}, u32[]{:S(2)}) copy-start(bf16[256,256]{1,0:T(8,128)(2,1)} %w_mix.7) | copy-start | bytes 393220
  11.9 1.8 %copy-start.1 = (bf16[9,256]{1,0:T(8,128)(2,1)S(1)}, bf16[9,256]{1,0:T(8,128)(2,1)}, u32[]{:S(2)}) copy-start(bf16[9,256]{1,0:T(8,128)(2,1)} %k_first.7) | copy-start | bytes 13828
  11.9 1.7 %copy-start.2 = (bf16[9,256]{1,0:T(8,128)(2,1)S(1)}, bf16[9,256]{1,0:T(8,128)(2,1)}, u32[]{:S(2)}) copy-start(bf16[9,256]{1,0:T(8,128)(2,1)} %k_deep.7) | copy-start | bytes 13828
  13.7 4.0 %copy-start.3 = (s32[32,256]{1,0:T(8,128)S(1)}, s32[32,256]{1,0:T(8,128)}, u32[]{:S(2)}) copy-start(s32[32,256]{1,0:T(8,128)} %land.1) | copy-start | bytes 98308
  15.7 4.6 %collective-permute-start.4 = (f32[1,16,128]{2,1,0:T(8,128)S(1)}, f32[1,16,128]{2,1,0:T(8,128)S(1)}, u32[]{:S(2)}, u32[]{:S(2)}) collective-permute-start(f32[1,16,128]{2,1,0:T(8,128)S(1)} %bitcast.35), channel_id=1, source_target_pairs={{0,8},{1,9},{2,10},{3,11},{4,12},{5,13},{6,14},{7,15},{8,0},{9,1},... | collective-permute-start | bytes 24584 | tf_op jit(solution)/shard_map/ppermute | solution.py:687
  20.3 3.8 %collective-permute-start.5 = (f32[2,16,128]{2,1,0:T(8,128)S(1)}, f32[2,16,128]{2,1,0:T(8,128)S(1)}, u32[]{:S(2)}, u32[]{:S(2)}) collective-permute-start(f32[2,16,128]{2,1,0:T(8,128)S(1)} %pad_maximum_fusion.2.after), channel_id=1, source_target_pairs={{0,4},{1,5},{2,6},{3,7},{4,0},{5,1},{6,2},{7,3},{8,12},{9,13},{10,... | collective-permute-start | bytes 49160 | tf_op jit(solution)/shard_map/ppermute | solution.py:687
  24.1 8.4 %collective-permute-start.6 = (f32[4,16,128]{2,1,0:T(8,128)S(1)}, f32[4,16,128]{2,1,0:T(8,128)S(1)}, u32[]{:S(2)}, u32[]{:S(2)}) collective-permute-start(f32[4,16,128]{2,1,0:T(8,128)S(1)} %pad_maximum_fusion.1.after), channel_id=1, source_target_pairs={{0,2},{1,3},{2,0},{3,1},{4,6},{5,7},{6,4},{7,5},{8,10},{9,11},{10,... | collective-permute-start | bytes 98312 | tf_op jit(solution)/shard_map/ppermute | solution.py:687
  32.5 1.3 %collective-permute-start.7 = (f32[8,16,128]{2,1,0:T(8,128)S(1)}, f32[8,16,128]{2,1,0:T(8,128)S(1)}, u32[]{:S(2)}, u32[]{:S(2)}) collective-permute-start(f32[8,16,128]{2,1,0:T(8,128)S(1)} %pad_maximum_fusion), channel_id=1, source_target_pairs={{0,1},{1,0},{2,3},{3,2},{4,5},{5,4},{6,7},{7,6},{8,9},{9,8},{10,11... | collective-permute-start | bytes 196616 | tf_op jit(solution)/shard_map/ppermute | solution.py:687

commit v6 on v5

--- a/solution.py
+++ b/solution.py
@@ -355,10 +355,14 @@
     slope_rim[...] = gelu_slope(mixed[...])
 
 
-def slope_kernel(after, mix, deep, pred, land, slope_mix, slope_deep, cells):
+def slope_kernel(after, mix, deep, slope_mix, slope_deep):
     del after
     slope_mix[...] = gelu_slope(mix[...])
     slope_deep[...] = gelu_slope(deep[...])
+
+
+def pred_kernel(after, pred, land, cells):
+    del after
     rows, cols = land.shape
     turned = pred[...].T
     wide = jnp.concatenate([turned[b * rows : (b + 1) * rows] for b in range(4)], axis=1)
@@ -666,13 +670,12 @@
     def slopes(after):
         return call(
             slope_kernel,
-            [
-                ((crows + 2, width, chan), F32),
-                ((crows, width, chan), F32),
-                ((rows, cols), F32),
-            ],
+            [((crows + 2, width, chan), F32), ((crows, width, chan), F32)],
             hbm=1,
-        )(after, pre_mix, pre_deep, pred, land_mask)
+        )(after, pre_mix, pre_deep)
+
+    def cells(after):
+        return call(pred_kernel, [((rows, cols), F32)], hbm=1)(after, pred, land_mask)
 
     def rim(side, after):
         return call(
@@ -687,14 +690,14 @@
         return lax.ppermute(x, ("tile", "band"), pairs)
 
     masks = hop_masks(bands, tiles)
-    beside = [slopes, functools.partial(rim, 0), functools.partial(rim, 1)]
+    beside = [slopes, lambda after: (rim(0, after), rim(1, after)), cells]
     made = []
     msgs = msg[None]
     for n, mask in enumerate(masks):
         if n < len(beside):
             made.append(beside[n](msgs))
         msgs = jnp.concatenate([msgs, send(msgs, mask)], axis=0)
-    (slope_mix, slope_deep, cell_pred), (rim_above,), (rim_below,) = made
+    (slope_mix, slope_deep), ((rim_above,), (rim_below,)), (cell_pred,) = made
 
     height = ndev * share_rows
     mean, loss, grad = call(

time: 37.8 us -> 37.8 us (level)
    pallas_call x10 -> x11, Pallas kernels: 11.7 us -> 11.5 us  [run(): pl.pallas_call(kernel, out_shape=[jax.ShapeDtypeStruct(s, d) for s, d in...]
where the time goes in v6:
time: 37.8 us; the launch traced here: 37.5 us
  starting transfers between devices  17.8 us (47%)
  Pallas kernels  11.5 us (30%)
  waiting for transfers between devices  6.44 us (17%)
  between operations  0.84 us (2%)
  local copies, waits for them, and re-layouts  0.81 us (2%)
    pallas_call x11, Pallas kernels, run(): pl.pallas_call(kernel, out_shape=[jax.ShapeDtypeStruct(s, d) for s, d in...  11.5 us
    ppermute x4, starting transfers between devices, send(): return lax.ppermute(x, ('tile', 'band'), pairs)  10.5 us
    ppermute x4, starting transfers between devices, exchange(): lax.ppermute(message(), axis, pairs + [(j, i) for i, j in pairs])  7.33 us
    ppermute x4, waiting for transfers between devices, send(): return lax.ppermute(x, ('tile', 'band'), pairs)  5.34 us
    ppermute x4, waiting for transfers between devices, exchange(): lax.ppermute(message(), axis, pairs + [(j, i) for i, j in pairs])  1.1 us
  transfers between devices with their start and end apart: 8, of which 5 were waited for; matrix products, arithmetic and copies ran while one was open for 1% of the time, Pallas kernels for 8%

profile of v6, /device:TPU:0, one launch (start us, length us, event | category | flops | bytes accessed | tf_op | source)
XLA Modules:
  0.0 37.5 jit_solution(14792020935531532306)
XLA Ops:
  0.6 2.8 %shard_map.129 = (f32[512,256]{1,0:T(8,128)S(1)}, bf16[8,64,256]{2,1,0:T(8,128)(2,1)S(1)}, f32[64,128]{1,0:T(8,128)S(1)}, bf16[288,256]{1,0:T(8,128)(2,1)S(1)}, bf16[512,256]{1,0:T(8,128)(2,1)S(1)}) custom-call(bf16[32,24,256]{2,1,0:T(8,128)(2,1)} %bitcast.40, bf16[384,256]{1,0:T(8,128)(2,1)} %w_hbm.1, s32[32,256]{1,0:T(8,128)} %land.1, s32[81,1,128]{2,1,0:T(1,128)} %bitcast.42), custom_call_target="tpu_custom_call" | custom-call | flops 1000000 | bytes 1000000 | tf_op jit(solution)/shard_map/pallas_call | solution.py:556
  3.4 0.0 copy-start.4
  3.5 0.0 copy-start.6
  3.5 0.5 %collective-permute-start = (bf16[288,256]{1,0:T(8,128)(2,1)S(1)}, bf16[288,256]{1,0:T(8,128)(2,1)S(1)}, u32[]{:S(2)}, u32[]{:S(2)}) collective-permute-start(bf16[288,256]{1,0:T(8,128)(2,1)S(1)} %shard_map.130), channel_id=1, source_target_pairs={{0,1},{2,3},{1,0},{3,2},{4,5},{6,7},{5,4},{7,6},{8,9},{10,11},{9,8... | collective-permute-start | bytes 442376 | tf_op jit(solution)/shard_map/ppermute | solution.py:583
  4.0 0.7 %collective-permute-start.1 = (bf16[288,256]{1,0:T(8,128)(2,1)S(1)}, bf16[288,256]{1,0:T(8,128)(2,1)S(1)}, u32[]{:S(2)}, u32[]{:S(2)}) collective-permute-start(bf16[288,256]{1,0:T(8,128)(2,1)S(1)} %get-tuple-element.24), channel_id=1, source_target_pairs={{1,2},{2,1},{5,6},{6,5},{9,10},{10,9},{13,14},{14,13},{17,18},{18,... | collective-permute-start | bytes 442376 | tf_op jit(solution)/shard_map/ppermute | solution.py:583
  4.8 0.6 %copy-done.5 = f32[880]{0:T(1024)S(1)} copy-done((f32[880]{0:T(1024)S(1)}, f32[880]{0:T(1024)}, u32[]{:S(2)}) %copy-start.5) | copy-done | bytes 3544
  5.5 0.7 %collective-permute-start.3 = (bf16[80,256]{1,0:T(8,128)(2,1)S(1)}, bf16[80,256]{1,0:T(8,128)(2,1)S(1)}, u32[]{:S(2)}, u32[]{:S(2)}) collective-permute-start(bf16[80,256]{1,0:T(8,128)(2,1)S(1)} %shard_map.132), channel_id=1, source_target_pairs={{4,8},{8,4},{5,9},{9,5},{6,10},{10,6},{7,11},{11,7},{20,24},{24,20... | collective-permute-start | bytes 122888 | tf_op jit(solution)/shard_map/ppermute | solution.py:583
  6.2 5.5 %collective-permute-start.2 = (bf16[80,256]{1,0:T(8,128)(2,1)S(1)}, bf16[80,256]{1,0:T(8,128)(2,1)S(1)}, u32[]{:S(2)}, u32[]{:S(2)}) collective-permute-start(bf16[80,256]{1,0:T(8,128)(2,1)S(1)} %shard_map.131), channel_id=1, source_target_pairs={{0,4},{8,12},{4,0},{12,8},{1,5},{9,13},{5,1},{13,9},{2,6},{10,14},... | collective-permute-start | bytes 122888 | tf_op jit(solution)/shard_map/ppermute | solution.py:583
  11.7 0.1 pad_convert_fusion
  11.9 0.6 %shard_map.133 = (f32[512,256]{1,0:T(8,128)S(1)}, f32[16,128]{1,0:T(8,128)S(1)}) custom-call(f32[512,256]{1,0:T(8,128)S(1)} %get-tuple-element.25.pre_first, f32[64,128]{1,0:T(8,128)S(1)} %get-tuple-element.23.bm, f32[16,128]{1,0:T(8,128)S(1)} %concatenate.22.msg_in), custom_call_target="tpu_custom_call" | custom-call | flops 1000000 | bytes 1000000 | tf_op jit(solution)/shard_map/pallas_call | solution.py:556
  12.6 1.1 %collective-permute-done.2.t1 = bf16[80,256]{1,0:T(8,128)(2,1)S(1)} collective-permute-done((bf16[80,256]{1,0:T(8,128)(2,1)S(1)}, bf16[80,256]{1,0:T(8,128)(2,1)S(1)}, u32[]{:S(2)}, u32[]{:S(2)}) %collective-permute-start.2) | collective-permute-done | bytes 40992 | tf_op jit(solution)/shard_map/ppermute | solution.py:583
  13.7 2.0 %shard_map.134 = (f32[12,72,256]{2,1,0:T(8,128)S(1)}, f32[10,72,256]{2,1,0:T(8,128)S(1)}, f32[10,72,256]{2,1,0:T(8,128)S(1)}, f32[8,72,256]{2,1,0:T(8,128)S(1)},...) custom-call(bf16[8,64,256]{2,1,0:T(8,128)(2,1)S(1)} %get-tuple-element.22.act, f32[64,128]{1,0:T(8,128)S(1)} %get-tuple-element.23.bm, ...), custom_call_target="tpu_custom_call" | custom-call | flops 1000000 | bytes 1000000 | tf_op jit(solution)/shard_map/pallas_call | solution.py:556
  15.7 2.0 %collective-permute-start.4 = (f32[1,16,128]{2,1,0:T(8,128)S(1)}, f32[1,16,128]{2,1,0:T(8,128)S(1)}, u32[]{:S(2)}, u32[]{:S(2)}) collective-permute-start(f32[1,16,128]{2,1,0:T(8,128)S(1)} %bitcast.35), channel_id=1, source_target_pairs={{0,8},{1,9},{2,10},{3,11},{4,12},{5,13},{6,14},{7,15},{8,0},{9,1},... | collective-permute-start | bytes 24584 | tf_op jit(solution)/shard_map/ppermute | solution.py:690
  17.6 0.5 %shard_map.136 = (f32[10,72,256]{2,1,0:T(8,128)S(1)}, f32[8,72,256]{2,1,0:T(8,128)S(1)}) custom-call(f32[1,16,128]{2,1,0:T(8,128)S(1)} %bitcast.36, f32[10,72,256]{2,1,0:T(8,128)S(1)} %get-tuple-element.29.mix, f32[8,72,256]{2,1,0:T(8,128)S(1)} %get-tuple-element.30.deep), custom_call_target="tpu_custom_call" | custom-call | flops 1000000 | bytes 1000000 | tf_op jit(solution)/shard_map/pallas_call | solution.py:556
  18.1 2.2 %collective-permute-done.4 = f32[1,16,128]{2,1,0:T(8,128)S(1)} collective-permute-done((f32[1,16,128]{2,1,0:T(8,128)S(1)}, f32[1,16,128]{2,1,0:T(8,128)S(1)}, u32[]{:S(2)}, u32[]{:S(2)}) %collective-permute-start.4) | collective-permute-done | bytes 8224 | tf_op jit(solution)/shard_map/ppermute | solution.py:690
  20.3 2.0 %collective-permute-start.5 = (f32[2,16,128]{2,1,0:T(8,128)S(1)}, f32[2,16,128]{2,1,0:T(8,128)S(1)}, u32[]{:S(2)}, u32[]{:S(2)}) collective-permute-start(f32[2,16,128]{2,1,0:T(8,128)S(1)} %pad_maximum_fusion.2.after), channel_id=1, source_target_pairs={{0,4},{1,5},{2,6},{3,7},{4,0},{5,1},{6,2},{7,3},{8,12},{9,13},{10,... | collective-permute-start | bytes 49160 | tf_op jit(solution)/shard_map/ppermute | solution.py:690
  22.3 0.4 %shard_map.138.rim_below = f32[2,72,256]{2,1,0:T(8,128)S(1)} custom-call(f32[2,16,128]{2,1,0:T(8,128)S(1)} %pad_maximum_fusion.2.after, bf16[8,64,256]{2,1,0:T(8,128)(2,1)S(1)} %get-tuple-element.22.act, bf16[288,256]{1,0:T(8,128)(2,1)S(1)} %collective-permute-done.p1, bf16[288,256]{1,0:T(8,128)(2,1)S(1)} %collective-permute-done.1.p2, ...), custom_call_target="tpu_custom_call" | custom-call | flops 1000000 | bytes 1000000 | tf_op jit(solution)/shard_map/pallas_call | solution.py:556
  22.7 0.4 %shard_map.137.rim_above = f32[2,72,256]{2,1,0:T(8,128)S(1)} custom-call(f32[2,16,128]{2,1,0:T(8,128)S(1)} %pad_maximum_fusion.2.after, bf16[8,64,256]{2,1,0:T(8,128)(2,1)S(1)} %get-tuple-element.22.act, bf16[288,256]{1,0:T(8,128)(2,1)S(1)} %collective-permute-done.p1, bf16[288,256]{1,0:T(8,128)(2,1)S(1)} %collective-permute-done.1.p2, ...), custom_call_target="tpu_custom_call" | custom-call | flops 1000000 | bytes 1000000 | tf_op jit(solution)/shard_map/pallas_call | solution.py:556
  23.1 1.0 %collective-permute-done.5 = f32[2,16,128]{2,1,0:T(8,128)S(1)} collective-permute-done((f32[2,16,128]{2,1,0:T(8,128)S(1)}, f32[2,16,128]{2,1,0:T(8,128)S(1)}, u32[]{:S(2)}, u32[]{:S(2)}) %collective-permute-start.5) | collective-permute-done | bytes 16416 | tf_op jit(solution)/shard_map/ppermute | solution.py:690
  24.1 6.5 %collective-permute-start.6 = (f32[4,16,128]{2,1,0:T(8,128)S(1)}, f32[4,16,128]{2,1,0:T(8,128)S(1)}, u32[]{:S(2)}, u32[]{:S(2)}) collective-permute-start(f32[4,16,128]{2,1,0:T(8,128)S(1)} %pad_maximum_fusion.1.after), channel_id=1, source_target_pairs={{0,2},{1,3},{2,0},{3,1},{4,6},{5,7},{6,4},{7,5},{8,10},{9,11},{10,... | collective-permute-start | bytes 98312 | tf_op jit(solution)/shard_map/ppermute | solution.py:690
  30.6 0.9 %shard_map.135 = f32[32,256]{1,0:T(8,128)} custom-call(f32[4,16,128]{2,1,0:T(8,128)S(1)} %pad_maximum_fusion.1.after, f32[64,128]{1,0:T(8,128)S(1)} %get-tuple-element.28.pred, s32[32,256]{1,0:T(8,128)S(1)} %copy-done.3), custom_call_target="tpu_custom_call" | custom-call | flops 1000000 | bytes 1000000 | tf_op jit(solution)/shard_map/pallas_call | solution.py:556
  31.5 1.0 %collective-permute-done.6 = f32[4,16,128]{2,1,0:T(8,128)S(1)} collective-permute-done((f32[4,16,128]{2,1,0:T(8,128)S(1)}, f32[4,16,128]{2,1,0:T(8,128)S(1)}, u32[]{:S(2)}, u32[]{:S(2)}) %collective-permute-start.6) | collective-permute-done | bytes 32800 | tf_op jit(solution)/shard_map/ppermute | solution.py:690
  32.5 1.2 %collective-permute-done.7 = f32[8,16,128]{2,1,0:T(8,128)S(1)} collective-permute-done((f32[8,16,128]{2,1,0:T(8,128)S(1)}, f32[8,16,128]{2,1,0:T(8,128)S(1)}, u32[]{:S(2)}, u32[]{:S(2)}) %collective-permute-start.7) | collective-permute-done | bytes 65568 | tf_op jit(solution)/shard_map/ppermute | solution.py:690
  33.8 3.8 %shard_map.139 = (f32[8,128]{1,0:T(8,128)}, f32[1,1]{1,0:T(1,128)}, bf16[32,24,256]{2,1,0:T(8,128)(2,1)}) custom-call(f32[16,16,128]{2,1,0:T(8,128)S(1)} %constant_dynamic-update-slice_fusion.gathered, f32[64,128]{1,0:T(8,128)S(1)} %get-tuple-element.23.bm, bf16[288,256]{1,0:T(8,128)(2,1)S(1)} %collective-permute-done.p1, ...), custom_call_target="tpu_custom_call" | custom-call | flops 1000000 | bytes 1000000 | tf_op jit(solution)/shard_map/pallas_call | solution.py:556
  (37 shorter events, 0.3 us)
Async XLA Ops:
  3.4 1.3 %copy-start.4 = (bf16[256,16]{0,1:T(8,128)(2,1)S(1)}, bf16[256,16]{0,1:T(8,128)(2,1)}, u32[]{:S(2)}) copy-start(bf16[256,16]{0,1:T(8,128)(2,1)} %param.19) | copy-start | bytes 24580
  3.5 1.2 %copy-start.6 = (s32[1,1,81]{2,1,0:T(1,128)S(1)}, s32[1,1,81]{2,1,0:T(1,128)}, u32[]{:S(2)}) copy-start(s32[1,1,81]{2,1,0:T(1,128)} %param.13) | copy-start | bytes 976
  3.5 1.9 %collective-permute-start = (bf16[288,256]{1,0:T(8,128)(2,1)S(1)}, bf16[288,256]{1,0:T(8,128)(2,1)S(1)}, u32[]{:S(2)}, u32[]{:S(2)}) collective-permute-start(bf16[288,256]{1,0:T(8,128)(2,1)S(1)} %shard_map.130), channel_id=1, source_target_pairs={{0,1},{2,3},{1,0},{3,2},{4,5},{6,7},{5,4},{7,6},{8,9},{10,11},{9,8... | collective-permute-start | bytes 442376 | tf_op jit(solution)/shard_map/ppermute | solution.py:583
  4.0 1.4 %collective-permute-start.1 = (bf16[288,256]{1,0:T(8,128)(2,1)S(1)}, bf16[288,256]{1,0:T(8,128)(2,1)S(1)}, u32[]{:S(2)}, u32[]{:S(2)}) collective-permute-start(bf16[288,256]{1,0:T(8,128)(2,1)S(1)} %get-tuple-element.24), channel_id=1, source_target_pairs={{1,2},{2,1},{5,6},{6,5},{9,10},{10,9},{13,14},{14,13},{17,18},{18,... | collective-permute-start | bytes 442376 | tf_op jit(solution)/shard_map/ppermute | solution.py:583
  4.7 0.7 %copy-start.5 = (f32[880]{0:T(1024)S(1)}, f32[880]{0:T(1024)}, u32[]{:S(2)}) copy-start(f32[880]{0:T(1024)} %param.14) | copy-start | bytes 10564
  5.5 7.1 %collective-permute-start.3 = (bf16[80,256]{1,0:T(8,128)(2,1)S(1)}, bf16[80,256]{1,0:T(8,128)(2,1)S(1)}, u32[]{:S(2)}, u32[]{:S(2)}) collective-permute-start(bf16[80,256]{1,0:T(8,128)(2,1)S(1)} %shard_map.132), channel_id=1, source_target_pairs={{4,8},{8,4},{5,9},{9,5},{6,10},{10,6},{7,11},{11,7},{20,24},{24,20... | collective-permute-start | bytes 122888 | tf_op jit(solution)/shard_map/ppermute | solution.py:583
  6.2 7.5 %collective-permute-start.2 = (bf16[80,256]{1,0:T(8,128)(2,1)S(1)}, bf16[80,256]{1,0:T(8,128)(2,1)S(1)}, u32[]{:S(2)}, u32[]{:S(2)}) collective-permute-start(bf16[80,256]{1,0:T(8,128)(2,1)S(1)} %shard_map.131), channel_id=1, source_target_pairs={{0,4},{8,12},{4,0},{12,8},{1,5},{9,13},{5,1},{13,9},{2,6},{10,14},... | collective-permute-start | bytes 122888 | tf_op jit(solution)/shard_map/ppermute | solution.py:583
  11.9 1.8 %copy-start = (bf16[256,256]{1,0:T(8,128)(2,1)S(1)}, bf16[256,256]{1,0:T(8,128)(2,1)}, u32[]{:S(2)}) copy-start(bf16[256,256]{1,0:T(8,128)(2,1)} %w_mix.7) | copy-start | bytes 393220
  11.9 1.8 %copy-start.1 = (bf16[9,256]{1,0:T(8,128)(2,1)S(1)}, bf16[9,256]{1,0:T(8,128)(2,1)}, u32[]{:S(2)}) copy-start(bf16[9,256]{1,0:T(8,128)(2,1)} %k_first.7) | copy-start | bytes 13828
  11.9 1.7 %copy-start.2 = (bf16[9,256]{1,0:T(8,128)(2,1)S(1)}, bf16[9,256]{1,0:T(8,128)(2,1)}, u32[]{:S(2)}) copy-start(bf16[9,256]{1,0:T(8,128)(2,1)} %k_deep.7) | copy-start | bytes 13828
  15.7 4.6 %collective-permute-start.4 = (f32[1,16,128]{2,1,0:T(8,128)S(1)}, f32[1,16,128]{2,1,0:T(8,128)S(1)}, u32[]{:S(2)}, u32[]{:S(2)}) collective-permute-start(f32[1,16,128]{2,1,0:T(8,128)S(1)} %bitcast.35), channel_id=1, source_target_pairs={{0,8},{1,9},{2,10},{3,11},{4,12},{5,13},{6,14},{7,15},{8,0},{9,1},... | collective-permute-start | bytes 24584 | tf_op jit(solution)/shard_map/ppermute | solution.py:690
  20.3 3.8 %collective-permute-start.5 = (f32[2,16,128]{2,1,0:T(8,128)S(1)}, f32[2,16,128]{2,1,0:T(8,128)S(1)}, u32[]{:S(2)}, u32[]{:S(2)}) collective-permute-start(f32[2,16,128]{2,1,0:T(8,128)S(1)} %pad_maximum_fusion.2.after), channel_id=1, source_target_pairs={{0,4},{1,5},{2,6},{3,7},{4,0},{5,1},{6,2},{7,3},{8,12},{9,13},{10,... | collective-permute-start | bytes 49160 | tf_op jit(solution)/shard_map/ppermute | solution.py:690
  24.1 6.5 %copy-start.3 = (s32[32,256]{1,0:T(8,128)S(1)}, s32[32,256]{1,0:T(8,128)}, u32[]{:S(2)}) copy-start(s32[32,256]{1,0:T(8,128)} %land.1) | copy-start | bytes 98308
  24.1 8.4 %collective-permute-start.6 = (f32[4,16,128]{2,1,0:T(8,128)S(1)}, f32[4,16,128]{2,1,0:T(8,128)S(1)}, u32[]{:S(2)}, u32[]{:S(2)}) collective-permute-start(f32[4,16,128]{2,1,0:T(8,128)S(1)} %pad_maximum_fusion.1.after), channel_id=1, source_target_pairs={{0,2},{1,3},{2,0},{3,1},{4,6},{5,7},{6,4},{7,5},{8,10},{9,11},{10,... | collective-permute-start | bytes 98312 | tf_op jit(solution)/shard_map/ppermute | solution.py:690
  32.5 1.3 %collective-permute-start.7 = (f32[8,16,128]{2,1,0:T(8,128)S(1)}, f32[8,16,128]{2,1,0:T(8,128)S(1)}, u32[]{:S(2)}, u32[]{:S(2)}) collective-permute-start(f32[8,16,128]{2,1,0:T(8,128)S(1)} %pad_maximum_fusion), channel_id=1, source_target_pairs={{0,1},{1,0},{2,3},{3,2},{4,5},{5,4},{6,7},{7,6},{8,9},{9,8},{10,11... | collective-permute-start | bytes 196616 | tf_op jit(solution)/shard_map/ppermute | solution.py:690

commit v7 on v5

--- a/solution.py
+++ b/solution.py
@@ -300,7 +300,7 @@
     for j in range(ccols):
         sums = sums + jnp.where(maps[j : j + 1, :] == slots, pred[j : j + 1, :], 0.0)
     msg_out[...] = msg_in[...]
-    msg_out[0:1, :] = across_lanes(sums)
+    msg_out[0] = across_lanes(sums)
 
 
 def across_lanes(acc):
@@ -318,7 +318,7 @@
     for j in range(maps.shape[0]):
         counts = counts + jnp.where(maps[j : j + 1, :] == slots, 1.0, 0.0)
     msg_out[...] = msg_in[...]
-    msg_out[1:2, :] = across_lanes(counts)
+    msg_out[1] = across_lanes(counts)
 
 
 def rim_kernel(
@@ -396,7 +396,7 @@
 
     height = ndev * share_rows
     chunk = min(16, ndev)
-    first_target = gathered.shape[1] - share_rows
+    target_rows = gathered.shape[1] - 4
     sub = iota((height, LANES), 0).astype(F32).astype(BF16)
     sub_lo = iota((LANES, LANES), 0).astype(F32).astype(BF16)
     one, none = jnp.ones((), BF16), jnp.zeros((), BF16)
@@ -406,16 +406,17 @@
         for o in range(chunk):
             owner = c * chunk + o
             m = gathered[slot_at(owner)]
-            hot_hi.append(jnp.where(sub == m[2:3].astype(BF16), one, none))
-            low_hit = sub_lo == m[3:4].astype(BF16)
-            high = rounded(m[0:1])
-            parts = [high, m[0:1] - high, m[1:2]]
+            hot_hi.append(jnp.where(sub == m[2].astype(BF16), one, none))
+            low_hit = sub_lo == m[3].astype(BF16)
+            high = rounded(m[0])
+            parts = [high, m[0] - high, m[1]]
             hot_lo.append(
                 jnp.concatenate(
                     [jnp.where(low_hit, part.astype(BF16), none) for part in parts], axis=0
                 )
             )
-            targets[pl.ds(owner * share_rows, share_rows)] = m[first_target:]
+            for n in range(target_rows):
+                targets[pl.ds(owner * share_rows + n, 1)] = m[4 + n]
         return acc + dot_nt(
             jnp.concatenate(hot_hi, axis=1), jnp.concatenate(hot_lo, axis=1)
         )
@@ -445,8 +446,8 @@
 
     def block_grads(slot):
         m = gathered[slot]
-        low = jnp.broadcast_to(jnp.maximum(m[3:4], 0.0), (8, LANES)).astype(jnp.int32)
-        high = m[2:3]
+        low = jnp.broadcast_to(jnp.maximum(m[3], 0.0), (8, LANES)).astype(jnp.int32)
+        high = m[2]
         total = jnp.zeros((8, LANES), F32)
         for at in range(0, height, 8):
             found = jnp.take_along_axis(grads[at : at + 8], low, axis=1)
@@ -593,7 +594,8 @@
     ndev = bands * tiles
     share = targets.shape[0]
     share_rows = pl.next_power_of_2(pl.cdiv(share, LANES))
-    msg_rows = pl.cdiv(4 + share_rows, 8) * 8
+    target_rows = pl.cdiv(share, LANES)
+    msg_rows = 4 + target_rows
 
     rid = region_ids.reshape(1, nblk)
     owner, place = rid // share, rid % share
@@ -601,12 +603,10 @@
     high = jnp.pad(owner * share_rows + place // LANES, pad, constant_values=-1)
     low = jnp.pad(place % LANES, pad, constant_values=-1)
     blank = jnp.zeros((1, LANES), F32)
-    tgt = jnp.pad(targets, (0, share_rows * LANES - share)).reshape(share_rows, LANES)
+    tgt = jnp.pad(targets, (0, target_rows * LANES - share)).reshape(target_rows, LANES)
     msg_in = jnp.concatenate(
-        [blank, blank, high.astype(F32), low.astype(F32)]
-        + [jnp.zeros((msg_rows - 4 - share_rows, LANES), F32), tgt],
-        axis=0,
-    )
+        [blank, blank, high.astype(F32), low.astype(F32), tgt], axis=0
+    ).reshape(msg_rows, 1, LANES)
     head = w_head.T.reshape(4, 4, chan).transpose(1, 0, 2).astype(F32)
     wall = jnp.broadcast_to(head[:, None], (4, crows, 4, chan)).reshape(16 * crows, chan)
 
@@ -647,7 +647,7 @@
 
     t1, t2 = exchange(lambda: edges(False), lambda: edges(True), "tile")
     slope_first, msg_in = call(
-        count_kernel, [((crows * ccols, chan), F32), ((msg_rows, LANES), F32)]
+        count_kernel, [((crows * ccols, chan), F32), ((msg_rows, 1, LANES), F32)]
     )(pre_first, bm, msg_in)
     nrow = crows + 2 * HALO
     field, act_mix, pre_mix, pre_deep, pred, msg = call(
@@ -658,7 +658,7 @@
             ((crows + 2, width, chan), F32),
             ((crows, width, chan), F32),
             ((ccols, LANES), F32),
-            ((msg_rows, LANES), F32),
+            ((msg_rows, 1, LANES), F32),
         ],
         [((crows + 2, width, chan), F32)],
     )(act, bm, p1, p2, t1, t2, w_mix, k_first, k_deep, wall, msg_in)

time: 37.8 us -> 37.8 us (level)
  no operation moved by 1% of the time
where the time goes in v7:
time: 37.8 us; the launch traced here: 37.6 us
  starting transfers between devices  18 us (48%)
  Pallas kernels  11.8 us (31%)
  waiting for transfers between devices  5.95 us (16%)
  between operations  0.84 us (2%)
  local copies, waits for them, and re-layouts  0.78 us (2%)
    pallas_call x10, Pallas kernels, run(): pl.pallas_call(kernel, out_shape=[jax.ShapeDtypeStruct(s, d) for s, d in...  11.8 us
    ppermute x4, starting transfers between devices, send(): return lax.ppermute(x, ('tile', 'band'), pairs)  10.7 us
    ppermute x4, starting transfers between devices, exchange(): lax.ppermute(message(), axis, pairs + [(j, i) for i, j in pairs])  7.33 us
    ppermute x4, waiting for transfers between devices, send(): return lax.ppermute(x, ('tile', 'band'), pairs)  4.82 us
    ppermute x4, waiting for transfers between devices, exchange(): lax.ppermute(message(), axis, pairs + [(j, i) for i, j in pairs])  1.13 us
  transfers between devices with their start and end apart: 8, of which 5 were waited for; matrix products, arithmetic and copies ran while one was open for 1% of the time, Pallas kernels for 8%

profile of v7, /device:TPU:0, one launch (start us, length us, event | category | flops | bytes accessed | tf_op | source)
XLA Modules:
  0.0 37.6 jit_solution(6736736018668236010)
XLA Ops:
  0.6 2.8 %shard_map.129 = (f32[512,256]{1,0:T(8,128)S(1)}, bf16[8,64,256]{2,1,0:T(8,128)(2,1)S(1)}, f32[64,128]{1,0:T(8,128)S(1)}, bf16[288,256]{1,0:T(8,128)(2,1)S(1)}, bf16[512,256]{1,0:T(8,128)(2,1)S(1)}) custom-call(bf16[32,24,256]{2,1,0:T(8,128)(2,1)} %bitcast.40, bf16[384,256]{1,0:T(8,128)(2,1)} %w_hbm.1, s32[32,256]{1,0:T(8,128)} %land.1, s32[81,1,128]{2,1,0:T(1,128)} %bitcast.42), custom_call_target="tpu_custom_call" | custom-call | flops 1000000 | bytes 1000000 | tf_op jit(solution)/shard_map/pallas_call | solution.py:553
  3.4 0.0 copy-start.4
  3.5 0.5 %collective-permute-start = (bf16[288,256]{1,0:T(8,128)(2,1)S(1)}, bf16[288,256]{1,0:T(8,128)(2,1)S(1)}, u32[]{:S(2)}, u32[]{:S(2)}) collective-permute-start(bf16[288,256]{1,0:T(8,128)(2,1)S(1)} %shard_map.130), channel_id=1, source_target_pairs={{0,1},{2,3},{1,0},{3,2},{4,5},{6,7},{5,4},{7,6},{8,9},{10,11},{9,8... | collective-permute-start | bytes 442376 | tf_op jit(solution)/shard_map/ppermute | solution.py:580
  4.0 0.7 %collective-permute-start.1 = (bf16[288,256]{1,0:T(8,128)(2,1)S(1)}, bf16[288,256]{1,0:T(8,128)(2,1)S(1)}, u32[]{:S(2)}, u32[]{:S(2)}) collective-permute-start(bf16[288,256]{1,0:T(8,128)(2,1)S(1)} %get-tuple-element.25), channel_id=1, source_target_pairs={{1,2},{2,1},{5,6},{6,5},{9,10},{10,9},{13,14},{14,13},{17,18},{18,... | collective-permute-start | bytes 442376 | tf_op jit(solution)/shard_map/ppermute | solution.py:580
  4.7 0.1 pad_convert_fusion
  4.8 0.6 %copy-done.5 = f32[880]{0:T(1024)S(1)} copy-done((f32[880]{0:T(1024)S(1)}, f32[880]{0:T(1024)}, u32[]{:S(2)}) %copy-start.5) | copy-done | bytes 3544
  5.5 0.7 %collective-permute-start.3 = (bf16[80,256]{1,0:T(8,128)(2,1)S(1)}, bf16[80,256]{1,0:T(8,128)(2,1)S(1)}, u32[]{:S(2)}, u32[]{:S(2)}) collective-permute-start(bf16[80,256]{1,0:T(8,128)(2,1)S(1)} %shard_map.132), channel_id=1, source_target_pairs={{4,8},{8,4},{5,9},{9,5},{6,10},{10,6},{7,11},{11,7},{20,24},{24,20... | collective-permute-start | bytes 122888 | tf_op jit(solution)/shard_map/ppermute | solution.py:580
  6.2 5.5 %collective-permute-start.2 = (bf16[80,256]{1,0:T(8,128)(2,1)S(1)}, bf16[80,256]{1,0:T(8,128)(2,1)S(1)}, u32[]{:S(2)}, u32[]{:S(2)}) collective-permute-start(bf16[80,256]{1,0:T(8,128)(2,1)S(1)} %shard_map.131), channel_id=1, source_target_pairs={{0,4},{8,12},{4,0},{12,8},{1,5},{9,13},{5,1},{13,9},{2,6},{10,14},... | collective-permute-start | bytes 122888 | tf_op jit(solution)/shard_map/ppermute | solution.py:580
  11.7 0.1 pad_maximum_fusion.3
  11.9 0.6 %shard_map.133 = (f32[512,256]{1,0:T(8,128)S(1)}, f32[11,1,128]{2,1,0:T(1,128)S(1)}) custom-call(f32[512,256]{1,0:T(8,128)S(1)} %get-tuple-element.26.pre_first, f32[64,128]{1,0:T(8,128)S(1)} %get-tuple-element.24.bm, f32[11,1,128]{2,1,0:T(1,128)S(1)} %reshape.220.msg_in), custom_call_target="tpu_custom_call" | custom-call | flops 1000000 | bytes 1000000 | tf_op jit(solution)/shard_map/pallas_call | solution.py:553
  12.5 1.1 %collective-permute-done.2.t1 = bf16[80,256]{1,0:T(8,128)(2,1)S(1)} collective-permute-done((bf16[80,256]{1,0:T(8,128)(2,1)S(1)}, bf16[80,256]{1,0:T(8,128)(2,1)S(1)}, u32[]{:S(2)}, u32[]{:S(2)}) %collective-permute-start.2) | collective-permute-done | bytes 40992 | tf_op jit(solution)/shard_map/ppermute | solution.py:580
  13.7 2.0 %shard_map.134 = (f32[12,72,256]{2,1,0:T(8,128)S(1)}, f32[10,72,256]{2,1,0:T(8,128)S(1)}, f32[10,72,256]{2,1,0:T(8,128)S(1)}, f32[8,72,256]{2,1,0:T(8,128)S(1)},...) custom-call(bf16[8,64,256]{2,1,0:T(8,128)(2,1)S(1)} %get-tuple-element.23.act, f32[64,128]{1,0:T(8,128)S(1)} %get-tuple-element.24.bm, ...), custom_call_target="tpu_custom_call" | custom-call | flops 1000000 | bytes 1000000 | tf_op jit(solution)/shard_map/pallas_call | solution.py:553
  15.7 2.0 %collective-permute-start.4 = (f32[1,11,1,128]{3,2,1,0:T(1,128)S(1)}, f32[1,11,1,128]{3,2,1,0:T(1,128)S(1)}, u32[]{:S(2)}, u32[]{:S(2)}) collective-permute-start(f32[1,11,1,128]{3,2,1,0:T(1,128)S(1)} %bitcast.35), channel_id=1, source_target_pairs={{0,8},{1,9},{2,10},{3,11},{4,12},{5,13},{6,14},{7,15},{8,0},{9,1},... | collective-permute-start | bytes 16904 | tf_op jit(solution)/shard_map/ppermute | solution.py:687
  17.7 1.6 %shard_map.135 = (f32[10,72,256]{2,1,0:T(8,128)S(1)}, f32[8,72,256]{2,1,0:T(8,128)S(1)}, f32[32,256]{1,0:T(8,128)}) custom-call(f32[1,11,1,128]{3,2,1,0:T(1,128)S(1)} %bitcast.36, f32[10,72,256]{2,1,0:T(8,128)S(1)} %get-tuple-element.29.mix, f32[8,72,256]{2,1,0:T(8,128)S(1)} %get-tuple-element.30.deep, f32[64,128]{1,0:T(8,128)S(1)} %get-tuple-element.31.pred, ...), custom_call_target="tpu_custom_call" | custom-call | flops 1000000 | bytes 1000000 | tf_op jit(solution)/shard_map/pallas_call | solution.py:553
  19.3 1.0 %collective-permute-done.4 = f32[1,11,1,128]{3,2,1,0:T(1,128)S(1)} collective-permute-done((f32[1,11,1,128]{3,2,1,0:T(1,128)S(1)}, f32[1,11,1,128]{3,2,1,0:T(1,128)S(1)}, u32[]{:S(2)}, u32[]{:S(2)}) %collective-permute-start.4) | collective-permute-done | bytes 5664 | tf_op jit(solution)/shard_map/ppermute | solution.py:687
  20.3 2.1 %collective-permute-start.5 = (f32[2,11,1,128]{3,2,1,0:T(1,128)S(1)}, f32[2,11,1,128]{3,2,1,0:T(1,128)S(1)}, u32[]{:S(2)}, u32[]{:S(2)}) collective-permute-start(f32[2,11,1,128]{3,2,1,0:T(1,128)S(1)} %pad_maximum_fusion.2.after), channel_id=1, source_target_pairs={{0,4},{1,5},{2,6},{3,7},{4,0},{5,1},{6,2},{7,3},{8,12},{9,13},{10,... | collective-permute-start | bytes 33800 | tf_op jit(solution)/shard_map/ppermute | solution.py:687
  22.4 0.4 %shard_map.136.rim_above = f32[2,72,256]{2,1,0:T(8,128)S(1)} custom-call(f32[2,11,1,128]{3,2,1,0:T(1,128)S(1)} %pad_maximum_fusion.2.after, bf16[8,64,256]{2,1,0:T(8,128)(2,1)S(1)} %get-tuple-element.23.act, bf16[288,256]{1,0:T(8,128)(2,1)S(1)} %collective-permute-done.p1, bf16[288,256]{1,0:T(8,128)(2,1)S(1)} %collective-permute-done.1.p2, ...), custom_call_target="tpu_custom_call" | custom-call | flops 1000000 | bytes 1000000 | tf_op jit(solution)/shard_map/pallas_call | solution.py:553
  22.8 1.3 %collective-permute-done.5 = f32[2,11,1,128]{3,2,1,0:T(1,128)S(1)} collective-permute-done((f32[2,11,1,128]{3,2,1,0:T(1,128)S(1)}, f32[2,11,1,128]{3,2,1,0:T(1,128)S(1)}, u32[]{:S(2)}, u32[]{:S(2)}) %collective-permute-start.5) | collective-permute-done | bytes 11296 | tf_op jit(solution)/shard_map/ppermute | solution.py:687
  24.1 6.5 %collective-permute-start.6 = (f32[4,11,1,128]{3,2,1,0:T(1,128)S(1)}, f32[4,11,1,128]{3,2,1,0:T(1,128)S(1)}, u32[]{:S(2)}, u32[]{:S(2)}) collective-permute-start(f32[4,11,1,128]{3,2,1,0:T(1,128)S(1)} %pad_maximum_fusion.1.after), channel_id=1, source_target_pairs={{0,2},{1,3},{2,0},{3,1},{4,6},{5,7},{6,4},{7,5},{8,10},{9,11},{10,... | collective-permute-start | bytes 67592 | tf_op jit(solution)/shard_map/ppermute | solution.py:687
  30.7 0.4 %shard_map.137.rim_below = f32[2,72,256]{2,1,0:T(8,128)S(1)} custom-call(f32[4,11,1,128]{3,2,1,0:T(1,128)S(1)} %pad_maximum_fusion.1.after, bf16[8,64,256]{2,1,0:T(8,128)(2,1)S(1)} %get-tuple-element.23.act, bf16[288,256]{1,0:T(8,128)(2,1)S(1)} %collective-permute-done.p1, bf16[288,256]{1,0:T(8,128)(2,1)S(1)} %collective-permute-done.1.p2, ...), custom_call_target="tpu_custom_call" | custom-call | flops 1000000 | bytes 1000000 | tf_op jit(solution)/shard_map/pallas_call | solution.py:553
  31.1 1.4 %collective-permute-done.6 = f32[4,11,1,128]{3,2,1,0:T(1,128)S(1)} collective-permute-done((f32[4,11,1,128]{3,2,1,0:T(1,128)S(1)}, f32[4,11,1,128]{3,2,1,0:T(1,128)S(1)}, u32[]{:S(2)}, u32[]{:S(2)}) %collective-permute-start.6) | collective-permute-done | bytes 22560 | tf_op jit(solution)/shard_map/ppermute | solution.py:687
  32.5 0.1 collective-permute-start.7
  32.6 1.2 %collective-permute-done.7 = f32[8,11,1,128]{3,2,1,0:T(1,128)S(1)} collective-permute-done((f32[8,11,1,128]{3,2,1,0:T(1,128)S(1)}, f32[8,11,1,128]{3,2,1,0:T(1,128)S(1)}, u32[]{:S(2)}, u32[]{:S(2)}) %collective-permute-start.7) | collective-permute-done | bytes 45088 | tf_op jit(solution)/shard_map/ppermute | solution.py:687
  33.8 3.8 %shard_map.138 = (f32[8,128]{1,0:T(8,128)}, f32[1,1]{1,0:T(1,128)}, bf16[32,24,256]{2,1,0:T(8,128)(2,1)}) custom-call(f32[16,11,1,128]{3,2,1,0:T(1,128)S(1)} %constant_dynamic-update-slice_fusion.gathered, f32[64,128]{1,0:T(8,128)S(1)} %get-tuple-element.24.bm, bf16[288,256]{1,0:T(8,128)(2,1)S(1)} %collective-permute-done.p1, ...), custom_call_target="tpu_custom_call" | custom-call | flops 1000000 | bytes 1000000 | tf_op jit(solution)/shard_map/pallas_call | solution.py:553
  (37 shorter events, 0.4 us)
Async XLA Ops:
  3.4 1.3 %copy-start.4 = (bf16[256,16]{0,1:T(8,128)(2,1)S(1)}, bf16[256,16]{0,1:T(8,128)(2,1)}, u32[]{:S(2)}) copy-start(bf16[256,16]{0,1:T(8,128)(2,1)} %param.19) | copy-start | bytes 24580
  3.5 1.2 %copy-start.6 = (s32[1,1,81]{2,1,0:T(1,128)S(1)}, s32[1,1,81]{2,1,0:T(1,128)}, u32[]{:S(2)}) copy-start(s32[1,1,81]{2,1,0:T(1,128)} %param.13) | copy-start | bytes 976
  3.5 2.0 %collective-permute-start = (bf16[288,256]{1,0:T(8,128)(2,1)S(1)}, bf16[288,256]{1,0:T(8,128)(2,1)S(1)}, u32[]{:S(2)}, u32[]{:S(2)}) collective-permute-start(bf16[288,256]{1,0:T(8,128)(2,1)S(1)} %shard_map.130), channel_id=1, source_target_pairs={{0,1},{2,3},{1,0},{3,2},{4,5},{6,7},{5,4},{7,6},{8,9},{10,11},{9,8... | collective-permute-start | bytes 442376 | tf_op jit(solution)/shard_map/ppermute | solution.py:580
  4.0 1.4 %collective-permute-start.1 = (bf16[288,256]{1,0:T(8,128)(2,1)S(1)}, bf16[288,256]{1,0:T(8,128)(2,1)S(1)}, u32[]{:S(2)}, u32[]{:S(2)}) collective-permute-start(bf16[288,256]{1,0:T(8,128)(2,1)S(1)} %get-tuple-element.25), channel_id=1, source_target_pairs={{1,2},{2,1},{5,6},{6,5},{9,10},{10,9},{13,14},{14,13},{17,18},{18,... | collective-permute-start | bytes 442376 | tf_op jit(solution)/shard_map/ppermute | solution.py:580
  4.7 0.7 %copy-start.5 = (f32[880]{0:T(1024)S(1)}, f32[880]{0:T(1024)}, u32[]{:S(2)}) copy-start(f32[880]{0:T(1024)} %param.14) | copy-start | bytes 10564
  5.5 7.1 %collective-permute-start.3 = (bf16[80,256]{1,0:T(8,128)(2,1)S(1)}, bf16[80,256]{1,0:T(8,128)(2,1)S(1)}, u32[]{:S(2)}, u32[]{:S(2)}) collective-permute-start(bf16[80,256]{1,0:T(8,128)(2,1)S(1)} %shard_map.132), channel_id=1, source_target_pairs={{4,8},{8,4},{5,9},{9,5},{6,10},{10,6},{7,11},{11,7},{20,24},{24,20... | collective-permute-start | bytes 122888 | tf_op jit(solution)/shard_map/ppermute | solution.py:580
  6.2 7.5 %collective-permute-start.2 = (bf16[80,256]{1,0:T(8,128)(2,1)S(1)}, bf16[80,256]{1,0:T(8,128)(2,1)S(1)}, u32[]{:S(2)}, u32[]{:S(2)}) collective-permute-start(bf16[80,256]{1,0:T(8,128)(2,1)S(1)} %shard_map.131), channel_id=1, source_target_pairs={{0,4},{8,12},{4,0},{12,8},{1,5},{9,13},{5,1},{13,9},{2,6},{10,14},... | collective-permute-start | bytes 122888 | tf_op jit(solution)/shard_map/ppermute | solution.py:580
  11.9 1.8 %copy-start = (bf16[256,256]{1,0:T(8,128)(2,1)S(1)}, bf16[256,256]{1,0:T(8,128)(2,1)}, u32[]{:S(2)}) copy-start(bf16[256,256]{1,0:T(8,128)(2,1)} %w_mix.7) | copy-start | bytes 393220
  11.9 1.8 %copy-start.1 = (bf16[9,256]{1,0:T(8,128)(2,1)S(1)}, bf16[9,256]{1,0:T(8,128)(2,1)}, u32[]{:S(2)}) copy-start(bf16[9,256]{1,0:T(8,128)(2,1)} %k_first.7) | copy-start | bytes 13828
  11.9 1.8 %copy-start.2 = (bf16[9,256]{1,0:T(8,128)(2,1)S(1)}, bf16[9,256]{1,0:T(8,128)(2,1)}, u32[]{:S(2)}) copy-start(bf16[9,256]{1,0:T(8,128)(2,1)} %k_deep.7) | copy-start | bytes 13828
  13.7 4.0 %copy-start.3 = (s32[32,256]{1,0:T(8,128)S(1)}, s32[32,256]{1,0:T(8,128)}, u32[]{:S(2)}) copy-start(s32[32,256]{1,0:T(8,128)} %land.1) | copy-start | bytes 98308
  15.7 4.6 %collective-permute-start.4 = (f32[1,11,1,128]{3,2,1,0:T(1,128)S(1)}, f32[1,11,1,128]{3,2,1,0:T(1,128)S(1)}, u32[]{:S(2)}, u32[]{:S(2)}) collective-permute-start(f32[1,11,1,128]{3,2,1,0:T(1,128)S(1)} %bitcast.35), channel_id=1, source_target_pairs={{0,8},{1,9},{2,10},{3,11},{4,12},{5,13},{6,14},{7,15},{8,0},{9,1},... | collective-permute-start | bytes 16904 | tf_op jit(solution)/shard_map/ppermute | solution.py:687
  20.3 3.8 %collective-permute-start.5 = (f32[2,11,1,128]{3,2,1,0:T(1,128)S(1)}, f32[2,11,1,128]{3,2,1,0:T(1,128)S(1)}, u32[]{:S(2)}, u32[]{:S(2)}) collective-permute-start(f32[2,11,1,128]{3,2,1,0:T(1,128)S(1)} %pad_maximum_fusion.2.after), channel_id=1, source_target_pairs={{0,4},{1,5},{2,6},{3,7},{4,0},{5,1},{6,2},{7,3},{8,12},{9,13},{10,... | collective-permute-start | bytes 33800 | tf_op jit(solution)/shard_map/ppermute | solution.py:687
  24.1 8.3 %collective-permute-start.6 = (f32[4,11,1,128]{3,2,1,0:T(1,128)S(1)}, f32[4,11,1,128]{3,2,1,0:T(1,128)S(1)}, u32[]{:S(2)}, u32[]{:S(2)}) collective-permute-start(f32[4,11,1,128]{3,2,1,0:T(1,128)S(1)} %pad_maximum_fusion.1.after), channel_id=1, source_target_pairs={{0,2},{1,3},{2,0},{3,1},{4,6},{5,7},{6,4},{7,5},{8,10},{9,11},{10,... | collective-permute-start | bytes 67592 | tf_op jit(solution)/shard_map/ppermute | solution.py:687
  32.5 1.3 %collective-permute-start.7 = (f32[8,11,1,128]{3,2,1,0:T(1,128)S(1)}, f32[8,11,1,128]{3,2,1,0:T(1,128)S(1)}, u32[]{:S(2)}, u32[]{:S(2)}) collective-permute-start(f32[8,11,1,128]{3,2,1,0:T(1,128)S(1)} %pad_maximum_fusion), channel_id=1, source_target_pairs={{0,1},{1,0},{2,3},{3,2},{4,5},{5,4},{6,7},{7,6},{8,9},{9,8},{10,11... | collective-permute-start | bytes 135176 | tf_op jit(solution)/shard_map/ppermute | solution.py:687
